TPU v7x, 32 devices: a whole 2x2x4 slice. The times are simulated.
32 devices in a mesh: width: 8 (over z, x), chan: 4 (over y, core).
Axes of the slice: x: 2, y: 2, z: 4, core: 2. Of those that a mesh axis runs over, the one named last changes fastest.
Arguments:
- activations: bfloat16 [512, 2, 6144], P('chan', None, 'width'), may hold values from -6 to 6
- filters: bfloat16 [512, 3, 3, 512], P('chan'), may hold values from -0.125 to 0.125
- cotangent: bfloat16 [512, 2, 6144], P('chan', None, 'width'), may hold values from -6 to 6
Outputs:
- conv_output: bfloat16 [512, 2, 6144], P('chan', None, 'width')
- input_grad: bfloat16 [512, 2, 6144], P('chan', None, 'width')
- filter_grad: float32 [512, 3, 3, 512], P('chan')
All inputs are finite; a program needn't handle non-finite values.
Results may differ from a plain program's by a relative error of at most 0.001.
Values may be sent and summed in bfloat16 or wider, within the bound.
No kernel may reach another device: no remote copies, remote signals or barrier semaphores. Data moves between devices by JAX's collectives and lax.ppermute only.
A program may use at most 128 MiB of HBM per device.

v0:
```python
import math

import jax
import jax.numpy as jnp
from jax import lax
from jax.sharding import PartitionSpec as P


def padded_2(shard, sides, width):
    for axis, dim in sides:
        devices, length = (lax.axis_size(axis), shard.shape[dim])
        up = [(i, (i + 1) % devices) for i in range(devices - 1)]
        down = [(j, i) for i, j in up]
        last = lax.slice_in_dim(shard, length - width, length, axis=dim)
        leading = lax.slice_in_dim(shard, 0, width, axis=dim)
        before = lax.ppermute(last, axis, up)
        after = lax.ppermute(leading, axis, down)
        shard = jnp.concatenate([before, shard, after], axis=dim)
    return shard


def pad_rows(field):
    return jnp.pad(field, ((0, 0), (1, 1), (0, 0)))


def stack_taps(padded, rows, cols, flipped):
    pieces = []
    for tap_row in range(3):
        for tap_col in range(3):
            first_row = 2 - tap_row if flipped else tap_row
            first_col = 2 - tap_col if flipped else tap_col
            pieces.append(
                padded[:, first_row : first_row + rows, first_col : first_col + cols].reshape(
                    padded.shape[0], rows * cols
                )
            )
    return jnp.concatenate(pieces, 0)


def tap_major(block):
    number_in = block.shape[0]
    number_out = block.shape[3]
    return jnp.transpose(block, (1, 2, 0, 3)).reshape(9 * number_in, number_out)


def body(activations, filters, cotangent):
    cin_dev, rows, cols = activations.shape
    cout_dev = cotangent.shape[0]
    edged = padded_2(activations, (("width", 2),), 1)
    source_stack = stack_taps(pad_rows(edged), rows, cols, False)
    block = tap_major(filters)
    summed = lax.dot_general(
        block, source_stack, (((0,), (0,)), ((), ())), preferred_element_type=jnp.float32
    )
    forward = lax.psum_scatter(
        summed.reshape(cout_dev * lax.axis_size("chan"), rows, cols),
        "chan",
        scatter_dimension=0,
        tiled=True,
    )
    conv_output = forward.astype(jnp.bfloat16)
    grad_edged = padded_2(cotangent, (("width", 2),), 1)
    shards = lax.all_gather(grad_edged, "chan", axis=0, tiled=True)
    number_rows = shards.shape[0]
    block = filters.reshape(cin_dev, 9 * number_rows)
    grad_stack = stack_taps(pad_rows(shards), rows, cols, True)
    input_sum = jnp.dot(block, grad_stack, preferred_element_type=jnp.float32)
    interior = shards[:, :, 1:-1].reshape(number_rows, rows * cols)
    tap_grads = lax.dot_general(
        source_stack, interior, (((1,), (1,)), ((), ())), preferred_element_type=jnp.float32
    )
    tap_grads = jnp.transpose(tap_grads.reshape(3, 3, cin_dev, number_rows), (2, 0, 1, 3))
    filter_sum = tap_grads
    input_sum, filter_sum = (input_sum, filter_sum)
    filter_total = lax.psum(filter_sum, "width")
    factor = 1.0 / math.sqrt(rows * cols * lax.axis_size("width"))
    input_grad = input_sum.reshape(cin_dev, rows, cols).astype(jnp.bfloat16)
    return (conv_output, input_grad, filter_total * factor)


def solution(mesh):
    in_specs = (P("chan", None, "width"), P("chan", None, None, None), P("chan", None, "width"))
    out_specs = (P("chan", None, "width"), P("chan", None, "width"), P("chan", None, None, None))
    return jax.shard_map(body, mesh=mesh, in_specs=in_specs, out_specs=out_specs, check_vma=False)
```

profile of v0, /device:TPU:0, one launch (start us, length us, event | category | flops | bytes accessed | tf_op | source)
XLA Modules:
  0.0 254.1 jit_solution(8286925592780814535)
XLA Ops:
  8.6 4.8 %collective-permute-start.2 = (bf16[128,2,1]{0,2,1:T(2,128)(2,1)S(1)}, bf16[128,2,1]{0,2,1:T(2,128)(2,1)S(1)}, u32[]{:S(2)}, u32[]{:S(2)}) collective-permute-start(bf16[128,2,1]{0,2,1:T(2,128)(2,1)S(1)} %get-tuple-element.27), channel_id=1, source_target_pairs={{0,4},{4,8},{8,12},{12,16},{16,20},{20,24},{24,28},{1,5},{5,9},{9,... | collective-permute-start | bytes 1544 | tf_op jit(solution)/shard_map/ppermute | solution.py:16
  15.8 4.5 %collective-permute-start = (bf16[128,2,1]{2,1,0:T(2,128)(2,1)S(1)}, bf16[128,2,1]{2,1,0:T(2,128)(2,1)S(1)}, u32[]{:S(2)}, u32[]{:S(2)}) collective-permute-start(bf16[128,2,1]{2,1,0:T(2,128)(2,1)S(1)} %get-tuple-element.31), channel_id=1, source_target_pairs={{0,4},{4,8},{8,12},{12,16},{16,20},{20,24},{24,28},{1,5},{5,9},{9,... | collective-permute-start | bytes 1544 | tf_op jit(solution)/shard_map/ppermute | solution.py:16
  21.6 2.4 copy.24
  26.9 1.8 select_maximum_fusion
  28.8 2.4 fusion.1
  34.3 3.9 %fusion.4 = f32[1536,512]{1,0:T(8,128)} fusion(bf16[1152,1536]{1,0:T(8,128)(2,1)S(1)} %constant_dynamic-update-slice_fusion, bf16[1152,512]{1,0:T(8,128)(2,1)S(1)} %bitcast.81), kind=kOutput, calls=%fused_computation.39 | convolution fusion | flops 1811939328 | bytes 7864320 | tf_op jit(solution)/shard_map/dot_general | solution.py:52
  38.2 4.3 %copy.11 = f32[512,2,768]{2,1,0:T(2,128)S(1)} copy(f32[512,2,768]{0,2,1:T(8,128)} %bitcast.63) | data formatting | bytes 6291456 | tf_op jit(solution)/shard_map/reshape | solution.py:56
  42.5 58.2 %all-reduce.7 = bf16[512,2,768]{2,1,0:T(2,128)(2,1)} all-reduce(f32[512,2,768]{2,1,0:T(2,128)S(1)} %copy.11), channel_id=2, replica_groups=mesh['width'=8,'chan'=4] {'chan'}, use_global_device_ids=true, to_apply=%region_0.1.clone | all-reduce | flops 786432 | bytes 4718592
  100.7 2.0 dynamic-slice_convert_fusion
  102.8 7.3 %pad_slice_fusion = (bf16[512,2,768]{0,2,1:T(8,128)(2,1)S(1)}, bf16[512,2,768]{0,2,1:T(8,128)(2,1)}, bf16[512,2,768]{0,2,1:T(8,128)(2,1)}, bf16[512,2,768]{0,2,1...) fusion(bf16[512,2,770]{0,2,1:T(8,128)(2,1)} %all-gather.2.clone, ...), kind=kLoop, calls=%fused_computation | loop fusion | bytes 20463616 | tf_op jit(solution)/shard_map/slice | solution.py:33
  110.1 2.6 %copy.27 = bf16[512,1536]{1,0:T(8,128)(2,1)} copy(bf16[512,1536]{0,1:T(8,128)(2,1)} %bitcast.61) | data formatting | bytes 3145728 | tf_op jit(solution)/shard_map/reshape | solution.py:33
  112.7 2.7 %constant_dynamic-update-slice_fusion.17 = bf16[4608,1536]{1,0:T(8,128)(2,1)} fusion(bf16[512,1536]{1,0:T(8,128)(2,1)} %copy.27), kind=kLoop, calls=%fused_computation.35 | loop fusion | bytes 3145728
  115.3 2.6 %copy.28 = bf16[512,1536]{1,0:T(8,128)(2,1)} copy(bf16[512,1536]{0,1:T(8,128)(2,1)} %bitcast.60) | data formatting | bytes 3145728 | tf_op jit(solution)/shard_map/reshape | solution.py:33
  117.9 2.6 %copy.29 = bf16[512,1536]{1,0:T(8,128)(2,1)} copy(bf16[512,1536]{0,1:T(8,128)(2,1)} %bitcast.59) | data formatting | bytes 3145728 | tf_op jit(solution)/shard_map/reshape | solution.py:33
  120.5 2.7 %copy.30 = bf16[512,1536]{1,0:T(8,128)(2,1)} copy(bf16[512,1536]{0,1:T(8,128)(2,1)} %bitcast.58) | data formatting | bytes 3145728 | tf_op jit(solution)/shard_map/reshape | solution.py:33
  123.1 2.6 %copy.31 = bf16[512,1536]{1,0:T(8,128)(2,1)} copy(bf16[512,1536]{0,1:T(8,128)(2,1)} %bitcast.56) | data formatting | bytes 3145728 | tf_op jit(solution)/shard_map/reshape | solution.py:33
  125.7 5.9 %convolution_bitcast_fusion = f32[128,3,3,512]{3,0,2,1:T(8,128)} fusion(bf16[3,3,128,1536]{3,2,1,0:T(8,128)(2,1)} %bitcast.84, bf16[512,1536,1,1]{0,1,3,2:T(8,128)(2,1)} %bitcast.57), kind=kOutput, calls=%fused_computation.10 | convolution fusion | flops 1811939328 | bytes 7471104 | tf_op jit(solution)/shard_map/dot_general | solution.py:69
  131.6 2.8 %constant_dynamic-update-slice_fusion.16 = bf16[4608,1536]{1,0:T(8,128)(2,1)} fusion(bf16[4608,1536]{1,0:T(8,128)(2,1)} %constant_dynamic-update-slice_fusion.17, bf16[512,1536]{1,0:T(8,128)(2,1)} %copy.28), kind=kLoop, calls=%fused_computation.34 | loop fusion | bytes 3145728
  138.3 2.6 %copy.32 = bf16[512,1536]{1,0:T(8,128)(2,1)} copy(bf16[512,1536]{0,1:T(8,128)(2,1)} %bitcast.55) | data formatting | bytes 3145728 | tf_op jit(solution)/shard_map/reshape | solution.py:33
  140.9 2.6 %copy.33 = bf16[512,1536]{1,0:T(8,128)(2,1)} copy(bf16[512,1536]{0,1:T(8,128)(2,1)} %bitcast.54) | data formatting | bytes 3145728 | tf_op jit(solution)/shard_map/reshape | solution.py:33
  145.8 2.9 %constant_dynamic-update-slice_fusion.12 = bf16[4608,1536]{1,0:T(8,128)(2,1)} fusion(bf16[4608,1536]{1,0:T(8,128)(2,1)} %constant_dynamic-update-slice_fusion.13, bf16[512,1536]{1,0:T(8,128)(2,1)} %copy.32), kind=kLoop, calls=%fused_computation.30 | loop fusion | bytes 3145728
  152.5 7.2 %convolution_convert_fusion = bf16[1536,128]{1,0:T(8,128)(2,1)S(1)} fusion(bf16[4608,1536]{1,0:T(8,128)(2,1)} %constant_dynamic-update-slice_fusion.9, bf16[128,4608]{0,1:T(8,128)(2,1)S(1)} %bitcast.82), kind=kOutput, calls=%fused_computation.8 | convolution fusion | flops 1812135936 | bytes 15728640 | tf_op jit(solution)/shard_map/dot_general | solution.py:67
  160.8 83.0 %all-reduce.6.cloned.1.call-done = f32[128,3,3,512]{3,0,2,1:T(8,128)} async-done(((f32[128,3,3,512]{3,0,2,1:T(8,128)}), f32[128,3,3,512]{3,0,2,1:T(8,128)}) %all-reduce.6.cloned.1.call-update) | async-done | bytes 2359312 | tf_op jit(solution)/shard_map/psum | solution.py:75
  243.8 3.4 %broadcast_multiply_fusion = f32[128,3,3,512]{3,0,2,1:T(8,128)} fusion(f32[128,3,3,512]{3,0,2,1:T(8,128)} %all-reduce.6.cloned.1.call-done), kind=kLoop, calls=%fused_computation.11 | loop fusion | flops 589824 | bytes 4718592 | tf_op jit(solution)/shard_map/mul | solution.py:78
  (64 shorter events, 21.1 us)
Async XLA Ops:
  7.2 16.9 %copy-start.9 = (u32[32]{0:T(128)S(1)}, u32[32]{0:T(128)}, u32[]{:S(2)}) copy-start(u32[32]{0:T(128)} %constant.11) | copy-start | bytes 388
  7.2 16.9 %copy-start.5 = (bf16[128,2,768]{2,1,0:T(2,128)(2,1)S(1)}, bf16[128,2,768]{2,1,0:T(2,128)(2,1)}, u32[]{:S(2)}) copy-start(bf16[128,2,768]{2,1,0:T(2,128)(2,1)} %param.3) | copy-start | bytes 1179652
  7.2 95.6 %all-gather.2.cloned.1.call-start = ((), (), s32[]{:S(2)}) async-start(), calls=%async_computation | async-start | bytes 1986560 | tf_op jit(solution)/shard_map/all_gather | solution.py:63
  8.6 16.7 %collective-permute-start.2 = (bf16[128,2,1]{0,2,1:T(2,128)(2,1)S(1)}, bf16[128,2,1]{0,2,1:T(2,128)(2,1)S(1)}, u32[]{:S(2)}, u32[]{:S(2)}) collective-permute-start(bf16[128,2,1]{0,2,1:T(2,128)(2,1)S(1)} %get-tuple-element.27), channel_id=1, source_target_pairs={{0,4},{4,8},{8,12},{12,16},{16,20},{20,24},{24,28},{1,5},{5,9},{9,... | collective-permute-start | bytes 1544 | tf_op jit(solution)/shard_map/ppermute | solution.py:16
  13.5 11.9 %collective-permute-start.3 = (bf16[128,2,1]{0,2,1:T(2,128)(2,1)S(1)}, bf16[128,2,1]{0,2,1:T(2,128)(2,1)S(1)}, u32[]{:S(2)}, u32[]{:S(2)}) collective-permute-start(bf16[128,2,1]{0,2,1:T(2,128)(2,1)S(1)} %get-tuple-element.28), channel_id=1, source_target_pairs={{4,0},{8,4},{12,8},{16,12},{20,16},{24,20},{28,24},{5,1},{9,5},{13... | collective-permute-start | bytes 1544 | tf_op jit(solution)/shard_map/ppermute | solution.py:17
  15.8 10.5 %collective-permute-start = (bf16[128,2,1]{2,1,0:T(2,128)(2,1)S(1)}, bf16[128,2,1]{2,1,0:T(2,128)(2,1)S(1)}, u32[]{:S(2)}, u32[]{:S(2)}) collective-permute-start(bf16[128,2,1]{2,1,0:T(2,128)(2,1)S(1)} %get-tuple-element.31), channel_id=1, source_target_pairs={{0,4},{4,8},{8,12},{12,16},{16,20},{20,24},{24,28},{1,5},{5,9},{9,... | collective-permute-start | bytes 1544 | tf_op jit(solution)/shard_map/ppermute | solution.py:16
  20.3 6.6 %collective-permute-start.1 = (bf16[128,2,1]{2,1,0:T(2,128)(2,1)S(1)}, bf16[128,2,1]{2,1,0:T(2,128)(2,1)S(1)}, u32[]{:S(2)}, u32[]{:S(2)}) collective-permute-start(bf16[128,2,1]{2,1,0:T(2,128)(2,1)S(1)} %get-tuple-element.32), channel_id=1, source_target_pairs={{4,0},{8,4},{12,8},{16,12},{20,16},{24,20},{28,24},{5,1},{9,5},{13... | collective-permute-start | bytes 1544 | tf_op jit(solution)/shard_map/ppermute | solution.py:17
  26.2 217.6 %all-reduce.6.cloned.1.call-start = ((), (), s32[]{:S(2)}) async-start(), calls=%async_computation.1 | async-start | bytes 4718592 | tf_op jit(solution)/shard_map/psum | solution.py:75
  32.9 1.4 copy-start.6
  33.2 5.0 %copy-start.8 = (bf16[1152,1536]{1,0:T(8,128)(2,1)}, bf16[1152,1536]{1,0:T(8,128)(2,1)S(1)}, u32[]{:S(2)}) copy-start(bf16[1152,1536]{1,0:T(8,128)(2,1)S(1)} %constant_dynamic-update-slice_fusion) | copy-start | bytes 10616836
  131.6 2.8 %copy-start.2 = (bf16[512,1536]{1,0:T(8,128)(2,1)S(1)}, bf16[512,1536]{1,0:T(8,128)(2,1)}, u32[]{:S(2)}) copy-start(bf16[512,1536]{1,0:T(8,128)(2,1)} %copy.29) | copy-start | bytes 4718596
  131.6 4.1 %copy-start.1 = (bf16[512,1536]{1,0:T(8,128)(2,1)S(1)}, bf16[512,1536]{1,0:T(8,128)(2,1)}, u32[]{:S(2)}) copy-start(bf16[512,1536]{1,0:T(8,128)(2,1)} %copy.30) | copy-start | bytes 4718596
  134.4 2.6 %copy-start = (bf16[512,1536]{1,0:T(8,128)(2,1)S(1)}, bf16[512,1536]{1,0:T(8,128)(2,1)}, u32[]{:S(2)}) copy-start(bf16[512,1536]{1,0:T(8,128)(2,1)} %copy.31) | copy-start | bytes 4718596
  145.8 2.9 %copy-start.4 = (bf16[512,1536]{1,0:T(8,128)(2,1)S(1)}, bf16[512,1536]{1,0:T(8,128)(2,1)}, u32[]{:S(2)}) copy-start(bf16[512,1536]{1,0:T(8,128)(2,1)} %copy.33) | copy-start | bytes 4718596
  145.8 4.2 %copy-start.3 = (bf16[512,1536]{1,0:T(8,128)(2,1)S(1)}, bf16[512,1536]{1,0:T(8,128)(2,1)}, u32[]{:S(2)}) copy-start(bf16[512,1536]{1,0:T(8,128)(2,1)} %copy.34) | copy-start | bytes 4718596
  149.9 2.6 %copy-start.7 = (bf16[128,3,3,512]{0,3,2,1:T(8,128)(2,1)S(1)}, bf16[128,3,3,512]{0,3,2,1:T(8,128)(2,1)}, u32[]{:S(2)}) copy-start(bf16[128,3,3,512]{0,3,2,1:T(8,128)(2,1)} %copy.24) | copy-start | bytes 3538948
Sparse Core Ops, SparseCore 0:
  26.4 23.2 all-gather.1
  131.7 112.0 all-reduce.5
where the time goes:
time: 255 us; the launch traced here: 254 us
  waiting for transfers between devices  83.7 us (33%)
  local copies, waits for them, and re-layouts  60.7 us (24%)
  blocking collectives  58.2 us (23%)
  matrix products  17 us (7%)
  between operations  15 us (6%)
  starting transfers between devices  12.1 us (5%)
  other arithmetic  7.42 us (3%)
    psum x1, waiting for transfers between devices, body(): filter_total = lax.psum(filter_sum, 'width')  83 us
    unnamed x1, blocking collectives  58.2 us
    unnamed x49, local copies, waits for them, and re-layouts  21.8 us
    reshape x9, local copies, waits for them, and re-layouts, stack_taps(): padded[:, first_row:first_row + rows, first_col:first_col + cols]  20.4 us
    slice x2, local copies, waits for them, and re-layouts, stack_taps(): padded[:, first_row:first_row + rows, first_col:first_col + cols]  9.72 us
    ppermute x2, starting transfers between devices, padded_2(): before = lax.ppermute(last, axis, up)  9.39 us
    dot_general x1, matrix products, body(): input_sum = jnp.dot(block, grad_stack, preferred_element_type=jnp.float32)  7.23 us
    dot_general x1, matrix products, body(): lax.dot_general(source_stack, interior, (((1,), (1,)), ((), ())), preferr...  5.88 us
  transfers between devices with their start and end apart: 6, of which 2 were waited for; matrix products, arithmetic and copies ran while one was open for 20% of the time, Pallas kernels for 0%

commit v1 on v0

v1 whole, which is shorter than its diff:
```python
import functools
import math

import jax
import jax.numpy as jnp
from jax import lax
from jax.experimental import pallas as pl
from jax.experimental.pallas import tpu as pltpu
from jax.sharding import PartitionSpec as P

BF16, F16, F32 = jnp.bfloat16, jnp.float16, jnp.float32
TOP = 14.0
TAIL = 16
VMEM = pl.BlockSpec(memory_space=pltpu.VMEM)
NT = (((1,), (1,)), ((), ()))
TN = (((0,), (0,)), ((), ()))


def exchange(value, axis, bit):
    devices = lax.axis_size(axis)
    return lax.ppermute(value, axis, [(i, i ^ bit) for i in range(devices)])


def bits_of(devices):
    return devices.bit_length() - 1


def reversed_bits(index, count):
    out = 0
    for b in range(count):
        out = out + (((index >> b) & 1) << (count - 1 - b))
    return out


def call(body, name, outs, scratch, flops, *args):
    outs = [jax.ShapeDtypeStruct(shape, dtype) for shape, dtype in outs]
    moved = sum(a.size * a.dtype.itemsize for a in list(args) + outs)
    result = pl.pallas_call(
        body,
        out_shape=outs,
        in_specs=[VMEM] * len(args),
        out_specs=[VMEM] * len(outs),
        scratch_shapes=[pltpu.VMEM(shape, dtype) for shape, dtype in scratch],
        compiler_params=pltpu.CompilerParams(vmem_limit_bytes=32 << 20),
        cost_estimate=pl.CostEstimate(flops=flops, bytes_accessed=moved, transcendentals=0),
        name=name,
    )(*args)
    return result[0] if len(outs) == 1 else result


def taps_kernel(x, before, after, out):
    chans, rows, cols = x.shape
    edge = before.shape[2]
    for i in range(rows):
        row = jnp.concatenate([before[:, i, :], x[:, i, :], after[:, i, :]], axis=1)
        for b in range(3):
            first = edge - 1 + b
            out[i, b * chans : (b + 1) * chans, :] = row[:, first : first + cols]


def filter_kernel(factor, piece, xs, ga, gb, send, keep, gsc, acc):
    rows, deep, cols = xs.shape
    width = lax.axis_size("width")
    nbits = bits_of(width)
    block = ga.shape[1]
    parity = lax.axis_index("chan") & 1
    gsc[:, pl.ds(pl.multiple_of(parity * block, block), block), :] = ga[...]
    gsc[:, pl.ds(pl.multiple_of((1 - parity) * block, block), block), :] = gb[...]
    for a in range(3):
        total = None
        for h in range(rows):
            i = h + a - 1
            if 0 <= i < rows:
                part = lax.dot_general(xs[i], gsc[h], NT, preferred_element_type=F32)
                total = part if total is None else total + part
        acc[a * deep : (a + 1) * deep, :] = total * factor
    if acc.shape[0] > 3 * deep:
        acc[3 * deep :, :] = jnp.zeros((acc.shape[0] - 3 * deep, acc.shape[1]), F32)
    most = jnp.max(jnp.abs(acc[...]), axis=(0, 1), keepdims=True)
    power = jnp.ceil(jnp.log2(jnp.maximum(most, 2.0**-110)))
    mine = reversed_bits(lax.axis_index("width"), nbits)
    half = width // 2
    for r in range(width):
        rows_of = acc[pl.ds(pl.multiple_of((mine ^ r) * piece, 16), piece), :]
        if r < half:
            keep[r * piece : (r + 1) * piece, :] = rows_of
        else:
            send[(r - half) * piece : (r - half + 1) * piece, :] = rows_of * jnp.exp2(TOP - power)
    send[half * piece :, :] = jnp.broadcast_to(power, (TAIL, acc.shape[1]))
    keep[half * piece :, :] = jnp.broadcast_to(power, (TAIL, acc.shape[1]))


def forward_kernel(xs, f, send, keep, acc):
    rows, deep, cols = xs.shape
    groups = lax.axis_size("chan")
    nbits = bits_of(groups)
    block = acc.shape[0] // groups
    me = lax.axis_index("chan")
    for h in range(rows):
        total = None
        for i in range(max(0, h - 1), min(rows, h + 2)):
            part = lax.dot_general(f[i - h + 1], xs[i], TN, preferred_element_type=F32)
            total = part if total is None else total + part
        acc[...] = total
        for q in range(groups):
            owner = me ^ reversed_bits(q, nbits)
            rows_of = acc[pl.ds(pl.multiple_of(owner * block, block), block), :]
            if q < groups // 2:
                keep[q, h] = rows_of
            else:
                send[q - groups // 2, h] = rows_of


def input_kernel(f, edge_rows, *refs):
    groups = lax.axis_size("chan")
    gs, (out, gsc, hsc) = refs[:groups], refs[groups:]
    rows, block, cols = gs[0].shape
    chans = out.shape[1]
    me = lax.axis_index("chan")
    for r in range(groups):
        at = pl.ds(pl.multiple_of((me ^ r) * block, block), block)
        gsc[:, at, :] = gs[r][...]
        if block % 128 == 0:
            hsc[:, at] = edge_rows[r]
    if block % 128:
        hsc[...] = edge_rows[...]
    lane = lax.broadcasted_iota(jnp.int32, (chans, cols), 1)
    sums = [None] * rows
    for i in range(rows):
        taps = [a for a in range(3) if 0 <= a - 1 + i < rows]
        mats = f[taps[0] * 3 * chans : (taps[-1] + 1) * 3 * chans, :]
        prod = jnp.dot(mats, gsc[i], preferred_element_type=F32)
        ends = lax.dot_general(mats, hsc[...], NT, preferred_element_type=F32)
        for n, a in enumerate(taps):
            h = a - 1 + i
            for b in range(3):
                at = slice((n * 3 + b) * chans, (n * 3 + b + 1) * chans)
                term = prod[at]
                if b == 0:
                    term = jnp.where(lane == cols - 1, ends[at, 2 * i + 1 : 2 * i + 2], pltpu.roll(term, cols - 1, 1))
                elif b == 2:
                    term = jnp.where(lane == 0, ends[at, 2 * i : 2 * i + 1], pltpu.roll(term, 1, 1))
                sums[h] = term if sums[h] is None else sums[h] + term
    for h in range(rows):
        out[h] = sums[h].astype(BF16)


def packed(values, power):
    tail = jnp.broadcast_to(power, (TAIL, values.shape[1]))
    return jnp.concatenate([values * jnp.exp2(TOP - power), tail], axis=0).astype(F16)


def reduce_pieces(send, keep):
    power = keep[-1:, :1]
    total = keep[:-TAIL]
    message = send.astype(F16)
    for b in range(bits_of(lax.axis_size("width"))):
        got = exchange(message, "width", 1 << b)
        count = got.shape[0] - TAIL
        other = got[count : count + 1, :1].astype(F32)
        total = total[:count] + got[:count].astype(F32) * jnp.exp2(other - TOP)
        power = jnp.maximum(power, other) + 1.0
        left = count // 2 if 2 << b < lax.axis_size("width") else 0
        message = packed(total[left:], power)
    return message


def gather_pieces(message):
    me = lax.axis_index("width")
    every = message[None]
    for b in reversed(range(bits_of(lax.axis_size("width")))):
        got = exchange(every, "width", 1 << b)
        late = ((me >> b) & 1) == 1
        every = jnp.concatenate([jnp.where(late, got, every), jnp.where(late, every, got)], axis=0)
    return every


def unpacked(every):
    rows = every.shape[1] - TAIL
    scale = jnp.exp2(every[:, rows : rows + 1].astype(F32) - TOP)
    return (every[:, :rows].astype(F32) * scale).reshape(-1, every.shape[2])


def body(activations, filters, cotangent):
    chans, rows, cols = activations.shape
    block = cotangent.shape[0]
    outs = filters.shape[3]
    groups, width = lax.axis_size("chan"), lax.axis_size("width")
    me = lax.axis_index("chan")
    up = [(i, i + 1) for i in range(width - 1)]
    down = [(i + 1, i) for i in range(width - 1)]
    edge = min(128, cols)

    g = {0: jnp.transpose(cotangent, (1, 0, 2))}
    for b in reversed(range(bits_of(groups))):
        for r in sorted(g):
            g[r | 1 << b] = exchange(g[r], "chan", 1 << b)

    before = lax.ppermute(activations[:, :, cols - edge :], "width", up)
    after = lax.ppermute(activations[:, :, :edge], "width", down)
    xs = call(taps_kernel, "shifted_taps", [((rows, 3 * chans, cols), BF16)], [], 0, activations, before, after)

    mats = jnp.transpose(filters, (1, 2, 0, 3))
    pairs_of_rows = sum(0 <= h + a - 1 < rows for h in range(rows) for a in range(3))
    flops = 2 * pairs_of_rows * 3 * chans * cols * outs

    piece = -(-9 * chans // width)
    piece = -(-piece // 16) * 16
    factor = 1.0 / math.sqrt(rows * cols * width)
    share = (width // 2 * piece + TAIL, 2 * block)
    pieces = []
    for j in range(groups // 2):
        send, keep = call(
            functools.partial(filter_kernel, factor, piece),
            "filter_terms",
            [(share, F32), (share, F32)],
            [((rows, 2 * block, cols), BF16), ((width * piece, 2 * block), F32)],
            flops * 2 // groups,
            xs,
            g[2 * j],
            g[2 * j + 1],
        )
        pieces.append(gather_pieces(reduce_pieces(send, keep)))

    send, keep = call(
        forward_kernel,
        "forward_terms",
        [((groups // 2, rows, block, cols), F32)] * 2,
        [((outs, cols), F32)],
        flops,
        xs,
        mats.reshape(3, 3 * chans, outs),
    )
    for b in range(bits_of(groups)):
        total = keep + exchange(send, "chan", 1 << b)
        keep, send = total[: total.shape[0] // 2], total[total.shape[0] // 2 :]
    conv_output = jnp.transpose(total[0].astype(BF16), (1, 0, 2))

    firsts = jnp.stack([g[r][:, :, 0] for r in range(groups)])
    lasts = jnp.stack([g[r][:, :, -1] for r in range(groups)])
    left = lax.ppermute(lasts, "width", up)
    right = lax.ppermute(firsts, "width", down)
    ends = jnp.stack([left, right], axis=2).reshape(groups, 2 * rows, block)
    ends = jnp.pad(ends, ((0, 0), (0, 16 - 2 * rows), (0, 0)))
    if block % 128:
        order = me ^ jnp.arange(groups)
        ends = jnp.transpose(ends[order], (1, 0, 2)).reshape(16, outs)
    input_grad = call(
        input_kernel,
        "input_terms",
        [((rows, chans, cols), BF16)],
        [((rows, outs, cols), BF16), ((16, outs), BF16)],
        flops,
        mats.reshape(9 * chans, outs),
        ends,
        *[g[r] for r in range(groups)],
    )
    input_grad = jnp.transpose(input_grad, (1, 0, 2))

    for b in range(bits_of(groups // 2)):
        swap = ((me >> (b + 1)) & 1) == 1
        pieces = [jnp.where(swap, pieces[j ^ 1 << b], pieces[j]) for j in range(len(pieces))]
    grads = jnp.concatenate([unpacked(p) for p in pieces], axis=1)[: 9 * chans]
    grads = jnp.transpose(grads.reshape(3, 3, chans, outs), (2, 0, 1, 3))
    return conv_output, input_grad, grads


def solution(mesh):
    cols = P("chan", None, "width")
    mats = P("chan", None, None, None)
    return jax.shard_map(body, mesh=mesh, in_specs=(cols, mats, cols), out_specs=(cols, cols, mats), check_vma=False)
```

time: 255 us -> 93.5 us (0.37)
  blocking collectives: 58.2 us -> 0 us
  waiting for transfers between devices: 83.7 us -> 25.8 us
  local copies, waits for them, and re-layouts: 60.7 us -> 9.46 us
  starting transfers between devices: 12.1 us -> 39.4 us
  matrix products: 17 us -> 0 us
  between operations: 15 us -> 6.75 us
  Pallas kernels: 0 us -> 7.78 us
  other arithmetic: 7.42 us -> 3.96 us
    psum x1 -> x0, waiting for transfers between devices: 83 us -> none  [body(): filter_total = lax.psum(filter_sum, 'width')]
    unnamed x1 -> x0, blocking collectives: 58.2 us -> none
    ppermute x4 -> x21, starting transfers between devices: 12 us -> 39.4 us  [the longest x17 28.9 us: exchange(): return lax.ppermute(value, axis, [(i, i ^ bit) for i in range(devices)])]
    ppermute x4 -> x21, waiting for transfers between devices: 0.63 us -> 25.8 us  [the longest x17 21.1 us: exchange(): return lax.ppermute(value, axis, [(i, i ^ bit) for i in range(devices)])]
    reshape x10 -> x0, local copies, waits for them, and re-layouts: 24.8 us -> none  [the longest x9 20.4 us: stack_taps(): padded[:, first_row:first_row + rows, first_col:first_col + cols]]
    unnamed x49 -> x9, local copies, waits for them, and re-layouts: 21.8 us -> 3.4 us
    dot_general x3 -> x0, matrix products: 17 us -> none  [the longest x1 7.23 us: body(): input_sum = jnp.dot(block, grad_stack, preferred_element_type=jnp.float32)]
    pallas_call x0 -> x5, Pallas kernels: none -> 7.78 us  [call(): pl.pallas_call(body, out_shape=outs, in_specs=[VMEM] * len(args), out_spe...]
  transfers between devices with their start and end apart: 6 -> 21, of which waited for: 2 -> 12; matrix products, arithmetic and copies ran while one was open for 20% -> 12% of each run, Pallas kernels for 0% -> 8%
where the time goes in v1:
time: 93.5 us; the launch traced here: 93.1 us
  starting transfers between devices  39.4 us (42%)
  waiting for transfers between devices  25.8 us (28%)
  local copies, waits for them, and re-layouts  9.46 us (10%)
  Pallas kernels  7.78 us (8%)
  between operations  6.75 us (7%)
  other arithmetic  3.96 us (4%)
    ppermute x17, starting transfers between devices, exchange(): return lax.ppermute(value, axis, [(i, i ^ bit) for i in range(devices)])  28.9 us
    ppermute x17, waiting for transfers between devices, exchange(): return lax.ppermute(value, axis, [(i, i ^ bit) for i in range(devices)])  21.1 us
    pallas_call x5, Pallas kernels, call(): pl.pallas_call(body, out_shape=outs, in_specs=[VMEM] * len(args), out_spe...  7.78 us
    ppermute x1, starting transfers between devices, body(): left = lax.ppermute(lasts, 'width', up)  4.51 us
    ppermute x1, waiting for transfers between devices, body(): after = lax.ppermute(activations[:, :, :edge], 'width', down)  4.27 us
    unnamed x9, local copies, waits for them, and re-layouts  3.4 us
    ppermute x1, starting transfers between devices, body(): before = lax.ppermute(activations[:, :, cols - edge:], 'width', up)  3.4 us
    slice x6, local copies, waits for them, and re-layouts, reduce_pieces(): other = got[count:count + 1, :1].astype(F32)  3.12 us
  transfers between devices with their start and end apart: 21, of which 12 were waited for; matrix products, arithmetic and copies ran while one was open for 12% of the time, Pallas kernels for 8%

profile of v1, /device:TPU:0, one launch (start us, length us, event | category | flops | bytes accessed | tf_op | source)
XLA Modules:
  0.0 93.1 jit_solution(8190972260385446477)
XLA Ops:
  2.2 2.6 %collective-permute-start.5 = (bf16[2,128,768]{2,1,0:T(8,128)(2,1)S(1)}, bf16[2,128,768]{2,1,0:T(8,128)(2,1)S(1)}, u32[]{:S(2)}, u32[]{:S(2)}) collective-permute-start(bf16[2,128,768]{2,1,0:T(8,128)(2,1)S(1)} %bitcast.65), channel_id=1, source_target_pairs={{0,2},{1,3},{2,0},{3,1},{4,6},{5,7},{6,4},{7,5},{8,10},{9,11},{10,... | collective-permute-start | bytes 1179656 | tf_op jit(solution)/shard_map/ppermute | solution.py:21
  5.8 3.4 %collective-permute-start = (bf16[128,2,128]{2,1,0:T(2,128)(2,1)S(1)}, bf16[128,2,128]{2,1,0:T(2,128)(2,1)S(1)}, u32[]{:S(2)}, u32[]{:S(2)}) collective-permute-start(bf16[128,2,128]{2,1,0:T(2,128)(2,1)S(1)} %get-tuple-element.60), channel_id=1, source_target_pairs={{0,4},{4,8},{8,12},{12,16},{16,20},{20,24},{24,28},{1,5},{5,9},{9,... | collective-permute-start | bytes 196616 | tf_op jit(solution)/shard_map/ppermute | solution.py:199
  9.2 1.3 %collective-permute-start.1 = (bf16[128,2,128]{2,1,0:T(2,128)(2,1)S(1)}, bf16[128,2,128]{2,1,0:T(2,128)(2,1)S(1)}, u32[]{:S(2)}, u32[]{:S(2)}) collective-permute-start(bf16[128,2,128]{2,1,0:T(2,128)(2,1)S(1)} %get-tuple-element.59), channel_id=1, source_target_pairs={{4,0},{8,4},{12,8},{16,12},{20,16},{24,20},{28,24},{5,1},{9,5},{13... | collective-permute-start | bytes 196616 | tf_op jit(solution)/shard_map/ppermute | solution.py:200
  11.1 4.3 %collective-permute-done.1.after = bf16[128,2,128]{2,1,0:T(2,128)(2,1)S(1)} collective-permute-done((bf16[128,2,128]{2,1,0:T(2,128)(2,1)S(1)}, bf16[128,2,128]{2,1,0:T(2,128)(2,1)S(1)}, u32[]{:S(2)}, u32[]{:S(2)}) %collective-permute-start.1) | collective-permute-done | bytes 65568 | tf_op jit(solution)/shard_map/ppermute | solution.py:200
  15.4 1.6 %shifted_taps.1.xs = bf16[2,384,768]{2,1,0:T(8,128)(2,1)S(1)} custom-call(bf16[128,2,768]{2,1,0:T(2,128)(2,1)S(1)} %copy-done, bf16[128,2,128]{2,1,0:T(2,128)(2,1)S(1)} %collective-permute-done.before, bf16[128,2,128]{2,1,0:T(2,128)(2,1)S(1)} %collective-permute-done.1.after), custom_call_target="tpu_custom_call" | custom-call | bytes 1703936 | tf_op jit(solution)/shard_map/shifted_taps/pallas_call | solution.py:38
  18.1 2.5 %collective-permute-start.15 = (f16[592,256]{1,0:T(8,128)(2,1)S(1)}, f16[592,256]{1,0:T(8,128)(2,1)S(1)}, u32[]{:S(2)}, u32[]{:S(2)}) collective-permute-start(f16[592,256]{1,0:T(8,128)(2,1)S(1)} %convert_element_type.77), channel_id=1, source_target_pairs={{0,4},{4,0},{8,12},{12,8},{16,20},{20,16},{24,28},{28,24},{1,5},{5... | collective-permute-start | bytes 909320 | tf_op jit(solution)/shard_map/ppermute | solution.py:21
  20.6 2.0 %forward_terms.1 = (f32[2,2,128,768]{3,2,1,0:T(8,128)S(1)}, f32[2,2,128,768]{3,2,1,0:T(8,128)S(1)}) custom-call(bf16[2,384,768]{2,1,0:T(8,128)(2,1)S(1)} %shifted_taps.1.xs, bf16[3,384,512]{2,1,0:T(8,128)(2,1)S(1)} %bitcast.70), custom_call_target="tpu_custom_call" | custom-call | flops 1207959552 | bytes 5505024 | tf_op jit(solution)/shard_map/forward_terms/pallas_call | solution.py:38
  24.1 2.6 %collective-permute-done.15 = f16[592,256]{1,0:T(8,128)(2,1)S(1)} collective-permute-done((f16[592,256]{1,0:T(8,128)(2,1)S(1)}, f16[592,256]{1,0:T(8,128)(2,1)S(1)}, u32[]{:S(2)}, u32[]{:S(2)}) %collective-permute-start.15) | collective-permute-done | bytes 303136 | tf_op jit(solution)/shard_map/ppermute | solution.py:21
  28.8 1.6 %collective-permute-start.16 = (f16[304,256]{1,0:T(8,128)(2,1)S(1)}, f16[304,256]{1,0:T(8,128)(2,1)S(1)}, u32[]{:S(2)}, u32[]{:S(2)}) collective-permute-start(f16[304,256]{1,0:T(8,128)(2,1)S(1)} %concatenate.50), channel_id=1, source_target_pairs={{0,8},{4,12},{8,0},{12,4},{16,24},{20,28},{24,16},{28,20},{1,9},{5... | collective-permute-start | bytes 466952 | tf_op jit(solution)/shard_map/ppermute | solution.py:21
  31.5 1.8 %collective-permute-start.9 = (f16[592,256]{1,0:T(8,128)(2,1)S(1)}, f16[592,256]{1,0:T(8,128)(2,1)S(1)}, u32[]{:S(2)}, u32[]{:S(2)}) collective-permute-start(f16[592,256]{1,0:T(8,128)(2,1)S(1)} %convert_element_type.70), channel_id=1, source_target_pairs={{0,4},{4,0},{8,12},{12,8},{16,20},{20,16},{24,28},{28,24},{1,5},{5... | collective-permute-start | bytes 909320 | tf_op jit(solution)/shard_map/ppermute | solution.py:21
  35.4 2.7 %collective-permute-start.17 = (f16[160,256]{1,0:T(8,128)(2,1)S(1)}, f16[160,256]{1,0:T(8,128)(2,1)S(1)}, u32[]{:S(2)}, u32[]{:S(2)}) collective-permute-start(f16[160,256]{1,0:T(8,128)(2,1)S(1)} %concatenate.51), channel_id=1, source_target_pairs={{0,16},{4,20},{8,24},{12,28},{16,0},{20,4},{24,8},{28,12},{1,17},{... | collective-permute-start | bytes 245768 | tf_op jit(solution)/shard_map/ppermute | solution.py:21
  38.1 1.3 %collective-permute-start.8 = (bf16[4,2,128]{2,1,0:T(2,128)(2,1)S(1)}, bf16[4,2,128]{2,1,0:T(2,128)(2,1)S(1)}, u32[]{:S(2)}, u32[]{:S(2)}) collective-permute-start(bf16[4,2,128]{2,1,0:T(2,128)(2,1)S(1)} %pad_maximum_fusion.8), channel_id=1, source_target_pairs={{4,0},{8,4},{12,8},{16,12},{20,16},{24,20},{28,24},{5,1},{9,5},{13... | collective-permute-start | bytes 6152 | tf_op jit(solution)/shard_map/ppermute | solution.py:242
  44.1 2.9 %collective-permute-start.10 = (f16[304,256]{1,0:T(8,128)(2,1)S(1)}, f16[304,256]{1,0:T(8,128)(2,1)S(1)}, u32[]{:S(2)}, u32[]{:S(2)}) collective-permute-start(f16[304,256]{1,0:T(8,128)(2,1)S(1)} %concatenate.44), channel_id=1, source_target_pairs={{0,8},{4,12},{8,0},{12,4},{16,24},{20,28},{24,16},{28,20},{1,9},{5... | collective-permute-start | bytes 466952 | tf_op jit(solution)/shard_map/ppermute | solution.py:21
  47.1 4.1 %collective-permute-done.10 = f16[304,256]{1,0:T(8,128)(2,1)S(1)} collective-permute-done((f16[304,256]{1,0:T(8,128)(2,1)S(1)}, f16[304,256]{1,0:T(8,128)(2,1)S(1)}, u32[]{:S(2)}, u32[]{:S(2)}) %collective-permute-start.10) | collective-permute-done | bytes 155680 | tf_op jit(solution)/shard_map/ppermute | solution.py:21
  53.5 2.1 %collective-permute-start.18 = (f16[1,160,256]{2,1,0:T(8,128)(2,1)S(1)}, f16[1,160,256]{2,1,0:T(8,128)(2,1)S(1)}, u32[]{:S(2)}, u32[]{:S(2)}) collective-permute-start(f16[1,160,256]{2,1,0:T(8,128)(2,1)S(1)} %pad_bitcast_fusion), channel_id=1, source_target_pairs={{0,16},{4,20},{8,24},{12,28},{16,0},{20,4},{24,8},{28,12},{1,17},{... | collective-permute-start | bytes 245768 | tf_op jit(solution)/shard_map/ppermute | solution.py:21
  55.7 3.2 %collective-permute-done.11 = f16[160,256]{1,0:T(8,128)(2,1)S(1)} collective-permute-done((f16[160,256]{1,0:T(8,128)(2,1)S(1)}, f16[160,256]{1,0:T(8,128)(2,1)S(1)}, u32[]{:S(2)}, u32[]{:S(2)}) %collective-permute-start.11) | collective-permute-done | bytes 81952 | tf_op jit(solution)/shard_map/ppermute | solution.py:21
  60.9 4.5 %collective-permute-start.7 = (bf16[4,2,128]{2,1,0:T(2,128)(2,1)S(1)}, bf16[4,2,128]{2,1,0:T(2,128)(2,1)S(1)}, u32[]{:S(2)}, u32[]{:S(2)}) collective-permute-start(bf16[4,2,128]{2,1,0:T(2,128)(2,1)S(1)} %pad_maximum_fusion.7), channel_id=1, source_target_pairs={{0,4},{4,8},{8,12},{12,16},{16,20},{20,24},{24,28},{1,5},{5,9},{9,... | collective-permute-start | bytes 6152 | tf_op jit(solution)/shard_map/ppermute | solution.py:241
  65.8 3.0 %collective-permute-start.19 = (f16[2,160,256]{2,1,0:T(8,128)(2,1)S(1)}, f16[2,160,256]{2,1,0:T(8,128)(2,1)S(1)}, u32[]{:S(2)}, u32[]{:S(2)}) collective-permute-start(f16[2,160,256]{2,1,0:T(8,128)(2,1)S(1)} %pad_maximum_fusion.5), channel_id=1, source_target_pairs={{0,8},{4,12},{8,0},{12,4},{16,24},{20,28},{24,16},{28,20},{1,9},{5... | collective-permute-start | bytes 491528 | tf_op jit(solution)/shard_map/ppermute | solution.py:21
  68.9 3.0 %collective-permute-start.13 = (f16[2,160,256]{2,1,0:T(8,128)(2,1)S(1)}, f16[2,160,256]{2,1,0:T(8,128)(2,1)S(1)}, u32[]{:S(2)}, u32[]{:S(2)}) collective-permute-start(f16[2,160,256]{2,1,0:T(8,128)(2,1)S(1)} %pad_maximum_fusion.4), channel_id=1, source_target_pairs={{0,8},{4,12},{8,0},{12,4},{16,24},{20,28},{24,16},{28,20},{1,9},{5... | collective-permute-start | bytes 491528 | tf_op jit(solution)/shard_map/ppermute | solution.py:21
  72.3 2.3 %collective-permute-start.20 = (f16[4,160,256]{2,1,0:T(8,128)(2,1)S(1)}, f16[4,160,256]{2,1,0:T(8,128)(2,1)S(1)}, u32[]{:S(2)}, u32[]{:S(2)}) collective-permute-start(f16[4,160,256]{2,1,0:T(8,128)(2,1)S(1)} %pad_maximum_fusion.3), channel_id=1, source_target_pairs={{0,4},{4,0},{8,12},{12,8},{16,20},{20,16},{24,28},{28,24},{1,5},{5... | collective-permute-start | bytes 983048 | tf_op jit(solution)/shard_map/ppermute | solution.py:21
  76.4 2.1 %input_terms.1 = bf16[2,128,768]{2,1,0:T(8,128)(2,1)S(1)} custom-call(bf16[1152,512]{1,0:T(8,128)(2,1)S(1)} %bitcast.71, bf16[4,16,128]{2,1,0:T(8,128)(2,1)S(1)} %pad.16.edge_rows, bf16[2,128,768]{2,1,0:T(8,128)(2,1)S(1)} %bitcast.68, bf16[2,128,768]{2,1,0:T(8,128)(2,1)S(1)} %collective-permute-done.4.refs_1_.gb, ...), custom_call_target="tpu_custom_call" | custom-call | flops 1207959552 | bytes 3162112 | tf_op jit(solution)/shard_map/input_terms/pallas_call | solution.py:38
  80.6 2.6 %collective-permute-done.14 = f16[4,160,256]{2,1,0:T(8,128)(2,1)S(1)} collective-permute-done((f16[4,160,256]{2,1,0:T(8,128)(2,1)S(1)}, f16[4,160,256]{2,1,0:T(8,128)(2,1)S(1)}, u32[]{:S(2)}, u32[]{:S(2)}) %collective-permute-start.14) | collective-permute-done | bytes 327712 | tf_op jit(solution)/shard_map/ppermute | solution.py:21
  84.0 1.7 %maximum_bitcast_fusion = f32[128,3,3,512]{3,0,2,1:T(8,128)} fusion(f32[3,3,128,256]{3,2,1,0:T(8,128)S(1)} %bitcast.72, f32[3,3,128,256]{3,2,1,0:T(8,128)S(1)} %bitcast.73), kind=kLoop, calls=%fused_computation | loop fusion | flops 589824 | bytes 4718592 | tf_op jit(solution)/shard_map/transpose | solution.py:264
  85.8 6.1 %collective-permute-done.3 = f32[1,2,128,768]{3,2,1,0:T(8,128)S(1)} collective-permute-done((f32[1,2,128,768]{3,2,1,0:T(8,128)S(1)}, f32[1,2,128,768]{3,2,1,0:T(8,128)S(1)}, u32[]{:S(2)}, u32[]{:S(2)}) %collective-permute-start.3) | collective-permute-done | bytes 786464 | tf_op jit(solution)/shard_map/ppermute | solution.py:21
  (86 shorter events, 21.1 us)
Async XLA Ops:
  0.6 14.7 %copy-start = (bf16[128,2,768]{2,1,0:T(2,128)(2,1)S(1)}, bf16[128,2,768]{2,1,0:T(2,128)(2,1)}, u32[]{:S(2)}) copy-start(bf16[128,2,768]{2,1,0:T(2,128)(2,1)} %x.15) | copy-start | bytes 1179652
  1.7 15.2 %collective-permute-start.4 = (bf16[2,128,768]{2,1,0:T(8,128)(2,1)S(1)}, bf16[2,128,768]{2,1,0:T(8,128)(2,1)S(1)}, u32[]{:S(2)}, u32[]{:S(2)}) collective-permute-start(bf16[2,128,768]{2,1,0:T(8,128)(2,1)S(1)} %bitcast.64), channel_id=1, source_target_pairs={{0,1},{1,0},{2,3},{3,2},{4,5},{5,4},{6,7},{7,6},{8,9},{9,8},{10,11... | collective-permute-start | bytes 1179656 | tf_op jit(solution)/shard_map/ppermute | solution.py:21
  2.2 21.0 %collective-permute-start.5 = (bf16[2,128,768]{2,1,0:T(8,128)(2,1)S(1)}, bf16[2,128,768]{2,1,0:T(8,128)(2,1)S(1)}, u32[]{:S(2)}, u32[]{:S(2)}) collective-permute-start(bf16[2,128,768]{2,1,0:T(8,128)(2,1)S(1)} %bitcast.65), channel_id=1, source_target_pairs={{0,2},{1,3},{2,0},{3,1},{4,6},{5,7},{6,4},{7,5},{8,10},{9,11},{10,... | collective-permute-start | bytes 1179656 | tf_op jit(solution)/shard_map/ppermute | solution.py:21
  5.8 5.3 %collective-permute-start = (bf16[128,2,128]{2,1,0:T(2,128)(2,1)S(1)}, bf16[128,2,128]{2,1,0:T(2,128)(2,1)S(1)}, u32[]{:S(2)}, u32[]{:S(2)}) collective-permute-start(bf16[128,2,128]{2,1,0:T(2,128)(2,1)S(1)} %get-tuple-element.60), channel_id=1, source_target_pairs={{0,4},{4,8},{8,12},{12,16},{16,20},{20,24},{24,28},{1,5},{5,9},{9,... | collective-permute-start | bytes 196616 | tf_op jit(solution)/shard_map/ppermute | solution.py:199
  9.2 6.2 %collective-permute-start.1 = (bf16[128,2,128]{2,1,0:T(2,128)(2,1)S(1)}, bf16[128,2,128]{2,1,0:T(2,128)(2,1)S(1)}, u32[]{:S(2)}, u32[]{:S(2)}) collective-permute-start(bf16[128,2,128]{2,1,0:T(2,128)(2,1)S(1)} %get-tuple-element.59), channel_id=1, source_target_pairs={{4,0},{8,4},{12,8},{16,12},{20,16},{24,20},{28,24},{5,1},{9,5},{13... | collective-permute-start | bytes 196616 | tf_op jit(solution)/shard_map/ppermute | solution.py:200
  17.0 3.7 %copy-start.1 = (bf16[128,3,3,512]{3,0,2,1:T(8,128)(2,1)S(1)}, bf16[128,3,3,512]{3,0,2,1:T(8,128)(2,1)}, u32[]{:S(2)}) copy-start(bf16[128,3,3,512]{3,0,2,1:T(8,128)(2,1)} %param.4) | copy-start | bytes 3538948
  18.1 8.6 %collective-permute-start.15 = (f16[592,256]{1,0:T(8,128)(2,1)S(1)}, f16[592,256]{1,0:T(8,128)(2,1)S(1)}, u32[]{:S(2)}, u32[]{:S(2)}) collective-permute-start(f16[592,256]{1,0:T(8,128)(2,1)S(1)} %convert_element_type.77), channel_id=1, source_target_pairs={{0,4},{4,0},{8,12},{12,8},{16,20},{20,16},{24,28},{28,24},{1,5},{5... | collective-permute-start | bytes 909320 | tf_op jit(solution)/shard_map/ppermute | solution.py:21
  22.6 56.9 %collective-permute-start.2 = (f32[2,2,128,768]{3,2,1,0:T(8,128)S(1)}, f32[2,2,128,768]{3,2,1,0:T(8,128)S(1)}, u32[]{:S(2)}, u32[]{:S(2)}) collective-permute-start(f32[2,2,128,768]{3,2,1,0:T(8,128)S(1)} %get-tuple-element.10), channel_id=1, source_target_pairs={{0,1},{1,0},{2,3},{3,2},{4,5},{5,4},{6,7},{7,6},{8,9},{9,8},{10,11... | collective-permute-start | bytes 4718600 | tf_op jit(solution)/shard_map/ppermute | solution.py:21
  23.2 7.2 %collective-permute-start.6 = (bf16[2,128,768]{2,1,0:T(8,128)(2,1)S(1)}, bf16[2,128,768]{2,1,0:T(8,128)(2,1)S(1)}, u32[]{:S(2)}, u32[]{:S(2)}) collective-permute-start(bf16[2,128,768]{2,1,0:T(8,128)(2,1)S(1)} %collective-permute-done.5.refs_2_.ga), channel_id=1, source_target_pairs={{0,1},{1,0},{2,3},{3,2},{4,5},{5,4},{6,7},{7,6},{8,9},{9,8},{10,11... | collective-permute-start | bytes 1179656 | tf_op jit(solution)/shard_map/ppermute | solution.py:21
  28.8 5.3 %collective-permute-start.16 = (f16[304,256]{1,0:T(8,128)(2,1)S(1)}, f16[304,256]{1,0:T(8,128)(2,1)S(1)}, u32[]{:S(2)}, u32[]{:S(2)}) collective-permute-start(f16[304,256]{1,0:T(8,128)(2,1)S(1)} %concatenate.50), channel_id=1, source_target_pairs={{0,8},{4,12},{8,0},{12,4},{16,24},{20,28},{24,16},{28,20},{1,9},{5... | collective-permute-start | bytes 466952 | tf_op jit(solution)/shard_map/ppermute | solution.py:21
  31.5 10.6 %collective-permute-start.9 = (f16[592,256]{1,0:T(8,128)(2,1)S(1)}, f16[592,256]{1,0:T(8,128)(2,1)S(1)}, u32[]{:S(2)}, u32[]{:S(2)}) collective-permute-start(f16[592,256]{1,0:T(8,128)(2,1)S(1)} %convert_element_type.70), channel_id=1, source_target_pairs={{0,4},{4,0},{8,12},{12,8},{16,20},{20,16},{24,28},{28,24},{1,5},{5... | collective-permute-start | bytes 909320 | tf_op jit(solution)/shard_map/ppermute | solution.py:21
  35.4 5.4 %collective-permute-start.17 = (f16[160,256]{1,0:T(8,128)(2,1)S(1)}, f16[160,256]{1,0:T(8,128)(2,1)S(1)}, u32[]{:S(2)}, u32[]{:S(2)}) collective-permute-start(f16[160,256]{1,0:T(8,128)(2,1)S(1)} %concatenate.51), channel_id=1, source_target_pairs={{0,16},{4,20},{8,24},{12,28},{16,0},{20,4},{24,8},{28,12},{1,17},{... | collective-permute-start | bytes 245768 | tf_op jit(solution)/shard_map/ppermute | solution.py:21
  38.1 30.7 %collective-permute-start.8 = (bf16[4,2,128]{2,1,0:T(2,128)(2,1)S(1)}, bf16[4,2,128]{2,1,0:T(2,128)(2,1)S(1)}, u32[]{:S(2)}, u32[]{:S(2)}) collective-permute-start(bf16[4,2,128]{2,1,0:T(2,128)(2,1)S(1)} %pad_maximum_fusion.8), channel_id=1, source_target_pairs={{4,0},{8,4},{12,8},{16,12},{20,16},{24,20},{28,24},{5,1},{9,5},{13... | collective-permute-start | bytes 6152 | tf_op jit(solution)/shard_map/ppermute | solution.py:242
  44.1 7.1 %collective-permute-start.10 = (f16[304,256]{1,0:T(8,128)(2,1)S(1)}, f16[304,256]{1,0:T(8,128)(2,1)S(1)}, u32[]{:S(2)}, u32[]{:S(2)}) collective-permute-start(f16[304,256]{1,0:T(8,128)(2,1)S(1)} %concatenate.44), channel_id=1, source_target_pairs={{0,8},{4,12},{8,0},{12,4},{16,24},{20,28},{24,16},{28,20},{1,9},{5... | collective-permute-start | bytes 466952 | tf_op jit(solution)/shard_map/ppermute | solution.py:21
  52.6 6.3 %collective-permute-start.11 = (f16[160,256]{1,0:T(8,128)(2,1)S(1)}, f16[160,256]{1,0:T(8,128)(2,1)S(1)}, u32[]{:S(2)}, u32[]{:S(2)}) collective-permute-start(f16[160,256]{1,0:T(8,128)(2,1)S(1)} %concatenate.45), channel_id=1, source_target_pairs={{0,16},{4,20},{8,24},{12,28},{16,0},{20,4},{24,8},{28,12},{1,17},{... | collective-permute-start | bytes 245768 | tf_op jit(solution)/shard_map/ppermute | solution.py:21
  53.5 11.9 %collective-permute-start.18 = (f16[1,160,256]{2,1,0:T(8,128)(2,1)S(1)}, f16[1,160,256]{2,1,0:T(8,128)(2,1)S(1)}, u32[]{:S(2)}, u32[]{:S(2)}) collective-permute-start(f16[1,160,256]{2,1,0:T(8,128)(2,1)S(1)} %pad_bitcast_fusion), channel_id=1, source_target_pairs={{0,16},{4,20},{8,24},{12,28},{16,0},{20,4},{24,8},{28,12},{1,17},{... | collective-permute-start | bytes 245768 | tf_op jit(solution)/shard_map/ppermute | solution.py:21
  60.2 5.5 %collective-permute-start.12 = (f16[1,160,256]{2,1,0:T(8,128)(2,1)S(1)}, f16[1,160,256]{2,1,0:T(8,128)(2,1)S(1)}, u32[]{:S(2)}, u32[]{:S(2)}) collective-permute-start(f16[1,160,256]{2,1,0:T(8,128)(2,1)S(1)} %pad_bitcast_fusion.1), channel_id=1, source_target_pairs={{0,16},{4,20},{8,24},{12,28},{16,0},{20,4},{24,8},{28,12},{1,17},{... | collective-permute-start | bytes 245768 | tf_op jit(solution)/shard_map/ppermute | solution.py:21
  60.9 7.9 %collective-permute-start.7 = (bf16[4,2,128]{2,1,0:T(2,128)(2,1)S(1)}, bf16[4,2,128]{2,1,0:T(2,128)(2,1)S(1)}, u32[]{:S(2)}, u32[]{:S(2)}) collective-permute-start(bf16[4,2,128]{2,1,0:T(2,128)(2,1)S(1)} %pad_maximum_fusion.7), channel_id=1, source_target_pairs={{0,4},{4,8},{8,12},{12,16},{16,20},{20,24},{24,28},{1,5},{5,9},{9,... | collective-permute-start | bytes 6152 | tf_op jit(solution)/shard_map/ppermute | solution.py:241
  65.8 6.3 %collective-permute-start.19 = (f16[2,160,256]{2,1,0:T(8,128)(2,1)S(1)}, f16[2,160,256]{2,1,0:T(8,128)(2,1)S(1)}, u32[]{:S(2)}, u32[]{:S(2)}) collective-permute-start(f16[2,160,256]{2,1,0:T(8,128)(2,1)S(1)} %pad_maximum_fusion.5), channel_id=1, source_target_pairs={{0,8},{4,12},{8,0},{12,4},{16,24},{20,28},{24,16},{28,20},{1,9},{5... | collective-permute-start | bytes 491528 | tf_op jit(solution)/shard_map/ppermute | solution.py:21
  68.9 6.3 %collective-permute-start.13 = (f16[2,160,256]{2,1,0:T(8,128)(2,1)S(1)}, f16[2,160,256]{2,1,0:T(8,128)(2,1)S(1)}, u32[]{:S(2)}, u32[]{:S(2)}) collective-permute-start(f16[2,160,256]{2,1,0:T(8,128)(2,1)S(1)} %pad_maximum_fusion.4), channel_id=1, source_target_pairs={{0,8},{4,12},{8,0},{12,4},{16,24},{20,28},{24,16},{28,20},{1,9},{5... | collective-permute-start | bytes 491528 | tf_op jit(solution)/shard_map/ppermute | solution.py:21
  72.3 8.1 %collective-permute-start.20 = (f16[4,160,256]{2,1,0:T(8,128)(2,1)S(1)}, f16[4,160,256]{2,1,0:T(8,128)(2,1)S(1)}, u32[]{:S(2)}, u32[]{:S(2)}) collective-permute-start(f16[4,160,256]{2,1,0:T(8,128)(2,1)S(1)} %pad_maximum_fusion.3), channel_id=1, source_target_pairs={{0,4},{4,0},{8,12},{12,8},{16,20},{20,16},{24,28},{28,24},{1,5},{5... | collective-permute-start | bytes 983048 | tf_op jit(solution)/shard_map/ppermute | solution.py:21
  75.4 7.8 %collective-permute-start.14 = (f16[4,160,256]{2,1,0:T(8,128)(2,1)S(1)}, f16[4,160,256]{2,1,0:T(8,128)(2,1)S(1)}, u32[]{:S(2)}, u32[]{:S(2)}) collective-permute-start(f16[4,160,256]{2,1,0:T(8,128)(2,1)S(1)} %pad_maximum_fusion.2), channel_id=1, source_target_pairs={{0,4},{4,0},{8,12},{12,8},{16,20},{20,16},{24,28},{28,24},{1,5},{5... | collective-permute-start | bytes 983048 | tf_op jit(solution)/shard_map/ppermute | solution.py:21
  79.8 12.1 %collective-permute-start.3 = (f32[1,2,128,768]{3,2,1,0:T(8,128)S(1)}, f32[1,2,128,768]{3,2,1,0:T(8,128)S(1)}, u32[]{:S(2)}, u32[]{:S(2)}) collective-permute-start(f32[1,2,128,768]{3,2,1,0:T(8,128)S(1)} %slice.161), channel_id=1, source_target_pairs={{0,2},{1,3},{2,0},{3,1},{4,6},{5,7},{6,4},{7,5},{8,10},{9,11},{10,... | collective-permute-start | bytes 2359304 | tf_op jit(solution)/shard_map/ppermute | solution.py:21

commit v2 on v1

v2 whole, which is shorter than its diff:
```python
import functools
import math

import jax
import jax.numpy as jnp
from jax import lax
from jax.experimental import pallas as pl
from jax.experimental.pallas import tpu as pltpu
from jax.sharding import PartitionSpec as P

BF16, F16, F32 = jnp.bfloat16, jnp.float16, jnp.float32
LANES = 128
TOP = 14.0
LEAST = 2.0**-110
POWER = 8
EDGE = 8
VMEM = pl.BlockSpec(memory_space=pltpu.VMEM)
NT = (((1,), (1,)), ((), ()))
TN = (((0,), (0,)), ((), ()))


def exchange(value, axis, bit):
    devices = lax.axis_size(axis)
    return lax.ppermute(value, axis, [(i, i ^ bit) for i in range(devices)])


def bits_of(devices):
    return devices.bit_length() - 1


def reversed_bits(index, count):
    out = 0
    for b in range(count):
        out = out + (((index >> b) & 1) << (count - 1 - b))
    return out


def call(body, name, outs, scratch, flops, *args):
    outs = [jax.ShapeDtypeStruct(shape, dtype) for shape, dtype in outs]
    moved = sum(a.size * a.dtype.itemsize for a in list(args) + outs)
    result = pl.pallas_call(
        body,
        out_shape=outs,
        in_specs=[VMEM] * len(args),
        out_specs=[VMEM] * len(outs),
        scratch_shapes=[pltpu.VMEM(shape, dtype) for shape, dtype in scratch],
        compiler_params=pltpu.CompilerParams(vmem_limit_bytes=16 << 20),
        cost_estimate=pl.CostEstimate(flops=flops, bytes_accessed=moved, transcendentals=0),
        name=name,
    )(*args)
    return result[0] if len(outs) == 1 else result


def exponent(values):
    most = jnp.max(jnp.abs(values), axis=(0, 1), keepdims=True)
    return jnp.ceil(jnp.log2(jnp.maximum(most, LEAST)))


def taps_kernel(x, *refs):
    *ends, out = refs
    chans, rows, cols = x.shape
    if ends:
        tiles = ends[0].shape[0]
        tile = lax.axis_index("width")
        left = ends[0][jnp.maximum(tile - 1, 0)]
        right = ends[0][jnp.minimum(tile + 1, tiles - 1)]
        left = jnp.where(tile > 0, left[3:4] * jnp.exp2(left[0:1] - TOP), 0.0)
        right = jnp.where(tile < tiles - 1, right[2:3] * jnp.exp2(right[0:1] - TOP), 0.0)
        row_of = lax.broadcasted_iota(jnp.int32, (16, LANES), 0)
        lane = lax.broadcasted_iota(jnp.int32, (16, LANES), 1)
        place = ((row_of == 0) & (lane == LANES - 1)) | ((row_of == 1) & (lane == 0))
        place = jnp.where(place, 1.0, 0.0).astype(BF16)
    for i in range(rows):
        side = jnp.zeros((chans, LANES), BF16)
        if ends:
            at = slice(i * chans, (i + 1) * chans)
            both = jnp.concatenate([left[:, at], right[:, at], jnp.zeros((14, chans), F32)], axis=0).astype(BF16)
            side = lax.dot_general(both, place, TN, preferred_element_type=F32).astype(BF16)
        row = jnp.concatenate([side, x[:, i, :], side], axis=1)
        for b in range(3):
            out[i, b * chans : (b + 1) * chans, :] = row[:, LANES - 1 + b : LANES - 1 + b + cols]


def filter_kernel(factor, piece, first, xs, ga, gb, send, keep, gsc, acc):
    rows, deep, cols = xs.shape
    chans = deep // 3
    width = lax.axis_size("width")
    block = ga.shape[1]
    lanes = 2 * block
    parity = lax.axis_index("chan") & 1
    gsc[:, pl.ds(pl.multiple_of(parity * block, block), block), :] = ga[...]
    gsc[:, pl.ds(pl.multiple_of((1 - parity) * block, block), block), :] = gb[...]
    for a in range(3):
        total = None
        for h in range(rows):
            i = h + a - 1
            if 0 <= i < rows:
                part = lax.dot_general(xs[i], gsc[h], NT, preferred_element_type=F32)
                total = part if total is None else total + part
        acc[a * deep : (a + 1) * deep, :] = total * factor
    if acc.shape[0] > 3 * deep:
        acc[3 * deep :, :] = jnp.zeros((acc.shape[0] - 3 * deep, lanes), F32)
    power = exponent(acc[...])
    mine = reversed_bits(lax.axis_index("width"), bits_of(width))
    half = width // 2
    for r in range(width):
        rows_of = acc[pl.ds(pl.multiple_of((mine ^ r) * piece, 16), piece), :]
        if r < half:
            keep[r * piece : (r + 1) * piece, :] = rows_of
        else:
            send[(r - half) * piece : (r - half + 1) * piece, :] = rows_of * jnp.exp2(TOP - power)
    power = jnp.broadcast_to(power, (POWER, lanes))
    send[half * piece : half * piece + POWER, :] = power
    keep[half * piece :, :] = power
    row_of = lax.broadcasted_iota(jnp.int32, (16, cols), 0)
    lane = lax.broadcasted_iota(jnp.int32, (16, cols), 1)
    pick = ((row_of == 0) & (lane == 0)) | ((row_of == 1) & (lane == cols - 1))
    pick = jnp.where(pick, 1.0, 0.0).astype(BF16)
    gends = [lax.dot_general(pick, gsc[h], NT, preferred_element_type=F32) for h in range(rows)]
    gends = jnp.concatenate([gends[h][s : s + 1] for s in range(2) for h in range(rows)], axis=0)
    if first:
        xends = [lax.dot_general(pick, xs[i, chans : 2 * chans], NT, preferred_element_type=F32) for i in range(rows)]
        xends = jnp.concatenate([v[:2] for v in xends], axis=1)
    else:
        xends = jnp.zeros((2, lanes), F32)
    xpower, gpower = exponent(xends), exponent(gends)
    send[half * piece + POWER :, :] = jnp.concatenate(
        [
            jnp.broadcast_to(xpower, (1, lanes)),
            jnp.broadcast_to(gpower, (1, lanes)),
            xends * jnp.exp2(TOP - xpower),
            gends * jnp.exp2(TOP - gpower),
        ],
        axis=0,
    )


def border_kernel(factor, total, xends, gends, out, acc):
    tiles, _, lanes = gends.shape
    piece = total.shape[0]
    rows = 2
    chans = lanes // rows
    tile = lax.broadcasted_iota(jnp.int32, (tiles, lanes), 0)

    def decoded(ref, kind, power):
        return ref[:, kind, :] * jnp.exp2(ref[:, power, :] - TOP)

    before = jnp.where(tile == 0, 0.0, pltpu.roll(decoded(xends, 3, 0), 1, 0))
    behind = jnp.where(tile == tiles - 1, 0.0, pltpu.roll(decoded(xends, 2, 0), tiles - 1, 0))
    acc[...] = jnp.zeros(acc.shape, F32)
    for b, source, kind in ((0, before, 4), (2, behind, 4 + rows)):
        grads = jnp.concatenate([decoded(gends, kind + h, 1) for h in range(rows)], axis=0).astype(BF16)
        nothing = jnp.zeros((tiles, chans), F32)
        for a in range(3):
            taken = [h + a - 1 for h in range(rows)]
            taken = [source[:, i * chans : (i + 1) * chans] if 0 <= i < rows else nothing for i in taken]
            terms = lax.dot_general(jnp.concatenate(taken, axis=0).astype(BF16), grads, TN, preferred_element_type=F32)
            acc[(3 * a + b) * chans : (3 * a + b + 1) * chans, :] = terms * factor
    mine = reversed_bits(lax.axis_index("width"), bits_of(tiles))
    value = total[...] + acc[pl.ds(pl.multiple_of(mine * piece, 16), piece), :]
    power = exponent(value)
    out[:piece, :] = value * jnp.exp2(TOP - power)
    out[piece:, :] = jnp.broadcast_to(power, (POWER, lanes))


def forward_kernel(xs, f, send, keep, acc):
    rows, deep, cols = xs.shape
    groups = lax.axis_size("chan")
    nbits = bits_of(groups)
    block = acc.shape[0] // groups
    me = lax.axis_index("chan")
    for h in range(rows):
        total = None
        for i in range(max(0, h - 1), min(rows, h + 2)):
            part = lax.dot_general(f[i - h + 1], xs[i], TN, preferred_element_type=F32)
            total = part if total is None else total + part
        acc[...] = total
        for q in range(groups):
            owner = me ^ reversed_bits(q, nbits)
            rows_of = acc[pl.ds(pl.multiple_of(owner * block, block), block), :]
            if q < groups // 2:
                keep[q, h] = rows_of
            else:
                send[q - groups // 2, h] = rows_of


def input_kernel(f, ends, *refs):
    groups = lax.axis_size("chan")
    gs, (out, gsc, hsc) = refs[:groups], refs[groups:]
    rows, block, cols = gs[0].shape
    chans = out.shape[1]
    tiles = ends.shape[1]
    lanes = 2 * block
    me, tile = lax.axis_index("chan"), lax.axis_index("width")
    for r in range(groups):
        gsc[:, pl.ds(pl.multiple_of((me ^ r) * block, block), block), :] = gs[r][...]
    for q in range(groups // 2):
        left = ends[(me >> 1) ^ q, jnp.maximum(tile - 1, 0)]
        right = ends[(me >> 1) ^ q, jnp.minimum(tile + 1, tiles - 1)]
        left = jnp.where(tile > 0, left * jnp.exp2(left[1:2] - TOP), 0.0)
        right = jnp.where(tile < tiles - 1, right * jnp.exp2(right[1:2] - TOP), 0.0)
        both = jnp.concatenate([left[4 + rows :], right[4 : 4 + rows], jnp.zeros((16 - 2 * rows, lanes), F32)], axis=0)
        hsc[:, q * lanes : (q + 1) * lanes] = both.astype(BF16)
    lane = lax.broadcasted_iota(jnp.int32, (chans, cols), 1)
    sums = [None] * rows
    for i in range(rows):
        taps = [a for a in range(3) if 0 <= a - 1 + i < rows]
        mats = f[taps[0] * 3 * chans : (taps[-1] + 1) * 3 * chans, :]
        prod = jnp.dot(mats, gsc[i], preferred_element_type=F32)
        sides = lax.dot_general(mats, hsc[...], NT, preferred_element_type=F32)
        for n, a in enumerate(taps):
            h = a - 1 + i
            for b in range(3):
                at = slice((n * 3 + b) * chans, (n * 3 + b + 1) * chans)
                term = prod[at]
                if b == 0:
                    term = jnp.where(lane == cols - 1, sides[at, rows + i : rows + i + 1], pltpu.roll(term, cols - 1, 1))
                elif b == 2:
                    term = jnp.where(lane == 0, sides[at, i : i + 1], pltpu.roll(term, 1, 1))
                sums[h] = term if sums[h] is None else sums[h] + term
    for h in range(rows):
        out[h] = sums[h].astype(BF16)


class Order:
    def __init__(self):
        self.last = None

    def __call__(self, value):
        if self.last is not None:
            value, _ = lax.optimization_barrier((value, self.last))
        self.last = value
        return value


def doubled(got, own, bit):
    late = (lax.axis_index("width") & bit) != 0
    return jnp.concatenate([jnp.where(late, got, own), jnp.where(late, own, got)], axis=0)


def chunk_stages(send, keep, finish, order):
    steps = bits_of(lax.axis_size("width"))
    lanes = send.shape[1]
    total, power = keep[:-POWER], keep[-1:]
    message = send.astype(F16)
    ends = message[-EDGE:][None]
    for b in range(steps):
        got = exchange(order(message), "width", 1 << b)
        yield None
        got = order(got)
        count = total.shape[0]
        other = got[count : count + 1].astype(F32)
        total = total + got[:count].astype(F32) * jnp.exp2(other - TOP)
        power = jnp.maximum(power, other) + 1.0
        ends = doubled(got[count + POWER :].reshape(-1, EDGE, lanes), ends, 1 << b)
        if b < steps - 1:
            scaled = total[count // 2 :] * jnp.exp2(TOP - power)
            tail = jnp.broadcast_to(power, (POWER, lanes))
            message = jnp.concatenate([scaled.astype(F16), tail.astype(F16), ends.reshape(-1, lanes)], axis=0)
            total = total[: count // 2]
    every = finish(total, ends.astype(F32)).astype(F16)[None]
    for b in reversed(range(steps)):
        got = exchange(order(every), "width", 1 << b)
        yield None
        every = doubled(order(got), every, 1 << b)
    yield every


def unpacked(every):
    rows = every.shape[1] - POWER
    scale = jnp.exp2(every[:, rows : rows + 1].astype(F32) - TOP)
    return (every[:, :rows].astype(F32) * scale).reshape(-1, every.shape[2])


def chunk_times(chunks, steps):
    times = []
    for j in range(chunks):
        now = 2.6 * j
        for step in range(2 * steps + 1):
            times.append((now, j))
            now += 2.0 if step in (0, 2 * steps - 1) else 1.0
    return sorted(times)


def body(activations, filters, cotangent):
    chans, rows, cols = activations.shape
    block = cotangent.shape[0]
    outs = filters.shape[3]
    groups, width = lax.axis_size("chan"), lax.axis_size("width")
    me = lax.axis_index("chan")
    lanes = 2 * block
    mats = jnp.transpose(filters, (1, 2, 0, 3))
    pairs_of_rows = sum(0 <= h + a - 1 < rows for h in range(rows) for a in range(3))
    flops = 2 * pairs_of_rows * 3 * chans * cols * outs
    piece = -(-9 * chans // width)
    piece = -(-piece // 16) * 16
    factor = 1.0 / math.sqrt(rows * cols * width)
    order = Order()
    ends = {}

    def shifted(*sides):
        return call(taps_kernel, "shifted_taps", [((rows, 3 * chans, cols), BF16)], [], 0, activations, *sides)

    def filter_chunk(j):
        send, keep = call(
            functools.partial(filter_kernel, factor, piece, j == 0),
            "filter_terms",
            [((width // 2 * piece + POWER + EDGE, lanes), F32), ((width // 2 * piece + POWER, lanes), F32)],
            [((rows, lanes, cols), BF16), ((width * piece, lanes), F32)],
            flops * 2 // groups,
            bare,
            g[2 * j],
            g[2 * j + 1],
        )

        def finish(total, arrived):
            ends[j] = arrived
            body = functools.partial(border_kernel, factor)
            shape = ((piece + POWER, lanes), F32)
            return call(body, "border_terms", [shape], [((width * piece, lanes), F32)], 0, total, ends[0], ends[j])

        return chunk_stages(send, keep, finish, order)

    def forward():
        send, keep = call(
            forward_kernel,
            "forward_terms",
            [((groups // 2, rows, block, cols), F32)] * 2,
            [((outs, cols), F32)],
            flops,
            shifted(order(ends[0])),
            mats.reshape(3, 3 * chans, outs),
        )
        for b in range(bits_of(groups)):
            got = exchange(order(send), "chan", 1 << b)
            yield None
            total = keep + order(got)
            keep, send = total[: total.shape[0] // 2], total[total.shape[0] // 2 :]
        yield jnp.transpose(total[0].astype(BF16), (1, 0, 2))

    def backward():
        out = call(
            input_kernel,
            "input_terms",
            [((rows, chans, cols), BF16)],
            [((rows, outs, cols), BF16), ((16, outs), BF16)],
            flops,
            mats.reshape(9 * chans, outs),
            jnp.stack([order(ends[j]) for j in range(groups // 2)]),
            *[g[r] for r in range(groups)],
        )
        return jnp.transpose(out, (1, 0, 2))

    g = {0: order(jnp.transpose(cotangent, (1, 0, 2)))}
    g[1] = exchange(g[0], "chan", 1)
    for b in reversed(range(1, bits_of(groups))):
        for r in [r for r in sorted(g) if r != 1]:
            g[r | 1 << b] = exchange(g[r], "chan", 1 << b)
    bare = shifted()
    chunks = [filter_chunk(0)]
    next(chunks[0])
    for r in sorted(g):
        if r > 1:
            g[r | 1] = exchange(order(g[r]), "chan", 1)
    pieces = [None] * (groups // 2)
    conv = forward()
    waits = bits_of(groups) + 1
    for now, j in chunk_times(groups // 2, bits_of(width))[1:]:
        if j == len(chunks):
            g[2 * j + 1] = order(g[2 * j + 1])
            chunks.append(filter_chunk(j))
        pieces[j] = next(chunks[j])
        if 0 in ends and waits > 1 and (waits > bits_of(groups) or now > 6.2):
            conv_output = next(conv)
            waits -= 1
    input_grad = backward()
    while waits:
        conv_output = next(conv)
        waits -= 1

    for b in range(bits_of(groups // 2)):
        swap = ((me >> (b + 1)) & 1) == 1
        pieces = [jnp.where(swap, pieces[j ^ 1 << b], pieces[j]) for j in range(len(pieces))]
    grads = jnp.concatenate([unpacked(p) for p in pieces], axis=1)[: 9 * chans]
    grads = jnp.transpose(grads.reshape(3, 3, chans, outs), (2, 0, 1, 3))
    return conv_output, input_grad, grads


def solution(mesh):
    cols = P("chan", None, "width")
    mats = P("chan", None, None, None)
    return jax.shard_map(body, mesh=mesh, in_specs=(cols, mats, cols), out_specs=(cols, cols, mats), check_vma=False)
```

time: 93.5 us -> 89.3 us (0.955)
  starting transfers between devices: 39.4 us -> 19.9 us
  waiting for transfers between devices: 25.8 us -> 39.2 us
  other arithmetic: 3.96 us -> 12.7 us
  between operations: 6.75 us -> 1.12 us
  local copies, waits for them, and re-layouts: 9.46 us -> 6.16 us
  Pallas kernels: 7.78 us -> 9.76 us
    ppermute x17, waiting for transfers between devices: 21.1 us -> 39.2 us  [exchange(): return lax.ppermute(value, axis, [(i, i ^ bit) for i in range(devices)])]
    ppermute x4 -> x0, starting transfers between devices: 10.5 us -> none  [the longest x1 4.51 us: body(): left = lax.ppermute(lasts, 'width', up)]
    ppermute x17, starting transfers between devices: 28.9 us -> 19.9 us  [exchange(): return lax.ppermute(value, axis, [(i, i ^ bit) for i in range(devices)])]
    slice x14 -> x1, local copies, waits for them, and re-layouts: 5.9 us -> 0.98 us  [forward(): keep, send = (total[:total.shape[0] // 2], total[total.shape[0] // 2:])]
    ppermute x4 -> x0, waiting for transfers between devices: 4.67 us -> none  [the longest x1 4.27 us: body(): after = lax.ppermute(activations[:, :, :edge], 'width', down)]
    select_n x5 -> x11, other arithmetic: 0.6 us -> 3.91 us  [doubled(): jnp.where(late, got, own)]
    add x5 -> x7, other arithmetic: 0.38 us -> 2.49 us  [the longest x6 2.19 us: chunk_stages(): total = total + got[:count].astype(F32) * jnp.exp2(other - TOP)]
    pallas_call x5 -> x8, Pallas kernels: 7.78 us -> 9.76 us  [call(): pl.pallas_call(body, out_shape=outs, in_specs=[VMEM] * len(args), out_spe...]
  transfers between devices with their start and end apart: 21 -> 17, of which waited for: 12 -> 12; matrix products, arithmetic and copies ran while one was open for 12% -> 12% of each run, Pallas kernels for 8% -> 11%
where the time goes in v2:
time: 89.3 us; the launch traced here: 88.8 us
  waiting for transfers between devices  39.2 us (44%)
  starting transfers between devices  19.9 us (22%)
  other arithmetic  12.7 us (14%)
  Pallas kernels  9.76 us (11%)
  local copies, waits for them, and re-layouts  6.16 us (7%)
  between operations  1.12 us (1%)
    ppermute x17, waiting for transfers between devices, exchange(): return lax.ppermute(value, axis, [(i, i ^ bit) for i in range(devices)])  39.2 us
    ppermute x17, starting transfers between devices, exchange(): return lax.ppermute(value, axis, [(i, i ^ bit) for i in range(devices)])  19.9 us
    pallas_call x8, Pallas kernels, call(): pl.pallas_call(body, out_shape=outs, in_specs=[VMEM] * len(args), out_spe...  9.76 us
    unnamed x35, local copies, waits for them, and re-layouts  5.14 us
    select_n x11, other arithmetic, doubled(): jnp.where(late, got, own)  3.91 us
    add x6, other arithmetic, chunk_stages(): total = total + got[:count].astype(F32) * jnp.exp2(other - TOP)  2.19 us
  transfers between devices with their start and end apart: 17, of which 12 were waited for; matrix products, arithmetic and copies ran while one was open for 12% of the time, Pallas kernels for 11%

profile of v2, /device:TPU:0, one launch (start us, length us, event | category | flops | bytes accessed | tf_op | source)
XLA Modules:
  0.0 88.8 jit_solution(9631819637097427289)
XLA Ops:
  2.2 2.6 %collective-permute-start.2 = (bf16[2,128,768]{2,1,0:T(8,128)(2,1)S(1)}, bf16[2,128,768]{2,1,0:T(8,128)(2,1)S(1)}, u32[]{:S(2)}, u32[]{:S(2)}) collective-permute-start(bf16[2,128,768]{2,1,0:T(8,128)(2,1)S(1)} %bitcast.74), channel_id=1, source_target_pairs={{0,2},{1,3},{2,0},{3,1},{4,6},{5,7},{6,4},{7,5},{8,10},{9,11},{10,... | collective-permute-start | bytes 1179656 | tf_op jit(solution)/shard_map/ppermute | solution.py:24
  8.3 1.6 %collective-permute-start.1 = (f16[592,256]{1,0:T(8,128)(2,1)S(1)}, f16[592,256]{1,0:T(8,128)(2,1)}, u32[]{:S(2)}, u32[]{:S(2)}) collective-permute-start(f16[592,256]{1,0:T(8,128)(2,1)S(1)} %convert_element_type.112), channel_id=1, source_target_pairs={{0,4},{4,0},{8,12},{12,8},{16,20},{20,16},{24,28},{28,24},{1,5},{5... | collective-permute-start | bytes 909320 | tf_op jit(solution)/shard_map/ppermute | solution.py:24
  9.8 4.7 %collective-permute-done.2.ga.refs_2_ = bf16[2,128,768]{2,1,0:T(8,128)(2,1)S(1)} collective-permute-done((bf16[2,128,768]{2,1,0:T(8,128)(2,1)S(1)}, bf16[2,128,768]{2,1,0:T(8,128)(2,1)S(1)}, u32[]{:S(2)}, u32[]{:S(2)}) %collective-permute-start.2) | collective-permute-done | bytes 393248 | tf_op jit(solution)/shard_map/ppermute | solution.py:24
  14.5 3.2 %collective-permute-done.1 = f16[592,256]{1,0:T(8,128)(2,1)} collective-permute-done((f16[592,256]{1,0:T(8,128)(2,1)S(1)}, f16[592,256]{1,0:T(8,128)(2,1)}, u32[]{:S(2)}, u32[]{:S(2)}) %collective-permute-start.1) | collective-permute-done | bytes 303136 | tf_op jit(solution)/shard_map/ppermute | solution.py:24
  20.9 1.6 %collective-permute-start.3 = (f16[312,256]{1,0:T(8,128)(2,1)}, f16[312,256]{1,0:T(8,128)(2,1)}, u32[]{:S(2)}, u32[]{:S(2)}) collective-permute-start(f16[312,256]{1,0:T(8,128)(2,1)} %pad_maximum_fusion.4), channel_id=1, source_target_pairs={{0,8},{4,12},{8,0},{12,4},{16,24},{20,28},{24,16},{28,20},{1,9},{5... | collective-permute-start | bytes 479240 | tf_op jit(solution)/shard_map/ppermute | solution.py:24
  23.7 2.9 %collective-permute-done.3 = f16[312,256]{1,0:T(8,128)(2,1)} collective-permute-done((f16[312,256]{1,0:T(8,128)(2,1)}, f16[312,256]{1,0:T(8,128)(2,1)}, u32[]{:S(2)}, u32[]{:S(2)}) %collective-permute-start.3) | collective-permute-done | bytes 159776 | tf_op jit(solution)/shard_map/ppermute | solution.py:24
  29.1 2.6 %collective-permute-start.5 = (f16[184,256]{1,0:T(8,128)(2,1)S(1)}, f16[184,256]{1,0:T(8,128)(2,1)S(1)}, u32[]{:S(2)}, u32[]{:S(2)}) collective-permute-start(f16[184,256]{1,0:T(8,128)(2,1)S(1)} %pad_maximum_fusion.9), channel_id=1, source_target_pairs={{0,16},{4,20},{8,24},{12,28},{16,0},{20,4},{24,8},{28,12},{1,17},{... | collective-permute-start | bytes 282632 | tf_op jit(solution)/shard_map/ppermute | solution.py:24
  31.8 1.5 %collective-permute-start.7 = (f16[592,256]{1,0:T(8,128)(2,1)S(1)}, f16[592,256]{1,0:T(8,128)(2,1)S(1)}, u32[]{:S(2)}, u32[]{:S(2)}) collective-permute-start(f16[592,256]{1,0:T(8,128)(2,1)S(1)} %convert_element_type.118), channel_id=1, source_target_pairs={{0,4},{4,0},{8,12},{12,8},{16,20},{20,16},{24,28},{28,24},{1,5},{5... | collective-permute-start | bytes 909320 | tf_op jit(solution)/shard_map/ppermute | solution.py:24
  35.3 2.7 %collective-permute-start.9 = (f16[1,152,256]{2,1,0:T(8,128)(2,1)S(1)}, f16[1,152,256]{2,1,0:T(8,128)(2,1)S(1)}, u32[]{:S(2)}, u32[]{:S(2)}) collective-permute-start(f16[1,152,256]{2,1,0:T(8,128)(2,1)S(1)} %convert_bitcast_fusion.1), channel_id=1, source_target_pairs={{0,16},{4,20},{8,24},{12,28},{16,0},{20,4},{24,8},{28,12},{1,17},{... | collective-permute-start | bytes 233480 | tf_op jit(solution)/shard_map/ppermute | solution.py:24
  39.2 2.0 %forward_terms.1 = (f32[2,2,128,768]{3,2,1,0:T(8,128)S(1)}, f32[2,2,128,768]{3,2,1,0:T(8,128)S(1)}) custom-call(bf16[2,384,768]{2,1,0:T(8,128)(2,1)S(1)} %shifted_taps.3.xs, bf16[3,384,512]{2,1,0:T(8,128)(2,1)S(1)} %bitcast.78), custom_call_target="tpu_custom_call" | custom-call | flops 1207959552 | bytes 5505024 | tf_op jit(solution)/shard_map/forward_terms/pallas_call | solution.py:41
  41.6 2.4 %collective-permute-start.8 = (f16[312,256]{1,0:T(8,128)(2,1)S(1)}, f16[312,256]{1,0:T(8,128)(2,1)S(1)}, u32[]{:S(2)}, u32[]{:S(2)}) collective-permute-start(f16[312,256]{1,0:T(8,128)(2,1)S(1)} %pad_maximum_fusion.5), channel_id=1, source_target_pairs={{0,8},{4,12},{8,0},{12,4},{16,24},{20,28},{24,16},{28,20},{1,9},{5... | collective-permute-start | bytes 479240 | tf_op jit(solution)/shard_map/ppermute | solution.py:24
  44.2 4.8 %collective-permute-done.8 = f16[312,256]{1,0:T(8,128)(2,1)S(1)} collective-permute-done((f16[312,256]{1,0:T(8,128)(2,1)S(1)}, f16[312,256]{1,0:T(8,128)(2,1)S(1)}, u32[]{:S(2)}, u32[]{:S(2)}) %collective-permute-start.8) | collective-permute-done | bytes 159776 | tf_op jit(solution)/shard_map/ppermute | solution.py:24
  49.2 2.9 %collective-permute-done.11 = f16[2,152,256]{2,1,0:T(8,128)(2,1)S(1)} collective-permute-done((f16[2,152,256]{2,1,0:T(8,128)(2,1)S(1)}, f16[2,152,256]{2,1,0:T(8,128)(2,1)S(1)}, u32[]{:S(2)}, u32[]{:S(2)}) %collective-permute-start.11) | collective-permute-done | bytes 155680 | tf_op jit(solution)/shard_map/ppermute | solution.py:24
  52.3 4.2 %collective-permute-done.10 = f16[184,256]{1,0:T(8,128)(2,1)S(1)} collective-permute-done((f16[184,256]{1,0:T(8,128)(2,1)S(1)}, f16[184,256]{1,0:T(8,128)(2,1)S(1)}, u32[]{:S(2)}, u32[]{:S(2)}) %collective-permute-start.10) | collective-permute-done | bytes 94240 | tf_op jit(solution)/shard_map/ppermute | solution.py:24
  57.5 1.5 %collective-permute-start.15 = (f16[4,152,256]{2,1,0:T(8,128)(2,1)S(1)}, f16[4,152,256]{2,1,0:T(8,128)(2,1)S(1)}, u32[]{:S(2)}, u32[]{:S(2)}) collective-permute-start(f16[4,152,256]{2,1,0:T(8,128)(2,1)S(1)} %pad_maximum_fusion.2), channel_id=1, source_target_pairs={{0,4},{4,0},{8,12},{12,8},{16,20},{20,16},{24,28},{28,24},{1,5},{5... | collective-permute-start | bytes 933896 | tf_op jit(solution)/shard_map/ppermute | solution.py:24
  60.3 2.7 %collective-permute-done.13 = f16[1,152,256]{2,1,0:T(8,128)(2,1)S(1)} collective-permute-done((f16[1,152,256]{2,1,0:T(8,128)(2,1)S(1)}, f16[1,152,256]{2,1,0:T(8,128)(2,1)S(1)}, u32[]{:S(2)}, u32[]{:S(2)}) %collective-permute-start.13) | collective-permute-done | bytes 77856 | tf_op jit(solution)/shard_map/ppermute | solution.py:24
  63.2 2.9 %collective-permute-done.15 = f16[4,152,256]{2,1,0:T(8,128)(2,1)S(1)} collective-permute-done((f16[4,152,256]{2,1,0:T(8,128)(2,1)S(1)}, f16[4,152,256]{2,1,0:T(8,128)(2,1)S(1)}, u32[]{:S(2)}, u32[]{:S(2)}) %collective-permute-start.15) | collective-permute-done | bytes 311328 | tf_op jit(solution)/shard_map/ppermute | solution.py:24
  66.1 2.3 %collective-permute-done.14 = f16[2,152,256]{2,1,0:T(8,128)(2,1)S(1)} collective-permute-done((f16[2,152,256]{2,1,0:T(8,128)(2,1)S(1)}, f16[2,152,256]{2,1,0:T(8,128)(2,1)S(1)}, u32[]{:S(2)}, u32[]{:S(2)}) %collective-permute-start.14) | collective-permute-done | bytes 155680 | tf_op jit(solution)/shard_map/ppermute | solution.py:24
  70.3 1.6 %collective-permute-start.16 = (f16[4,152,256]{2,1,0:T(8,128)(2,1)S(1)}, f16[4,152,256]{2,1,0:T(8,128)(2,1)S(1)}, u32[]{:S(2)}, u32[]{:S(2)}) collective-permute-start(f16[4,152,256]{2,1,0:T(8,128)(2,1)S(1)} %pad_maximum_fusion.3), channel_id=1, source_target_pairs={{0,4},{4,0},{8,12},{12,8},{16,20},{20,16},{24,28},{28,24},{1,5},{5... | collective-permute-start | bytes 933896 | tf_op jit(solution)/shard_map/ppermute | solution.py:24
  72.4 4.9 %collective-permute-done.16 = f16[4,152,256]{2,1,0:T(8,128)(2,1)S(1)} collective-permute-done((f16[4,152,256]{2,1,0:T(8,128)(2,1)S(1)}, f16[4,152,256]{2,1,0:T(8,128)(2,1)S(1)}, u32[]{:S(2)}, u32[]{:S(2)}) %collective-permute-start.16) | collective-permute-done | bytes 311328 | tf_op jit(solution)/shard_map/ppermute | solution.py:24
  77.3 1.5 %broadcast_select_fusion.3 = (f16[4,152,256]{2,1,0:T(8,128)(2,1)S(1)}, f16[4,152,256]{2,1,0:T(8,128)(2,1)S(1)}, f16[4,152,256]{2,1,0:T(8,128)(2,1)S(1)}, f16[4,152,256]{2,1,0:T(8,128)(2,1)S(1)}) fusion(f16[4,152,256]{2,1,0:T(8,128)(2,1)} %copy-done.12, pred[]{:T(512)S(6)} %ne.7, f16[2,152,256]{2,1,0:T(8,128)(2,1)} %copy-done.11, ...), kind=kLoop, calls=%fused_computation.16 | loop fusion | flops 933888 | bytes 2490369 | tf_op jit(solution)/shard_map/jit(_where)/select_n | solution.py:238
  80.0 2.1 %input_terms.1 = bf16[2,128,768]{2,1,0:T(8,128)(2,1)S(1)} custom-call(bf16[1152,512]{1,0:T(8,128)(2,1)S(1)} %bitcast.79, f32[2,8,8,256]{3,2,1,0:T(8,128)S(1)} %pad_maximum_fusion.8.ends, bf16[2,128,768]{2,1,0:T(8,128)(2,1)S(1)} %bitcast.76, bf16[2,128,768]{2,1,0:T(8,128)(2,1)S(1)} %copy-done.4, bf16[2,128,768]{2,1,0:T(8,128)(2,1)S(1)} %copy-done.6, ...), custom_call_target="tpu_custom_call" | custom-call | flops 1207959552 | bytes 3276800 | tf_op jit(solution)/shard_map/input_terms/pallas_call | solution.py:41
  83.4 1.7 %maximum_bitcast_fusion = f32[128,3,3,512]{3,0,2,1:T(8,128)} fusion(f32[3,3,128,256]{3,2,1,0:T(8,128)S(1)} %bitcast.80, f32[3,3,128,256]{3,2,1,0:T(8,128)S(1)} %bitcast.81), kind=kLoop, calls=%fused_computation | loop fusion | flops 589824 | bytes 4718592 | tf_op jit(solution)/shard_map/transpose | solution.py:385
  85.2 2.4 %collective-permute-done.12 = f32[1,2,128,768]{3,2,1,0:T(8,128)S(1)} collective-permute-done((f32[1,2,128,768]{3,2,1,0:T(8,128)}, f32[1,2,128,768]{3,2,1,0:T(8,128)S(1)}, u32[]{:S(2)}, u32[]{:S(2)}) %collective-permute-start.12) | collective-permute-done | bytes 786464 | tf_op jit(solution)/shard_map/ppermute | solution.py:24
  (116 shorter events, 24.5 us)
Async XLA Ops:
  1.7 5.3 %collective-permute-start = (bf16[2,128,768]{2,1,0:T(8,128)(2,1)S(1)}, bf16[2,128,768]{2,1,0:T(8,128)(2,1)S(1)}, u32[]{:S(2)}, u32[]{:S(2)}) collective-permute-start(bf16[2,128,768]{2,1,0:T(8,128)(2,1)S(1)} %bitcast.73), channel_id=1, source_target_pairs={{0,1},{1,0},{2,3},{3,2},{4,5},{5,4},{6,7},{7,6},{8,9},{9,8},{10,11... | collective-permute-start | bytes 1179656 | tf_op jit(solution)/shard_map/ppermute | solution.py:24
  2.2 12.3 %collective-permute-start.2 = (bf16[2,128,768]{2,1,0:T(8,128)(2,1)S(1)}, bf16[2,128,768]{2,1,0:T(8,128)(2,1)S(1)}, u32[]{:S(2)}, u32[]{:S(2)}) collective-permute-start(bf16[2,128,768]{2,1,0:T(8,128)(2,1)S(1)} %bitcast.74), channel_id=1, source_target_pairs={{0,2},{1,3},{2,0},{3,1},{4,6},{5,7},{6,4},{7,5},{8,10},{9,11},{10,... | collective-permute-start | bytes 1179656 | tf_op jit(solution)/shard_map/ppermute | solution.py:24
  8.3 9.4 %collective-permute-start.1 = (f16[592,256]{1,0:T(8,128)(2,1)S(1)}, f16[592,256]{1,0:T(8,128)(2,1)}, u32[]{:S(2)}, u32[]{:S(2)}) collective-permute-start(f16[592,256]{1,0:T(8,128)(2,1)S(1)} %convert_element_type.112), channel_id=1, source_target_pairs={{0,4},{4,0},{8,12},{12,8},{16,20},{20,16},{24,28},{28,24},{1,5},{5... | collective-permute-start | bytes 909320 | tf_op jit(solution)/shard_map/ppermute | solution.py:24
  14.5 9.2 %copy-start.5 = (bf16[2,128,768]{2,1,0:T(8,128)(2,1)}, bf16[2,128,768]{2,1,0:T(8,128)(2,1)S(1)}, u32[]{:S(2)}) copy-start(bf16[2,128,768]{2,1,0:T(8,128)(2,1)S(1)} %collective-permute-done.2.ga.refs_2_) | copy-start | bytes 1179652
  14.5 8.0 %collective-permute-start.4 = (bf16[2,128,768]{2,1,0:T(8,128)(2,1)S(1)}, bf16[2,128,768]{2,1,0:T(8,128)(2,1)S(1)}, u32[]{:S(2)}, u32[]{:S(2)}) collective-permute-start(bf16[2,128,768]{2,1,0:T(8,128)(2,1)S(1)} %collective-permute-done.2.ga.refs_2_), channel_id=1, source_target_pairs={{0,1},{1,0},{2,3},{3,2},{4,5},{5,4},{6,7},{7,6},{8,9},{9,8},{10,11... | collective-permute-start | bytes 1179656 | tf_op jit(solution)/shard_map/ppermute | solution.py:24
  20.9 5.7 %collective-permute-start.3 = (f16[312,256]{1,0:T(8,128)(2,1)}, f16[312,256]{1,0:T(8,128)(2,1)}, u32[]{:S(2)}, u32[]{:S(2)}) collective-permute-start(f16[312,256]{1,0:T(8,128)(2,1)} %pad_maximum_fusion.4), channel_id=1, source_target_pairs={{0,8},{4,12},{8,0},{12,4},{16,24},{20,28},{24,16},{28,20},{1,9},{5... | collective-permute-start | bytes 479240 | tf_op jit(solution)/shard_map/ppermute | solution.py:24
  22.5 4.1 %copy-start.14 = (f32[1,256]{1,0:T(1,128)S(1)}, f32[1,256]{1,0:T(1,128)}, u32[]{:S(2)}) copy-start(f32[1,256]{1,0:T(1,128)} %copy-done.13) | copy-start | bytes 3076
  27.3 10.7 %copy-start.1 = (bf16[128,2,768]{2,1,0:T(2,128)(2,1)S(1)}, bf16[128,2,768]{2,1,0:T(2,128)(2,1)}, u32[]{:S(2)}) copy-start(bf16[128,2,768]{2,1,0:T(2,128)(2,1)} %x.3) | copy-start | bytes 1179652
  29.1 5.5 %collective-permute-start.5 = (f16[184,256]{1,0:T(8,128)(2,1)S(1)}, f16[184,256]{1,0:T(8,128)(2,1)S(1)}, u32[]{:S(2)}, u32[]{:S(2)}) collective-permute-start(f16[184,256]{1,0:T(8,128)(2,1)S(1)} %pad_maximum_fusion.9), channel_id=1, source_target_pairs={{0,16},{4,20},{8,24},{12,28},{16,0},{20,4},{24,8},{28,12},{1,17},{... | collective-permute-start | bytes 282632 | tf_op jit(solution)/shard_map/ppermute | solution.py:24
  31.8 9.5 %collective-permute-start.7 = (f16[592,256]{1,0:T(8,128)(2,1)S(1)}, f16[592,256]{1,0:T(8,128)(2,1)S(1)}, u32[]{:S(2)}, u32[]{:S(2)}) collective-permute-start(f16[592,256]{1,0:T(8,128)(2,1)S(1)} %convert_element_type.118), channel_id=1, source_target_pairs={{0,4},{4,0},{8,12},{12,8},{16,20},{20,16},{24,28},{28,24},{1,5},{5... | collective-permute-start | bytes 909320 | tf_op jit(solution)/shard_map/ppermute | solution.py:24
  34.7 4.5 %copy-start.2 = (bf16[128,3,3,512]{3,0,2,1:T(8,128)(2,1)S(1)}, bf16[128,3,3,512]{3,0,2,1:T(8,128)(2,1)}, u32[]{:S(2)}) copy-start(bf16[128,3,3,512]{3,0,2,1:T(8,128)(2,1)} %param.4) | copy-start | bytes 3538948
  35.3 8.7 %collective-permute-start.9 = (f16[1,152,256]{2,1,0:T(8,128)(2,1)S(1)}, f16[1,152,256]{2,1,0:T(8,128)(2,1)S(1)}, u32[]{:S(2)}, u32[]{:S(2)}) collective-permute-start(f16[1,152,256]{2,1,0:T(8,128)(2,1)S(1)} %convert_bitcast_fusion.1), channel_id=1, source_target_pairs={{0,16},{4,20},{8,24},{12,28},{16,0},{20,4},{24,8},{28,12},{1,17},{... | collective-permute-start | bytes 233480 | tf_op jit(solution)/shard_map/ppermute | solution.py:24
  41.2 17.8 %collective-permute-start.6 = (f32[2,2,128,768]{3,2,1,0:T(8,128)S(1)}, f32[2,2,128,768]{3,2,1,0:T(8,128)S(1)}, u32[]{:S(2)}, u32[]{:S(2)}) collective-permute-start(f32[2,2,128,768]{3,2,1,0:T(8,128)S(1)} %get-tuple-element.58), channel_id=1, source_target_pairs={{0,1},{1,0},{2,3},{3,2},{4,5},{5,4},{6,7},{7,6},{8,9},{9,8},{10,11... | collective-permute-start | bytes 4718600 | tf_op jit(solution)/shard_map/ppermute | solution.py:24
  41.6 7.4 %collective-permute-start.8 = (f16[312,256]{1,0:T(8,128)(2,1)S(1)}, f16[312,256]{1,0:T(8,128)(2,1)S(1)}, u32[]{:S(2)}, u32[]{:S(2)}) collective-permute-start(f16[312,256]{1,0:T(8,128)(2,1)S(1)} %pad_maximum_fusion.5), channel_id=1, source_target_pairs={{0,8},{4,12},{8,0},{12,4},{16,24},{20,28},{24,16},{28,20},{1,9},{5... | collective-permute-start | bytes 479240 | tf_op jit(solution)/shard_map/ppermute | solution.py:24
  44.1 8.0 %collective-permute-start.11 = (f16[2,152,256]{2,1,0:T(8,128)(2,1)S(1)}, f16[2,152,256]{2,1,0:T(8,128)(2,1)S(1)}, u32[]{:S(2)}, u32[]{:S(2)}) collective-permute-start(f16[2,152,256]{2,1,0:T(8,128)(2,1)S(1)} %pad_maximum_fusion.6), channel_id=1, source_target_pairs={{0,8},{4,12},{8,0},{12,4},{16,24},{20,28},{24,16},{28,20},{1,9},{5... | collective-permute-start | bytes 466952 | tf_op jit(solution)/shard_map/ppermute | solution.py:24
  49.2 7.3 %collective-permute-start.10 = (f16[184,256]{1,0:T(8,128)(2,1)S(1)}, f16[184,256]{1,0:T(8,128)(2,1)S(1)}, u32[]{:S(2)}, u32[]{:S(2)}) collective-permute-start(f16[184,256]{1,0:T(8,128)(2,1)S(1)} %pad_maximum_fusion.10), channel_id=1, source_target_pairs={{0,16},{4,20},{8,24},{12,28},{16,0},{20,4},{24,8},{28,12},{1,17},{... | collective-permute-start | bytes 282632 | tf_op jit(solution)/shard_map/ppermute | solution.py:24
  52.2 8.1 %copy-start.11 = (f16[2,152,256]{2,1,0:T(8,128)(2,1)}, f16[2,152,256]{2,1,0:T(8,128)(2,1)S(1)}, u32[]{:S(2)}) copy-start(f16[2,152,256]{2,1,0:T(8,128)(2,1)S(1)} %get-tuple-element.108) | copy-start | bytes 466948
  57.0 6.0 %collective-permute-start.13 = (f16[1,152,256]{2,1,0:T(8,128)(2,1)S(1)}, f16[1,152,256]{2,1,0:T(8,128)(2,1)S(1)}, u32[]{:S(2)}, u32[]{:S(2)}) collective-permute-start(f16[1,152,256]{2,1,0:T(8,128)(2,1)S(1)} %convert_bitcast_fusion), channel_id=1, source_target_pairs={{0,16},{4,20},{8,24},{12,28},{16,0},{20,4},{24,8},{28,12},{1,17},{... | collective-permute-start | bytes 233480 | tf_op jit(solution)/shard_map/ppermute | solution.py:24
  57.5 8.6 %collective-permute-start.15 = (f16[4,152,256]{2,1,0:T(8,128)(2,1)S(1)}, f16[4,152,256]{2,1,0:T(8,128)(2,1)S(1)}, u32[]{:S(2)}, u32[]{:S(2)}) collective-permute-start(f16[4,152,256]{2,1,0:T(8,128)(2,1)S(1)} %pad_maximum_fusion.2), channel_id=1, source_target_pairs={{0,4},{4,0},{8,12},{12,8},{16,20},{20,16},{24,28},{28,24},{1,5},{5... | collective-permute-start | bytes 933896 | tf_op jit(solution)/shard_map/ppermute | solution.py:24
  59.3 9.9 %copy-start.9 = (f32[2,2,128,768]{3,2,1,0:T(8,128)}, f32[2,2,128,768]{3,2,1,0:T(8,128)S(1)}, u32[]{:S(2)}) copy-start(f32[2,2,128,768]{3,2,1,0:T(8,128)S(1)} %add.54) | copy-start | bytes 4718596
  63.1 5.3 %collective-permute-start.14 = (f16[2,152,256]{2,1,0:T(8,128)(2,1)S(1)}, f16[2,152,256]{2,1,0:T(8,128)(2,1)S(1)}, u32[]{:S(2)}, u32[]{:S(2)}) collective-permute-start(f16[2,152,256]{2,1,0:T(8,128)(2,1)S(1)} %pad_maximum_fusion.7), channel_id=1, source_target_pairs={{0,8},{4,12},{8,0},{12,4},{16,24},{20,28},{24,16},{28,20},{1,9},{5... | collective-permute-start | bytes 466952 | tf_op jit(solution)/shard_map/ppermute | solution.py:24
  70.3 7.0 %collective-permute-start.16 = (f16[4,152,256]{2,1,0:T(8,128)(2,1)S(1)}, f16[4,152,256]{2,1,0:T(8,128)(2,1)S(1)}, u32[]{:S(2)}, u32[]{:S(2)}) collective-permute-start(f16[4,152,256]{2,1,0:T(8,128)(2,1)S(1)} %pad_maximum_fusion.3), channel_id=1, source_target_pairs={{0,4},{4,0},{8,12},{12,8},{16,20},{20,16},{24,28},{28,24},{1,5},{5... | collective-permute-start | bytes 933896 | tf_op jit(solution)/shard_map/ppermute | solution.py:24
  71.9 15.7 %collective-permute-start.12 = (f32[1,2,128,768]{3,2,1,0:T(8,128)}, f32[1,2,128,768]{3,2,1,0:T(8,128)S(1)}, u32[]{:S(2)}, u32[]{:S(2)}) collective-permute-start(f32[1,2,128,768]{3,2,1,0:T(8,128)} %slice.163), channel_id=1, source_target_pairs={{0,2},{1,3},{2,0},{3,1},{4,6},{5,7},{6,4},{7,5},{8,10},{9,11},{10,... | collective-permute-start | bytes 2359304 | tf_op jit(solution)/shard_map/ppermute | solution.py:24
  83.4 4.1 %copy-start.10 = (f32[2,2,128,768]{3,2,1,0:T(8,128)S(1)}, f32[2,2,128,768]{3,2,1,0:T(8,128)}, u32[]{:S(2)}) copy-start(f32[2,2,128,768]{3,2,1,0:T(8,128)} %copy-done.9) | copy-start | bytes 4718596
  (8 other events, 11.8 us)

commit v3 on v2

--- a/solution.py
+++ b/solution.py
@@ -33,6 +33,10 @@
     for b in range(count):
         out = out + (((index >> b) & 1) << (count - 1 - b))
     return out
+
+
+def piece_of(tile, tiles):
+    return (tile & 1) * (tiles // 2) + (tile >> 1)
 
 
 def call(body, name, outs, scratch, flops, *args):
@@ -56,29 +60,32 @@
     return jnp.ceil(jnp.log2(jnp.maximum(most, LEAST)))
 
 
+def pick_columns(cols):
+    row_of = lax.broadcasted_iota(jnp.int32, (16, cols), 0)
+    lane = lax.broadcasted_iota(jnp.int32, (16, cols), 1)
+    pick = ((row_of == 0) & (lane == 0)) | ((row_of == 1) & (lane == cols - 1))
+    return jnp.where(pick, 1.0, 0.0).astype(BF16)
+
+
 def taps_kernel(x, *refs):
-    *ends, out = refs
+    *sides, out, columns = refs
     chans, rows, cols = x.shape
-    if ends:
-        tiles = ends[0].shape[0]
-        tile = lax.axis_index("width")
-        left = ends[0][jnp.maximum(tile - 1, 0)]
-        right = ends[0][jnp.minimum(tile + 1, tiles - 1)]
-        left = jnp.where(tile > 0, left[3:4] * jnp.exp2(left[0:1] - TOP), 0.0)
-        right = jnp.where(tile < tiles - 1, right[2:3] * jnp.exp2(right[0:1] - TOP), 0.0)
-        row_of = lax.broadcasted_iota(jnp.int32, (16, LANES), 0)
-        lane = lax.broadcasted_iota(jnp.int32, (16, LANES), 1)
-        place = ((row_of == 0) & (lane == LANES - 1)) | ((row_of == 1) & (lane == 0))
-        place = jnp.where(place, 1.0, 0.0).astype(BF16)
+    row_of = lax.broadcasted_iota(jnp.int32, (16, LANES), 0)
+    lane = lax.broadcasted_iota(jnp.int32, (16, LANES), 1)
+    place = ((row_of == 0) & (lane == LANES - 1)) | ((row_of == 1) & (lane == 0))
+    place = jnp.where(place, 1.0, 0.0).astype(BF16)
     for i in range(rows):
         side = jnp.zeros((chans, LANES), BF16)
-        if ends:
-            at = slice(i * chans, (i + 1) * chans)
-            both = jnp.concatenate([left[:, at], right[:, at], jnp.zeros((14, chans), F32)], axis=0).astype(BF16)
+        if sides:
+            both = [side_ref[...].astype(F32)[:, i * chans : (i + 1) * chans] for side_ref in sides]
+            both = jnp.concatenate(both + [jnp.zeros((14, chans), F32)], axis=0).astype(BF16)
             side = lax.dot_general(both, place, TN, preferred_element_type=F32).astype(BF16)
         row = jnp.concatenate([side, x[:, i, :], side], axis=1)
         for b in range(3):
             out[i, b * chans : (b + 1) * chans, :] = row[:, LANES - 1 + b : LANES - 1 + b + cols]
+        for at, tile in ((0, x[:, i, :LANES]), (1, x[:, i, cols - LANES :])):
+            line = lax.dot_general(pick_columns(LANES), tile, NT, preferred_element_type=F32).astype(BF16)
+            columns[at : at + 1, i * chans : (i + 1) * chans] = line[at : at + 1]
 
 
 def filter_kernel(factor, piece, first, xs, ga, gb, send, keep, gsc, acc):
@@ -101,7 +108,7 @@
     if acc.shape[0] > 3 * deep:
         acc[3 * deep :, :] = jnp.zeros((acc.shape[0] - 3 * deep, lanes), F32)
     power = exponent(acc[...])
-    mine = reversed_bits(lax.axis_index("width"), bits_of(width))
+    mine = piece_of(lax.axis_index("width"), width)
     half = width // 2
     for r in range(width):
         rows_of = acc[pl.ds(pl.multiple_of((mine ^ r) * piece, 16), piece), :]
@@ -112,10 +119,7 @@
     power = jnp.broadcast_to(power, (POWER, lanes))
     send[half * piece : half * piece + POWER, :] = power
     keep[half * piece :, :] = power
-    row_of = lax.broadcasted_iota(jnp.int32, (16, cols), 0)
-    lane = lax.broadcasted_iota(jnp.int32, (16, cols), 1)
-    pick = ((row_of == 0) & (lane == 0)) | ((row_of == 1) & (lane == cols - 1))
-    pick = jnp.where(pick, 1.0, 0.0).astype(BF16)
+    pick = pick_columns(cols)
     gends = [lax.dot_general(pick, gsc[h], NT, preferred_element_type=F32) for h in range(rows)]
     gends = jnp.concatenate([gends[h][s : s + 1] for s in range(2) for h in range(rows)], axis=0)
     if first:
@@ -156,7 +160,7 @@
             taken = [source[:, i * chans : (i + 1) * chans] if 0 <= i < rows else nothing for i in taken]
             terms = lax.dot_general(jnp.concatenate(taken, axis=0).astype(BF16), grads, TN, preferred_element_type=F32)
             acc[(3 * a + b) * chans : (3 * a + b + 1) * chans, :] = terms * factor
-    mine = reversed_bits(lax.axis_index("width"), bits_of(tiles))
+    mine = piece_of(lax.axis_index("width"), tiles)
     value = total[...] + acc[pl.ds(pl.multiple_of(mine * piece, 16), piece), :]
     power = exponent(value)
     out[:piece, :] = value * jnp.exp2(TOP - power)
@@ -229,41 +233,70 @@
     def __call__(self, value):
         if self.last is not None:
             value, _ = lax.optimization_barrier((value, self.last))
-        self.last = value
+        self.last = jax.tree.leaves(value)[0]
         return value
 
 
-def doubled(got, own, bit):
-    late = (lax.axis_index("width") & bit) != 0
-    return jnp.concatenate([jnp.where(late, got, own), jnp.where(late, own, got)], axis=0)
-
-
-def chunk_stages(send, keep, finish, order):
-    steps = bits_of(lax.axis_size("width"))
+def doubled(got, own, late):
+    return [jnp.where(late, got, own), jnp.where(late, own, got)]
+
+
+def in_order(values, late):
+    for b, swap in enumerate(late):
+        values = [jnp.where(swap, values[n ^ 1 << b], values[n]) for n in range(len(values))]
+    return values
+
+
+def scaled(values, power):
+    return (values * jnp.exp2(TOP - power)).astype(F16)
+
+
+def added(total, got):
+    count = total.shape[0]
+    return total + got[:count].astype(F32) * jnp.exp2(got[count : count + 1].astype(F32) - TOP)
+
+
+def chunk_stages(send, keep, finish, order, late, arrived):
+    others = 1 << len(late) - 1
     lanes = send.shape[1]
     total, power = keep[:-POWER], keep[-1:]
+    piece = total.shape[0] // others
+
     message = send.astype(F16)
-    ends = message[-EDGE:][None]
-    for b in range(steps):
-        got = exchange(order(message), "width", 1 << b)
-        yield None
-        got = order(got)
-        count = total.shape[0]
-        other = got[count : count + 1].astype(F32)
-        total = total + got[:count].astype(F32) * jnp.exp2(other - TOP)
-        power = jnp.maximum(power, other) + 1.0
-        ends = doubled(got[count + POWER :].reshape(-1, EDGE, lanes), ends, 1 << b)
-        if b < steps - 1:
-            scaled = total[count // 2 :] * jnp.exp2(TOP - power)
-            tail = jnp.broadcast_to(power, (POWER, lanes))
-            message = jnp.concatenate([scaled.astype(F16), tail.astype(F16), ends.reshape(-1, lanes)], axis=0)
-            total = total[: count // 2]
-    every = finish(total, ends.astype(F32)).astype(F16)[None]
-    for b in reversed(range(steps)):
-        got = exchange(order(every), "width", 1 << b)
-        yield None
-        every = doubled(order(got), every, 1 << b)
-    yield every
+    got = exchange(order(message), "width", 1)
+    yield None
+    got = order(got)
+    yield None
+    arrived.append(got[-EDGE:])
+    total = added(total, got)
+    power = jnp.maximum(power, got[-POWER - EDGE : -POWER - EDGE + 1].astype(F32)) + 1.0
+    ends = jnp.concatenate(doubled(got[-EDGE:], message[-EDGE:], late[0]), axis=0)
+    tail = jnp.broadcast_to(power, (POWER, lanes)).astype(F16)
+    messages = []
+    for n in range(1, others):
+        part = scaled(total[n * piece : (n + 1) * piece], power)
+        messages.append(jnp.concatenate([part, tail, ends], axis=0))
+    messages = order(messages)
+    gots = [exchange(messages[n - 1], "width", 2 * n) for n in range(1, others)]
+    yield None
+    gots = order(gots)
+    yield None
+    total = total[:piece]
+    for got in gots:
+        total = added(total, got)
+    every = in_order([ends] + [got[piece + POWER :] for got in gots], late[1:])
+    every = jnp.concatenate([v.reshape(2, EDGE, lanes) for v in every], axis=0).astype(F32)
+    own = order(finish(total, every).astype(F16))
+    gots = [exchange(own, "width", 2 * n) for n in range(1, others)]
+    yield None
+    gots = order(gots)
+    yield None
+    own = order(jnp.stack(in_order([own] + gots, late[1:])))
+    got = exchange(own, "width", 1)
+    yield None
+    got = order(got)
+    yield None
+    yield jnp.concatenate(doubled(got, own, late[0]), axis=0)
 
 
 def unpacked(every):
@@ -272,14 +305,13 @@
     return (every[:, :rows].astype(F32) * scale).reshape(-1, every.shape[2])
 
 
-def chunk_times(chunks, steps):
-    times = []
-    for j in range(chunks):
-        now = 2.6 * j
-        for step in range(2 * steps + 1):
-            times.append((now, j))
-            now += 2.0 if step in (0, 2 * steps - 1) else 1.0
-    return sorted(times)
+def chunk_times(j):
+    now = 2.05 * j
+    times = [now - 0.1 if j else now]
+    for step in range(4):
+        now += 2.0
+        times += [now - (0.2 if j and step == 0 else 0.1), now]
+    return times
 
 
 def body(activations, filters, cotangent):
@@ -287,8 +319,10 @@
     block = cotangent.shape[0]
     outs = filters.shape[3]
     groups, width = lax.axis_size("chan"), lax.axis_size("width")
-    me = lax.axis_index("chan")
     lanes = 2 * block
+    late = [((lax.axis_index("width") >> b) & 1) == 1 for b in range(bits_of(width))]
+    swaps = [((lax.axis_index("chan") >> b) & 1) == 1 for b in range(1, bits_of(groups))]
+    cotangent, late, swaps = lax.optimization_barrier((cotangent, late, swaps))
     mats = jnp.transpose(filters, (1, 2, 0, 3))
     pairs_of_rows = sum(0 <= h + a - 1 < rows for h in range(rows) for a in range(3))
     flops = 2 * pairs_of_rows * 3 * chans * cols * outs
@@ -296,10 +330,11 @@
     piece = -(-piece // 16) * 16
     factor = 1.0 / math.sqrt(rows * cols * width)
     order = Order()
-    ends = {}
+    ends, arrived = {}, []
 
     def shifted(*sides):
-        return call(taps_kernel, "shifted_taps", [((rows, 3 * chans, cols), BF16)], [], 0, activations, *sides)
+        shapes = [((rows, 3 * chans, cols), BF16), ((2, rows * chans), BF16)]
+        return call(taps_kernel, "shifted_taps", shapes, [], 0, activations, *sides)
 
     def filter_chunk(j):
         send, keep = call(
@@ -319,24 +354,39 @@
             shape = ((piece + POWER, lanes), F32)
             return call(body, "border_terms", [shape], [((width * piece, lanes), F32)], 0, total, ends[0], ends[j])
 
-        return chunk_stages(send, keep, finish, order)
+        return chunk_stages(send, keep, finish, order, late, arrived)
 
     def forward():
+        odd = late[0]
+        pairs = [(i, i + 1) for i in range(1, width - 1, 2)]
+        mine = jnp.where(odd, columns[1:2], columns[0:1])
+        far = lax.ppermute(order(mine), "width", pairs + [(j, i) for i, j in pairs])
+        yield None
+        near = arrived[0].astype(F32)
+        near = (jnp.where(odd, near[3:4], near[2:3]) * jnp.exp2(near[0:1] - TOP)).astype(BF16)
+        far = order(far)
+        left, right = jnp.where(odd, near, far), jnp.where(odd, far, near)
         send, keep = call(
             forward_kernel,
             "forward_terms",
             [((groups // 2, rows, block, cols), F32)] * 2,
             [((outs, cols), F32)],
             flops,
-            shifted(order(ends[0])),
+            shifted(left, right)[0],
             mats.reshape(3, 3 * chans, outs),
         )
-        for b in range(bits_of(groups)):
+        for b in range(bits_of(groups) - 1):
             got = exchange(order(send), "chan", 1 << b)
             yield None
             total = keep + order(got)
             keep, send = total[: total.shape[0] // 2], total[total.shape[0] // 2 :]
-        yield jnp.transpose(total[0].astype(BF16), (1, 0, 2))
+        gots = [exchange(order(send[0, h]), "chan", 1 << bits_of(groups) - 1) for h in range(rows)]
+        yield None
+        sums = []
+        for h in range(rows):
+            sums.append((keep[0, h] + order(gots[h])).astype(BF16))
+            yield None
+        result["conv"] = jnp.transpose(jnp.stack(sums), (1, 0, 2))
 
     def backward():
         out = call(
@@ -349,38 +399,48 @@
             jnp.stack([order(ends[j]) for j in range(groups // 2)]),
             *[g[r] for r in range(groups)],
         )
-        return jnp.transpose(out, (1, 0, 2))
+        yield None
+        result["grad"] = order(jnp.transpose(out, (1, 0, 2)))
+
+    def chunk(j):
+        if j:
+            g[2 * j + 1] = order(g[2 * j + 1])
+        stages = filter_chunk(j)
+        if j == 0:
+            next(stages)
+            for r in sorted(g):
+                if r > 1:
+                    g[r | 1] = exchange(order(g[r]), "chan", 1)
+            yield None
+        for piece in stages:
+            pieces[j] = piece
+            yield None
 
     g = {0: order(jnp.transpose(cotangent, (1, 0, 2)))}
     g[1] = exchange(g[0], "chan", 1)
     for b in reversed(range(1, bits_of(groups))):
         for r in [r for r in sorted(g) if r != 1]:
             g[r | 1 << b] = exchange(g[r], "chan", 1 << b)
-    bare = shifted()
-    chunks = [filter_chunk(0)]
-    next(chunks[0])
-    for r in sorted(g):
-        if r > 1:
-            g[r | 1] = exchange(order(g[r]), "chan", 1)
-    pieces = [None] * (groups // 2)
+    bare, columns = shifted()
+    pieces, result = {}, {}
+    hops = bits_of(groups)
+    turns = []
+    for j in range(groups // 2):
+        stages = chunk(j)
+        turns += [(now, stages) for now in chunk_times(j)]
+    finale = turns[-1][0]
     conv = forward()
-    waits = bits_of(groups) + 1
-    for now, j in chunk_times(groups // 2, bits_of(width))[1:]:
-        if j == len(chunks):
-            g[2 * j + 1] = order(g[2 * j + 1])
-            chunks.append(filter_chunk(j))
-        pieces[j] = next(chunks[j])
-        if 0 in ends and waits > 1 and (waits > bits_of(groups) or now > 6.2):
-            conv_output = next(conv)
-            waits -= 1
-    input_grad = backward()
-    while waits:
-        conv_output = next(conv)
-        waits -= 1
+    turns += [(0.1, conv), (2.7, conv)] + [(4.2 + 2 * b, conv) for b in range(hops - 1)]
+    turns += [(1.98 + 2 * hops, conv), (3.5 + 2 * hops, conv), (3.6 + 2 * hops, conv)]
+    grad = backward()
+    turns += [(max(finale - 2.9, chunk_times(groups // 2 - 1)[4] + 0.2), grad), (finale - 0.4, grad)]
+    for now, stages in sorted(turns, key=lambda turn: turn[0]):
+        next(stages, None)
+    conv_output, input_grad = result["conv"], result["grad"]
+    pieces = [pieces[j] for j in range(groups // 2)]
 
     for b in range(bits_of(groups // 2)):
-        swap = ((me >> (b + 1)) & 1) == 1
-        pieces = [jnp.where(swap, pieces[j ^ 1 << b], pieces[j]) for j in range(len(pieces))]
+        pieces = [jnp.where(swaps[b], pieces[j ^ 1 << b], pieces[j]) for j in range(len(pieces))]
     grads = jnp.concatenate([unpacked(p) for p in pieces], axis=1)[: 9 * chans]
     grads = jnp.transpose(grads.reshape(3, 3, chans, outs), (2, 0, 1, 3))
     return conv_output, input_grad, grads

time: 89.3 us -> 74.1 us (0.83)
  waiting for transfers between devices: 39.2 us -> 21.7 us
  starting transfers between devices: 19.9 us -> 31.3 us
  other arithmetic: 12.7 us -> 4.47 us
  local copies, waits for them, and re-layouts: 6.16 us -> 4.42 us
  Pallas kernels: 9.76 us -> 10.9 us
    ppermute x17 -> x22, waiting for transfers between devices: 39.2 us -> 21.7 us  [exchange(): return lax.ppermute(value, axis, [(i, i ^ bit) for i in range(devices)])]
    ppermute x17 -> x22, starting transfers between devices: 19.9 us -> 30.4 us  [exchange(): return lax.ppermute(value, axis, [(i, i ^ bit) for i in range(devices)])]
    select_n x12 -> x7, other arithmetic: 4.29 us -> 0.72 us  [the longest x1 0.37 us: body(): jnp.where(swaps[b], pieces[j ^ 1 << b], pieces[j])]
    concatenate x8 -> x2, other arithmetic: 2.06 us -> 0.18 us  [chunk_stages(): messages.append(jnp.concatenate([part, tail, ends], axis=0))]
    add x6 -> x4, other arithmetic: 2.19 us -> 0.32 us  [added(): total + got[:count].astype(F32) * jnp.exp2(got[count:count + 1].astype(F3...]
    unnamed x35 -> x10, local copies, waits for them, and re-layouts: 5.14 us -> 3.32 us
    exp2 x6 -> x8, other arithmetic: 1.41 us -> 0.08 us  [the longest x6 0.05 us: added(): jnp.exp2(got[count:count + 1].astype(F32) - TOP)]
    pallas_call x8, Pallas kernels: 9.76 us -> 10.9 us  [call(): pl.pallas_call(body, out_shape=outs, in_specs=[VMEM] * len(args), out_spe...]
  transfers between devices with their start and end apart: 17 -> 23, of which waited for: 12 -> 9; matrix products, arithmetic and copies ran while one was open for 12% -> 5% of each run, Pallas kernels for 11% -> 15%
where the time goes in v3:
time: 74.1 us; the launch traced here: 73.9 us
  starting transfers between devices  31.3 us (42%)
  waiting for transfers between devices  21.7 us (29%)
  Pallas kernels  10.9 us (15%)
  other arithmetic  4.47 us (6%)
  local copies, waits for them, and re-layouts  4.42 us (6%)
  between operations  1.05 us (1%)
    ppermute x22, starting transfers between devices, exchange(): return lax.ppermute(value, axis, [(i, i ^ bit) for i in range(devices)])  30.4 us
    ppermute x22, waiting for transfers between devices, exchange(): return lax.ppermute(value, axis, [(i, i ^ bit) for i in range(devices)])  21.7 us
    pallas_call x8, Pallas kernels, call(): pl.pallas_call(body, out_shape=outs, in_specs=[VMEM] * len(args), out_spe...  10.9 us
    unnamed x10, local copies, waits for them, and re-layouts  3.32 us
    transpose x1, other arithmetic, body(): grads = jnp.transpose(grads.reshape(3, 3, chans, outs), (2, 0, 1, 3))  1.73 us
  transfers between devices with their start and end apart: 23, of which 9 were waited for; matrix products, arithmetic and copies ran while one was open for 5% of the time, Pallas kernels for 15%

profile of v3, /device:TPU:0, one launch (start us, length us, event | category | flops | bytes accessed | tf_op | source)
XLA Modules:
  0.0 73.9 jit_solution(14072380452834773703)
XLA Ops:
  2.2 2.6 %collective-permute-start.2 = (bf16[2,128,768]{2,1,0:T(8,128)(2,1)S(1)}, bf16[2,128,768]{2,1,0:T(8,128)(2,1)S(1)}, u32[]{:S(2)}, u32[]{:S(2)}) collective-permute-start(bf16[2,128,768]{2,1,0:T(8,128)(2,1)S(1)} %bitcast.92), channel_id=1, source_target_pairs={{0,2},{1,3},{2,0},{3,1},{4,6},{5,7},{6,4},{7,5},{8,10},{9,11},{10,... | collective-permute-start | bytes 1179656 | tf_op jit(solution)/shard_map/ppermute | solution.py:24
  8.6 1.5 %collective-permute-start.1 = (f16[592,256]{1,0:T(8,128)(2,1)S(1)}, f16[592,256]{1,0:T(8,128)(2,1)S(1)}, u32[]{:S(2)}, u32[]{:S(2)}) collective-permute-start(f16[592,256]{1,0:T(8,128)(2,1)S(1)} %convert_element_type.124), channel_id=1, source_target_pairs={{0,4},{4,0},{8,12},{12,8},{16,20},{20,16},{24,28},{28,24},{1,5},{5... | collective-permute-start | bytes 909320 | tf_op jit(solution)/shard_map/ppermute | solution.py:24
  10.1 4.4 %collective-permute-done.2.ga.refs_2_ = bf16[2,128,768]{2,1,0:T(8,128)(2,1)S(1)} collective-permute-done((bf16[2,128,768]{2,1,0:T(8,128)(2,1)S(1)}, bf16[2,128,768]{2,1,0:T(8,128)(2,1)S(1)}, u32[]{:S(2)}, u32[]{:S(2)}) %collective-permute-start.2) | collective-permute-done | bytes 393248 | tf_op jit(solution)/shard_map/ppermute | solution.py:24
  15.3 2.5 %collective-permute-done.1 = f16[592,256]{1,0:T(8,128)(2,1)S(1)} collective-permute-done((f16[592,256]{1,0:T(8,128)(2,1)S(1)}, f16[592,256]{1,0:T(8,128)(2,1)S(1)}, u32[]{:S(2)}, u32[]{:S(2)}) %collective-permute-start.1) | collective-permute-done | bytes 303136 | tf_op jit(solution)/shard_map/ppermute | solution.py:24
  19.4 2.1 %collective-permute-start.6 = (f16[592,256]{1,0:T(8,128)(2,1)S(1)}, f16[592,256]{1,0:T(8,128)(2,1)S(1)}, u32[]{:S(2)}, u32[]{:S(2)}) collective-permute-start(f16[592,256]{1,0:T(8,128)(2,1)S(1)} %convert_element_type.134), channel_id=1, source_target_pairs={{0,4},{4,0},{8,12},{12,8},{16,20},{20,16},{24,28},{28,24},{1,5},{5... | collective-permute-start | bytes 909320 | tf_op jit(solution)/shard_map/ppermute | solution.py:24
  21.5 1.6 %collective-permute-start.7 = (f16[168,256]{1,0:T(8,128)(2,1)S(1)}, f16[168,256]{1,0:T(8,128)(2,1)S(1)}, u32[]{:S(2)}, u32[]{:S(2)}) collective-permute-start(f16[168,256]{1,0:T(8,128)(2,1)S(1)} %get-tuple-element.71), channel_id=1, source_target_pairs={{0,8},{4,12},{8,0},{12,4},{16,24},{20,28},{24,16},{28,20},{1,9},{5... | collective-permute-start | bytes 258056 | tf_op jit(solution)/shard_map/ppermute | solution.py:24
  23.0 2.1 %collective-permute-start.8 = (f16[168,256]{1,0:T(8,128)(2,1)S(1)}, f16[168,256]{1,0:T(8,128)(2,1)S(1)}, u32[]{:S(2)}, u32[]{:S(2)}) collective-permute-start(f16[168,256]{1,0:T(8,128)(2,1)S(1)} %get-tuple-element.79), channel_id=1, source_target_pairs={{0,16},{4,20},{8,24},{12,28},{16,0},{20,4},{24,8},{28,12},{1,17},{... | collective-permute-start | bytes 258056 | tf_op jit(solution)/shard_map/ppermute | solution.py:24
  25.9 2.1 %shifted_taps.3 = (bf16[2,384,768]{2,1,0:T(8,128)(2,1)S(1)}, bf16[2,256]{1,0:T(2,128)(2,1)}) custom-call(bf16[128,2,768]{2,1,0:T(2,128)(2,1)S(1)} %copy-done.1, bf16[1,256]{1,0:T(2,128)(2,1)S(1)} %broadcast_select_fusion.27.refs_0_, bf16[1,256]{1,0:T(2,128)(2,1)S(1)} %get-tuple-element.121.refs_1_), custom_call_target="tpu_custom_call" | custom-call | bytes 1574912 | tf_op jit(solution)/shard_map/shifted_taps/pallas_call | solution.py:45
  28.0 2.0 %forward_terms.1 = (f32[2,2,128,768]{3,2,1,0:T(8,128)S(1)}, f32[2,2,128,768]{3,2,1,0:T(8,128)S(1)}) custom-call(bf16[2,384,768]{2,1,0:T(8,128)(2,1)S(1)} %get-tuple-element.73.xs, bf16[3,384,512]{2,1,0:T(8,128)(2,1)S(1)} %bitcast.96), custom_call_target="tpu_custom_call" | custom-call | flops 1207959552 | bytes 5505024 | tf_op jit(solution)/shard_map/forward_terms/pallas_call | solution.py:45
  30.1 2.6 %collective-permute-done.8 = f16[168,256]{1,0:T(8,128)(2,1)S(1)} collective-permute-done((f16[168,256]{1,0:T(8,128)(2,1)S(1)}, f16[168,256]{1,0:T(8,128)(2,1)S(1)}, u32[]{:S(2)}, u32[]{:S(2)}) %collective-permute-start.8) | collective-permute-done | bytes 86048 | tf_op jit(solution)/shard_map/ppermute | solution.py:24
  33.4 1.5 %collective-permute-start.14 = (f16[152,256]{1,0:T(8,128)(2,1)S(1)}, f16[152,256]{1,0:T(8,128)(2,1)S(1)}, u32[]{:S(2)}, u32[]{:S(2)}) collective-permute-start(f16[152,256]{1,0:T(8,128)(2,1)S(1)} %convert_element_type.149), channel_id=1, source_target_pairs={{0,8},{4,12},{8,0},{12,4},{16,24},{20,28},{24,16},{28,20},{1,9},{5... | collective-permute-start | bytes 233480 | tf_op jit(solution)/shard_map/ppermute | solution.py:24
  36.1 1.8 %collective-permute-start.16 = (f16[152,256]{1,0:T(8,128)(2,1)S(1)}, f16[152,256]{1,0:T(8,128)(2,1)S(1)}, u32[]{:S(2)}, u32[]{:S(2)}) collective-permute-start(f16[152,256]{1,0:T(8,128)(2,1)S(1)} %convert_element_type.149), channel_id=1, source_target_pairs={{0,24},{4,28},{8,16},{12,20},{16,8},{20,12},{24,0},{28,4},{1,25},{... | collective-permute-start | bytes 233480 | tf_op jit(solution)/shard_map/ppermute | solution.py:24
  38.8 2.0 %collective-permute-start.12 = (f16[168,256]{1,0:T(8,128)(2,1)S(1)}, f16[168,256]{1,0:T(8,128)(2,1)S(1)}, u32[]{:S(2)}, u32[]{:S(2)}) collective-permute-start(f16[168,256]{1,0:T(8,128)(2,1)S(1)} %get-tuple-element.90), channel_id=1, source_target_pairs={{0,16},{4,20},{8,24},{12,28},{16,0},{20,4},{24,8},{28,12},{1,17},{... | collective-permute-start | bytes 258056 | tf_op jit(solution)/shard_map/ppermute | solution.py:24
  41.1 1.8 %collective-permute-start.13 = (f16[168,256]{1,0:T(8,128)(2,1)S(1)}, f16[168,256]{1,0:T(8,128)(2,1)S(1)}, u32[]{:S(2)}, u32[]{:S(2)}) collective-permute-start(f16[168,256]{1,0:T(8,128)(2,1)S(1)} %get-tuple-element.91), channel_id=1, source_target_pairs={{0,24},{4,28},{8,16},{12,20},{16,8},{20,12},{24,0},{28,4},{1,25},{... | collective-permute-start | bytes 258056 | tf_op jit(solution)/shard_map/ppermute | solution.py:24
  44.1 1.5 %collective-permute-start.10 = (f32[128,768]{1,0:T(8,128)S(1)}, f32[128,768]{1,0:T(8,128)S(1)}, u32[]{:S(2)}, u32[]{:S(2)}) collective-permute-start(f32[128,768]{1,0:T(8,128)S(1)} %get-tuple-element.89), channel_id=1, source_target_pairs={{0,2},{1,3},{2,0},{3,1},{4,6},{5,7},{6,4},{7,5},{8,10},{9,11},{10,... | collective-permute-start | bytes 1179656 | tf_op jit(solution)/shard_map/ppermute | solution.py:24
  45.7 4.6 %collective-permute-done.12 = f16[168,256]{1,0:T(8,128)(2,1)S(1)} collective-permute-done((f16[168,256]{1,0:T(8,128)(2,1)S(1)}, f16[168,256]{1,0:T(8,128)(2,1)S(1)}, u32[]{:S(2)}, u32[]{:S(2)}) %collective-permute-start.12) | collective-permute-done | bytes 86048 | tf_op jit(solution)/shard_map/ppermute | solution.py:24
  50.4 1.6 %collective-permute-start.17 = (f32[128,768]{1,0:T(8,128)S(1)}, f32[128,768]{1,0:T(8,128)S(1)}, u32[]{:S(2)}, u32[]{:S(2)}) collective-permute-start(f32[128,768]{1,0:T(8,128)S(1)} %get-tuple-element.92), channel_id=1, source_target_pairs={{0,2},{1,3},{2,0},{3,1},{4,6},{5,7},{6,4},{7,5},{8,10},{9,11},{10,... | collective-permute-start | bytes 1179656 | tf_op jit(solution)/shard_map/ppermute | solution.py:24
  53.1 2.4 %collective-permute-start.21 = (f16[4,152,256]{2,1,0:T(8,128)(2,1)S(1)}, f16[4,152,256]{2,1,0:T(8,128)(2,1)S(1)}, u32[]{:S(2)}, u32[]{:S(2)}) collective-permute-start(f16[4,152,256]{2,1,0:T(8,128)(2,1)S(1)} %pad_maximum_fusion.2), channel_id=1, source_target_pairs={{0,4},{4,0},{8,12},{12,8},{16,20},{20,16},{24,28},{28,24},{1,5},{5... | collective-permute-start | bytes 933896 | tf_op jit(solution)/shard_map/ppermute | solution.py:24
  56.1 1.7 %collective-permute-start.19 = (f16[152,256]{1,0:T(8,128)(2,1)S(1)}, f16[152,256]{1,0:T(8,128)(2,1)S(1)}, u32[]{:S(2)}, u32[]{:S(2)}) collective-permute-start(f16[152,256]{1,0:T(8,128)(2,1)S(1)} %convert_element_type.158), channel_id=1, source_target_pairs={{0,16},{4,20},{8,24},{12,28},{16,0},{20,4},{24,8},{28,12},{1,17},{... | collective-permute-start | bytes 233480 | tf_op jit(solution)/shard_map/ppermute | solution.py:24
  57.8 2.7 %collective-permute-start.20 = (f16[152,256]{1,0:T(8,128)(2,1)S(1)}, f16[152,256]{1,0:T(8,128)(2,1)S(1)}, u32[]{:S(2)}, u32[]{:S(2)}) collective-permute-start(f16[152,256]{1,0:T(8,128)(2,1)S(1)} %convert_element_type.158), channel_id=1, source_target_pairs={{0,24},{4,28},{8,16},{12,20},{16,8},{20,12},{24,0},{28,4},{1,25},{... | collective-permute-start | bytes 233480 | tf_op jit(solution)/shard_map/ppermute | solution.py:24
  61.5 2.4 %collective-permute-done.20 = f16[152,256]{1,0:T(8,128)(2,1)S(1)} collective-permute-done((f16[152,256]{1,0:T(8,128)(2,1)S(1)}, f16[152,256]{1,0:T(8,128)(2,1)S(1)}, u32[]{:S(2)}, u32[]{:S(2)}) %collective-permute-start.20) | collective-permute-done | bytes 77856 | tf_op jit(solution)/shard_map/ppermute | solution.py:24
  65.8 2.1 %input_terms.1 = bf16[2,128,768]{2,1,0:T(8,128)(2,1)S(1)} custom-call(bf16[1152,512]{1,0:T(8,128)(2,1)S(1)} %bitcast.97, f32[2,8,8,256]{3,2,1,0:T(8,128)S(1)} %pad_maximum_fusion.22.ends, bf16[2,128,768]{2,1,0:T(8,128)(2,1)S(1)} %bitcast.94, bf16[2,128,768]{2,1,0:T(8,128)(2,1)S(1)} %collective-permute-done.gb.refs_1_, ...), custom_call_target="tpu_custom_call" | custom-call | flops 1207959552 | bytes 3276800 | tf_op jit(solution)/shard_map/input_terms/pallas_call | solution.py:45
  69.0 2.2 %collective-permute-done.22 = f16[4,152,256]{2,1,0:T(8,128)(2,1)S(1)} collective-permute-done((f16[4,152,256]{2,1,0:T(8,128)(2,1)S(1)}, f16[4,152,256]{2,1,0:T(8,128)(2,1)S(1)}, u32[]{:S(2)}, u32[]{:S(2)}) %collective-permute-start.22) | collective-permute-done | bytes 311328 | tf_op jit(solution)/shard_map/ppermute | solution.py:24
  72.2 1.7 %maximum_bitcast_fusion = f32[128,3,3,512]{3,0,2,1:T(8,128)} fusion(f32[3,3,128,256]{3,2,1,0:T(8,128)S(1)} %bitcast.99, f32[3,3,128,256]{3,2,1,0:T(8,128)S(1)} %bitcast.98), kind=kLoop, calls=%fused_computation | loop fusion | flops 589824 | bytes 4718592 | tf_op jit(solution)/shard_map/transpose | solution.py:445
  (92 shorter events, 19.3 us)
Async XLA Ops:
  1.7 5.6 %collective-permute-start = (bf16[2,128,768]{2,1,0:T(8,128)(2,1)S(1)}, bf16[2,128,768]{2,1,0:T(8,128)(2,1)S(1)}, u32[]{:S(2)}, u32[]{:S(2)}) collective-permute-start(bf16[2,128,768]{2,1,0:T(8,128)(2,1)S(1)} %bitcast.91), channel_id=1, source_target_pairs={{0,1},{1,0},{2,3},{3,2},{4,5},{5,4},{6,7},{7,6},{8,9},{9,8},{10,11... | collective-permute-start | bytes 1179656 | tf_op jit(solution)/shard_map/ppermute | solution.py:24
  2.2 12.3 %collective-permute-start.2 = (bf16[2,128,768]{2,1,0:T(8,128)(2,1)S(1)}, bf16[2,128,768]{2,1,0:T(8,128)(2,1)S(1)}, u32[]{:S(2)}, u32[]{:S(2)}) collective-permute-start(bf16[2,128,768]{2,1,0:T(8,128)(2,1)S(1)} %bitcast.92), channel_id=1, source_target_pairs={{0,2},{1,3},{2,0},{3,1},{4,6},{5,7},{6,4},{7,5},{8,10},{9,11},{10,... | collective-permute-start | bytes 1179656 | tf_op jit(solution)/shard_map/ppermute | solution.py:24
  8.6 9.3 %collective-permute-start.1 = (f16[592,256]{1,0:T(8,128)(2,1)S(1)}, f16[592,256]{1,0:T(8,128)(2,1)S(1)}, u32[]{:S(2)}, u32[]{:S(2)}) collective-permute-start(f16[592,256]{1,0:T(8,128)(2,1)S(1)} %convert_element_type.124), channel_id=1, source_target_pairs={{0,4},{4,0},{8,12},{12,8},{16,20},{20,16},{24,28},{28,24},{1,5},{5... | collective-permute-start | bytes 909320 | tf_op jit(solution)/shard_map/ppermute | solution.py:24
  14.5 3.7 %collective-permute-start.4 = (bf16[2,128,768]{2,1,0:T(8,128)(2,1)S(1)}, bf16[2,128,768]{2,1,0:T(8,128)(2,1)S(1)}, u32[]{:S(2)}, u32[]{:S(2)}) collective-permute-start(bf16[2,128,768]{2,1,0:T(8,128)(2,1)S(1)} %collective-permute-done.2.ga.refs_2_), channel_id=1, source_target_pairs={{0,1},{1,0},{2,3},{3,2},{4,5},{5,4},{6,7},{7,6},{8,9},{9,8},{10,11... | collective-permute-start | bytes 1179656 | tf_op jit(solution)/shard_map/ppermute | solution.py:24
  14.5 8.5 %collective-permute-start.3 = (bf16[1,256]{1,0:T(2,128)(2,1)S(1)}, bf16[1,256]{1,0:T(2,128)(2,1)S(1)}, u32[]{:S(2)}, u32[]{:S(2)}) collective-permute-start(bf16[1,256]{1,0:T(2,128)(2,1)S(1)} %broadcast_select_fusion.29), channel_id=1, source_target_pairs={{4,8},{12,16},{20,24},{8,4},{16,12},{24,20},{5,9},{13,17},{21,25},... | collective-permute-start | bytes 1544 | tf_op jit(solution)/shard_map/ppermute | solution.py:363
  19.3 8.7 %copy-start.2 = (bf16[128,3,3,512]{3,0,2,1:T(8,128)(2,1)S(1)}, bf16[128,3,3,512]{3,0,2,1:T(8,128)(2,1)}, u32[]{:S(2)}) copy-start(bf16[128,3,3,512]{3,0,2,1:T(8,128)(2,1)} %param.4) | copy-start | bytes 3538948
  19.4 10.7 %collective-permute-start.6 = (f16[592,256]{1,0:T(8,128)(2,1)S(1)}, f16[592,256]{1,0:T(8,128)(2,1)S(1)}, u32[]{:S(2)}, u32[]{:S(2)}) collective-permute-start(f16[592,256]{1,0:T(8,128)(2,1)S(1)} %convert_element_type.134), channel_id=1, source_target_pairs={{0,4},{4,0},{8,12},{12,8},{16,20},{20,16},{24,28},{28,24},{1,5},{5... | collective-permute-start | bytes 909320 | tf_op jit(solution)/shard_map/ppermute | solution.py:24
  21.5 8.7 %collective-permute-start.7 = (f16[168,256]{1,0:T(8,128)(2,1)S(1)}, f16[168,256]{1,0:T(8,128)(2,1)S(1)}, u32[]{:S(2)}, u32[]{:S(2)}) collective-permute-start(f16[168,256]{1,0:T(8,128)(2,1)S(1)} %get-tuple-element.71), channel_id=1, source_target_pairs={{0,8},{4,12},{8,0},{12,4},{16,24},{20,28},{24,16},{28,20},{1,9},{5... | collective-permute-start | bytes 258056 | tf_op jit(solution)/shard_map/ppermute | solution.py:24
  23.0 9.7 %collective-permute-start.8 = (f16[168,256]{1,0:T(8,128)(2,1)S(1)}, f16[168,256]{1,0:T(8,128)(2,1)S(1)}, u32[]{:S(2)}, u32[]{:S(2)}) collective-permute-start(f16[168,256]{1,0:T(8,128)(2,1)S(1)} %get-tuple-element.79), channel_id=1, source_target_pairs={{0,16},{4,20},{8,24},{12,28},{16,0},{20,4},{24,8},{28,12},{1,17},{... | collective-permute-start | bytes 258056 | tf_op jit(solution)/shard_map/ppermute | solution.py:24
  25.1 7.6 %collective-permute-start.9 = (f16[168,256]{1,0:T(8,128)(2,1)S(1)}, f16[168,256]{1,0:T(8,128)(2,1)S(1)}, u32[]{:S(2)}, u32[]{:S(2)}) collective-permute-start(f16[168,256]{1,0:T(8,128)(2,1)S(1)} %get-tuple-element.80), channel_id=1, source_target_pairs={{0,24},{4,28},{8,16},{12,20},{16,8},{20,12},{24,0},{28,4},{1,25},{... | collective-permute-start | bytes 258056 | tf_op jit(solution)/shard_map/ppermute | solution.py:24
  30.0 8.8 %collective-permute-start.5 = (f32[2,2,128,768]{3,2,1,0:T(8,128)S(1)}, f32[2,2,128,768]{3,2,1,0:T(8,128)S(1)}, u32[]{:S(2)}, u32[]{:S(2)}) collective-permute-start(f32[2,2,128,768]{3,2,1,0:T(8,128)S(1)} %get-tuple-element.76), channel_id=1, source_target_pairs={{0,1},{1,0},{2,3},{3,2},{4,5},{5,4},{6,7},{7,6},{8,9},{9,8},{10,11... | collective-permute-start | bytes 4718600 | tf_op jit(solution)/shard_map/ppermute | solution.py:24
  33.4 7.7 %collective-permute-start.14 = (f16[152,256]{1,0:T(8,128)(2,1)S(1)}, f16[152,256]{1,0:T(8,128)(2,1)S(1)}, u32[]{:S(2)}, u32[]{:S(2)}) collective-permute-start(f16[152,256]{1,0:T(8,128)(2,1)S(1)} %convert_element_type.149), channel_id=1, source_target_pairs={{0,8},{4,12},{8,0},{12,4},{16,24},{20,28},{24,16},{28,20},{1,9},{5... | collective-permute-start | bytes 233480 | tf_op jit(solution)/shard_map/ppermute | solution.py:24
  34.9 9.2 %collective-permute-start.15 = (f16[152,256]{1,0:T(8,128)(2,1)S(1)}, f16[152,256]{1,0:T(8,128)(2,1)S(1)}, u32[]{:S(2)}, u32[]{:S(2)}) collective-permute-start(f16[152,256]{1,0:T(8,128)(2,1)S(1)} %convert_element_type.149), channel_id=1, source_target_pairs={{0,16},{4,20},{8,24},{12,28},{16,0},{20,4},{24,8},{28,12},{1,17},{... | collective-permute-start | bytes 233480 | tf_op jit(solution)/shard_map/ppermute | solution.py:24
  36.1 9.6 %collective-permute-start.16 = (f16[152,256]{1,0:T(8,128)(2,1)S(1)}, f16[152,256]{1,0:T(8,128)(2,1)S(1)}, u32[]{:S(2)}, u32[]{:S(2)}) collective-permute-start(f16[152,256]{1,0:T(8,128)(2,1)S(1)} %convert_element_type.149), channel_id=1, source_target_pairs={{0,24},{4,28},{8,16},{12,20},{16,8},{20,12},{24,0},{28,4},{1,25},{... | collective-permute-start | bytes 233480 | tf_op jit(solution)/shard_map/ppermute | solution.py:24
  38.1 7.5 %collective-permute-start.11 = (f16[168,256]{1,0:T(8,128)(2,1)S(1)}, f16[168,256]{1,0:T(8,128)(2,1)S(1)}, u32[]{:S(2)}, u32[]{:S(2)}) collective-permute-start(f16[168,256]{1,0:T(8,128)(2,1)S(1)} %get-tuple-element.87), channel_id=1, source_target_pairs={{0,8},{4,12},{8,0},{12,4},{16,24},{20,28},{24,16},{28,20},{1,9},{5... | collective-permute-start | bytes 258056 | tf_op jit(solution)/shard_map/ppermute | solution.py:24
  38.8 11.5 %collective-permute-start.12 = (f16[168,256]{1,0:T(8,128)(2,1)S(1)}, f16[168,256]{1,0:T(8,128)(2,1)S(1)}, u32[]{:S(2)}, u32[]{:S(2)}) collective-permute-start(f16[168,256]{1,0:T(8,128)(2,1)S(1)} %get-tuple-element.90), channel_id=1, source_target_pairs={{0,16},{4,20},{8,24},{12,28},{16,0},{20,4},{24,8},{28,12},{1,17},{... | collective-permute-start | bytes 258056 | tf_op jit(solution)/shard_map/ppermute | solution.py:24
  41.1 9.2 %collective-permute-start.13 = (f16[168,256]{1,0:T(8,128)(2,1)S(1)}, f16[168,256]{1,0:T(8,128)(2,1)S(1)}, u32[]{:S(2)}, u32[]{:S(2)}) collective-permute-start(f16[168,256]{1,0:T(8,128)(2,1)S(1)} %get-tuple-element.91), channel_id=1, source_target_pairs={{0,24},{4,28},{8,16},{12,20},{16,8},{20,12},{24,0},{28,4},{1,25},{... | collective-permute-start | bytes 258056 | tf_op jit(solution)/shard_map/ppermute | solution.py:24
  44.1 9.0 %collective-permute-start.10 = (f32[128,768]{1,0:T(8,128)S(1)}, f32[128,768]{1,0:T(8,128)S(1)}, u32[]{:S(2)}, u32[]{:S(2)}) collective-permute-start(f32[128,768]{1,0:T(8,128)S(1)} %get-tuple-element.89), channel_id=1, source_target_pairs={{0,2},{1,3},{2,0},{3,1},{4,6},{5,7},{6,4},{7,5},{8,10},{9,11},{10,... | collective-permute-start | bytes 1179656 | tf_op jit(solution)/shard_map/ppermute | solution.py:24
  50.4 10.0 %collective-permute-start.17 = (f32[128,768]{1,0:T(8,128)S(1)}, f32[128,768]{1,0:T(8,128)S(1)}, u32[]{:S(2)}, u32[]{:S(2)}) collective-permute-start(f32[128,768]{1,0:T(8,128)S(1)} %get-tuple-element.92), channel_id=1, source_target_pairs={{0,2},{1,3},{2,0},{3,1},{4,6},{5,7},{6,4},{7,5},{8,10},{9,11},{10,... | collective-permute-start | bytes 1179656 | tf_op jit(solution)/shard_map/ppermute | solution.py:24
  53.1 7.4 %collective-permute-start.21 = (f16[4,152,256]{2,1,0:T(8,128)(2,1)S(1)}, f16[4,152,256]{2,1,0:T(8,128)(2,1)S(1)}, u32[]{:S(2)}, u32[]{:S(2)}) collective-permute-start(f16[4,152,256]{2,1,0:T(8,128)(2,1)S(1)} %pad_maximum_fusion.2), channel_id=1, source_target_pairs={{0,4},{4,0},{8,12},{12,8},{16,20},{20,16},{24,28},{28,24},{1,5},{5... | collective-permute-start | bytes 933896 | tf_op jit(solution)/shard_map/ppermute | solution.py:24
  56.0 5.6 %collective-permute-start.18 = (f16[152,256]{1,0:T(8,128)(2,1)S(1)}, f16[152,256]{1,0:T(8,128)(2,1)S(1)}, u32[]{:S(2)}, u32[]{:S(2)}) collective-permute-start(f16[152,256]{1,0:T(8,128)(2,1)S(1)} %convert_element_type.158), channel_id=1, source_target_pairs={{0,8},{4,12},{8,0},{12,4},{16,24},{20,28},{24,16},{28,20},{1,9},{5... | collective-permute-start | bytes 233480 | tf_op jit(solution)/shard_map/ppermute | solution.py:24
  56.1 5.5 %collective-permute-start.19 = (f16[152,256]{1,0:T(8,128)(2,1)S(1)}, f16[152,256]{1,0:T(8,128)(2,1)S(1)}, u32[]{:S(2)}, u32[]{:S(2)}) collective-permute-start(f16[152,256]{1,0:T(8,128)(2,1)S(1)} %convert_element_type.158), channel_id=1, source_target_pairs={{0,16},{4,20},{8,24},{12,28},{16,0},{20,4},{24,8},{28,12},{1,17},{... | collective-permute-start | bytes 233480 | tf_op jit(solution)/shard_map/ppermute | solution.py:24
  57.8 6.2 %collective-permute-start.20 = (f16[152,256]{1,0:T(8,128)(2,1)S(1)}, f16[152,256]{1,0:T(8,128)(2,1)S(1)}, u32[]{:S(2)}, u32[]{:S(2)}) collective-permute-start(f16[152,256]{1,0:T(8,128)(2,1)S(1)} %convert_element_type.158), channel_id=1, source_target_pairs={{0,24},{4,28},{8,16},{12,20},{16,8},{20,12},{24,0},{28,4},{1,25},{... | collective-permute-start | bytes 233480 | tf_op jit(solution)/shard_map/ppermute | solution.py:24
  64.2 7.0 %collective-permute-start.22 = (f16[4,152,256]{2,1,0:T(8,128)(2,1)S(1)}, f16[4,152,256]{2,1,0:T(8,128)(2,1)S(1)}, u32[]{:S(2)}, u32[]{:S(2)}) collective-permute-start(f16[4,152,256]{2,1,0:T(8,128)(2,1)S(1)} %pad_maximum_fusion.3), channel_id=1, source_target_pairs={{0,4},{4,0},{8,12},{12,8},{16,20},{20,16},{24,28},{28,24},{1,5},{5... | collective-permute-start | bytes 933896 | tf_op jit(solution)/shard_map/ppermute | solution.py:24
  (2 other events, 8.7 us)

commit v4 on v3

--- a/solution.py
+++ b/solution.py
@@ -167,6 +167,24 @@
     out[piece:, :] = jnp.broadcast_to(power, (POWER, lanes))
 
 
+def place_kernel(piece, layout, *refs):
+    *parts, out, sems = refs
+    tile, me = lax.axis_index("width"), lax.axis_index("chan") >> 1
+    half = lax.axis_size("width") // 2
+    lanes = parts[0].shape[1]
+    copies = []
+    for part, (chunk, other, first) in zip(parts, layout):
+        col = pl.multiple_of((me ^ chunk) * lanes, LANES)
+        for n in range(part.shape[0] // piece):
+            row = ((tile & 1) ^ other) * half + ((tile >> 1) ^ (first + n))
+            place = out.at[pl.ds(pl.multiple_of(row * piece, 16), piece), pl.ds(col, lanes)]
+            copies.append(pltpu.make_async_copy(part.at[pl.ds(n * piece, piece)], place, sems.at[len(copies)]))
+    for copy in copies:
+        copy.start()
+    for copy in copies:
+        copy.wait()
+
+
 def forward_kernel(xs, f, send, keep, acc):
     rows, deep, cols = xs.shape
     groups = lax.axis_size("chan")
@@ -256,7 +274,7 @@
     return total + got[:count].astype(F32) * jnp.exp2(got[count : count + 1].astype(F32) - TOP)
 
 
-def chunk_stages(send, keep, finish, order, late, arrived):
+def chunk_stages(send, keep, finish, order, late, direct, halves, arrived):
     others = 1 << len(late) - 1
     lanes = send.shape[1]
     total, power = keep[:-POWER], keep[-1:]
@@ -287,16 +305,30 @@
     every = in_order([ends] + [got[piece + POWER :] for got in gots], late[1:])
     every = jnp.concatenate([v.reshape(2, EDGE, lanes) for v in every], axis=0).astype(F32)
     own = order(finish(total, every).astype(F16))
-    gots = [exchange(own, "width", 2 * n) for n in range(1, others)]
-    yield None
-    gots = order(gots)
-    yield None
-    own = order(jnp.stack(in_order([own] + gots, late[1:])))
-    got = exchange(own, "width", 1)
-    yield None
-    got = order(got)
-    yield None
-    yield jnp.concatenate(doubled(got, own, late[0]), axis=0)
+    own = [own]
+    if direct:
+        own += [exchange(own[0], "width", 2 * n) for n in range(1, others)]
+        yield None
+    else:
+        for b in reversed(range(1, len(late))):
+            got = exchange(jnp.stack(own), "width", 1 << b)
+            yield None
+            got = order(got)
+            yield None
+            own = order([piece for piece in own] + [got[n] for n in range(len(own))])
+        own = [own[reversed_bits(n, len(late) - 1)] for n in range(others)]
+    parts = (range(others // 2), range(others // 2, others)) if direct and halves else (range(others),)
+    gots = []
+    for part in parts:
+        part = order([own[n] for n in part])
+        yield None
+        part = order(jnp.stack(part))
+        gots.append((part, exchange(part, "width", 1)))
+    pairs = []
+    for part, got in gots:
+        yield None
+        pairs.append((unpacked(part), unpacked(order(got))))
+    yield pairs
 
 
 def unpacked(every):
@@ -305,13 +337,26 @@
     return (every[:, :rows].astype(F32) * scale).reshape(-1, every.shape[2])
 
 
-def chunk_times(j):
-    now = 2.05 * j
-    times = [now - 0.1 if j else now]
-    for step in range(4):
-        now += 2.0
-        times += [now - (0.2 if j and step == 0 else 0.1), now]
-    return times
+FIRST = (0.0, 1.9, 2.0, 3.9, 4.0, 5.9, 6.0, 7.9)
+LATER = (1.95, 3.85, 4.05, 5.95, 6.05, 6.5, 6.6, 6.7, 9.9, 10.0)
+FORWARD = (0.1, 0.2, 2.7, 4.2, 5.98, 6.75)
+BACKWARD = (6.72, 9.6)
+PARTNERS = 0.3
+AFTER = 2.0
+DIRECT = (True, True)
+SPLIT = True
+HALVES = (False, True)
+
+
+def chunk_times(j, steps):
+    base = FIRST if j == 0 else [now + AFTER * (j - 1) for now in LATER]
+    if DIRECT[min(j, 1)]:
+        return base
+    hops = []
+    for n in range(1, steps):
+        now = base[4] + (base[6] - base[4]) * n / (steps - 1)
+        hops += [now - 0.1 if n < steps - 1 else base[5], now]
+    return [*base[:5], *hops, *base[7:]]
 
 
 def body(activations, filters, cotangent):
@@ -354,7 +399,7 @@
             shape = ((piece + POWER, lanes), F32)
             return call(body, "border_terms", [shape], [((width * piece, lanes), F32)], 0, total, ends[0], ends[j])
 
-        return chunk_stages(send, keep, finish, order, late, arrived)
+        return chunk_stages(send, keep, finish, order, late, DIRECT[min(j, 1)], HALVES[min(j, 1)], arrived)
 
     def forward():
         odd = late[0]
@@ -362,9 +407,10 @@
         mine = jnp.where(odd, columns[1:2], columns[0:1])
         far = lax.ppermute(order(mine), "width", pairs + [(j, i) for i, j in pairs])
         yield None
-        near = arrived[0].astype(F32)
+        far = order(far)
+        yield None
+        near = order(arrived[0]).astype(F32)
         near = (jnp.where(odd, near[3:4], near[2:3]) * jnp.exp2(near[0:1] - TOP)).astype(BF16)
-        far = order(far)
         left, right = jnp.where(odd, near, far), jnp.where(odd, far, near)
         send, keep = call(
             forward_kernel,
@@ -380,12 +426,13 @@
             yield None
             total = keep + order(got)
             keep, send = total[: total.shape[0] // 2], total[total.shape[0] // 2 :]
-        gots = [exchange(order(send[0, h]), "chan", 1 << bits_of(groups) - 1) for h in range(rows)]
-        yield None
+        hop = 1 << bits_of(groups) - 1
+        gots = [exchange(order(send[0, h]), "chan", hop) for h in range(rows)] if SPLIT else []
         sums = []
         for h in range(rows):
-            sums.append((keep[0, h] + order(gots[h])).astype(BF16))
+            got = gots[h] if SPLIT else exchange(order(send[0, h]), "chan", hop)
             yield None
+            sums.append((keep[0, h] + order(got)).astype(BF16))
         result["conv"] = jnp.transpose(jnp.stack(sums), (1, 0, 2))
 
     def backward():
@@ -406,15 +453,15 @@
         if j:
             g[2 * j + 1] = order(g[2 * j + 1])
         stages = filter_chunk(j)
-        if j == 0:
-            next(stages)
-            for r in sorted(g):
-                if r > 1:
-                    g[r | 1] = exchange(order(g[r]), "chan", 1)
-            yield None
         for piece in stages:
             pieces[j] = piece
             yield None
+
+    def partners():
+        for r in sorted(g):
+            if r > 1:
+                g[r | 1] = exchange(order(g[r]), "chan", 1)
+        yield None
 
     g = {0: order(jnp.transpose(cotangent, (1, 0, 2)))}
     g[1] = exchange(g[0], "chan", 1)
@@ -427,21 +474,48 @@
     turns = []
     for j in range(groups // 2):
         stages = chunk(j)
-        turns += [(now, stages) for now in chunk_times(j)]
-    finale = turns[-1][0]
+        turns += [(now, stages) for now in chunk_times(j, bits_of(width))]
     conv = forward()
-    turns += [(0.1, conv), (2.7, conv)] + [(4.2 + 2 * b, conv) for b in range(hops - 1)]
-    turns += [(1.98 + 2 * hops, conv), (3.5 + 2 * hops, conv), (3.6 + 2 * hops, conv)]
+    extra = AFTER * (groups // 2 - 2)
+    turns += [(FORWARD[0], conv), (FORWARD[1], conv), (PARTNERS, partners()), (FORWARD[2], conv)]
+    turns += [(FORWARD[3] + b, conv) for b in range(hops - 1)]
+    turns += [(FORWARD[4] + hops - 2, conv), (FORWARD[5] + hops - 2, conv), (FORWARD[5] + hops - 1.99, conv)]
     grad = backward()
-    turns += [(max(finale - 2.9, chunk_times(groups // 2 - 1)[4] + 0.2), grad), (finale - 0.4, grad)]
+    turns += [(BACKWARD[0] + extra, grad), (BACKWARD[1] + extra, grad)]
     for now, stages in sorted(turns, key=lambda turn: turn[0]):
         next(stages, None)
+    for stages in dict.fromkeys(stages for _, stages in turns):
+        for _ in stages:
+            pass
     conv_output, input_grad = result["conv"], result["grad"]
     pieces = [pieces[j] for j in range(groups // 2)]
 
-    for b in range(bits_of(groups // 2)):
-        pieces = [jnp.where(swaps[b], pieces[j ^ 1 << b], pieces[j]) for j in range(len(pieces))]
-    grads = jnp.concatenate([unpacked(p) for p in pieces], axis=1)[: 9 * chans]
+    if lanes % LANES:
+        sides = [[jnp.concatenate([pair[side] for pair in pieces[j]], axis=0) for side in range(2)] for j in range(len(pieces))]
+        sides = [[jnp.split(v, width // 2, axis=0) for v in pair] for pair in sides]
+        sides = [[jnp.concatenate(in_order(v, late[1:]), axis=0) for v in pair] for pair in sides]
+        pieces = [jnp.concatenate(doubled(got, own, late[0]), axis=0) for own, got in sides]
+        for b in range(bits_of(groups // 2)):
+            pieces = [jnp.where(swaps[b], pieces[j ^ 1 << b], pieces[j]) for j in range(len(pieces))]
+        grads = jnp.concatenate(pieces, axis=1)
+    else:
+        parts, layout = [], []
+        for j, pairs in enumerate(pieces):
+            first = 0
+            for own, got in pairs:
+                parts += [own, got]
+                layout += [(j, 0, first), (j, 1, first)]
+                first += own.shape[0] // piece
+        grads = pl.pallas_call(
+            functools.partial(place_kernel, piece, layout),
+            out_shape=jax.ShapeDtypeStruct((width * piece, outs), F32),
+            in_specs=[VMEM] * len(parts),
+            out_specs=pl.BlockSpec(memory_space=pl.ANY),
+            scratch_shapes=[pltpu.SemaphoreType.DMA((width * groups // 2,))],
+            compiler_params=pltpu.CompilerParams(vmem_limit_bytes=16 << 20),
+            name="place_pieces",
+        )(*parts)
+    grads = grads[: 9 * chans]
     grads = jnp.transpose(grads.reshape(3, 3, chans, outs), (2, 0, 1, 3))
     return conv_output, input_grad, grads
 

time: 74.1 us -> 70.2 us (0.947)
  waiting for transfers between devices: 21.7 us -> 18.9 us
  other arithmetic: 4.47 us -> 1.82 us
  Pallas kernels: 10.9 us -> 12.5 us
    ppermute x22 -> x23, waiting for transfers between devices: 21.7 us -> 18.9 us  [exchange(): return lax.ppermute(value, axis, [(i, i ^ bit) for i in range(devices)])]
    transpose x1 -> x0, other arithmetic: 1.73 us -> none  [body(): grads = jnp.transpose(grads.reshape(3, 3, chans, outs), (2, 0, 1, 3))]
    pallas_call x0 -> x1, Pallas kernels: none -> 1.55 us  [body(): pl.pallas_call(functools.partial(place_kernel, piece, layout), out_shape=...]
    ppermute x22 -> x23, starting transfers between devices: 30.4 us -> 30.2 us  [exchange(): return lax.ppermute(value, axis, [(i, i ^ bit) for i in range(devices)])]
    unnamed x10 -> x14, local copies, waits for them, and re-layouts: 3.32 us -> 3.33 us
  transfers between devices with their start and end apart: 23 -> 24, of which waited for: 9 -> 10; matrix products, arithmetic and copies ran while one was open for 5% -> 6% of each run, Pallas kernels for 15% -> 14%
where the time goes in v4:
time: 70.2 us; the launch traced here: 70 us
  starting transfers between devices  31 us (44%)
  waiting for transfers between devices  18.9 us (27%)
  Pallas kernels  12.5 us (18%)
  local copies, waits for them, and re-layouts  4.43 us (6%)
  other arithmetic  1.82 us (3%)
  between operations  1.3 us (2%)
    ppermute x23, starting transfers between devices, exchange(): return lax.ppermute(value, axis, [(i, i ^ bit) for i in range(devices)])  30.2 us
    ppermute x23, waiting for transfers between devices, exchange(): return lax.ppermute(value, axis, [(i, i ^ bit) for i in range(devices)])  18.9 us
    pallas_call x8, Pallas kernels, call(): pl.pallas_call(body, out_shape=outs, in_specs=[VMEM] * len(args), out_spe...  10.9 us
    unnamed x14, local copies, waits for them, and re-layouts  3.33 us
    pallas_call x1, Pallas kernels, body(): pl.pallas_call(functools.partial(place_kernel, piece, layout), out_shape=...  1.55 us
  transfers between devices with their start and end apart: 24, of which 10 were waited for; matrix products, arithmetic and copies ran while one was open for 6% of the time, Pallas kernels for 14%

profile of v4, /device:TPU:0, one launch (start us, length us, event | category | flops | bytes accessed | tf_op | source)
XLA Modules:
  0.0 70.0 jit_solution(18260223701343713297)
XLA Ops:
  2.2 2.6 %collective-permute-start.2 = (bf16[2,128,768]{2,1,0:T(8,128)(2,1)S(1)}, bf16[2,128,768]{2,1,0:T(8,128)(2,1)S(1)}, u32[]{:S(2)}, u32[]{:S(2)}) collective-permute-start(bf16[2,128,768]{2,1,0:T(8,128)(2,1)S(1)} %bitcast.107), channel_id=1, source_target_pairs={{0,2},{1,3},{2,0},{3,1},{4,6},{5,7},{6,4},{7,5},{8,10},{9,11},{10,... | collective-permute-start | bytes 1179656 | tf_op jit(solution)/shard_map/ppermute | solution.py:24
  5.8 1.5 %shifted_taps.2 = (bf16[2,384,768]{2,1,0:T(8,128)(2,1)S(1)}, bf16[2,256]{1,0:T(2,128)(2,1)S(1)}) custom-call(bf16[128,2,768]{2,1,0:T(2,128)(2,1)S(1)} %copy-done), custom_call_target="tpu_custom_call" | custom-call | bytes 1573888 | tf_op jit(solution)/shard_map/shifted_taps/pallas_call | solution.py:45
  7.3 1.2 %filter_terms.2 = (f32[592,256]{1,0:T(8,128)S(1)}, f32[584,256]{1,0:T(8,128)S(1)}) custom-call(bf16[2,384,768]{2,1,0:T(8,128)(2,1)S(1)} %get-tuple-element.63.xs, bf16[2,128,768]{2,1,0:T(8,128)(2,1)S(1)} %bitcast.108, bf16[2,128,768]{2,1,0:T(8,128)(2,1)S(1)} %collective-permute-done.gb.refs_1_), custom_call_target="tpu_custom_call" | custom-call | flops 603979776 | bytes 3170304 | tf_op jit(solution)/shard_map/filter_terms/pallas_call | solution.py:45
  8.6 1.6 %collective-permute-start.1 = (f16[592,256]{1,0:T(8,128)(2,1)S(1)}, f16[592,256]{1,0:T(8,128)(2,1)S(1)}, u32[]{:S(2)}, u32[]{:S(2)}) collective-permute-start(f16[592,256]{1,0:T(8,128)(2,1)S(1)} %convert_element_type.148), channel_id=1, source_target_pairs={{0,4},{4,0},{8,12},{12,8},{16,20},{20,16},{24,28},{28,24},{1,5},{5... | collective-permute-start | bytes 909320 | tf_op jit(solution)/shard_map/ppermute | solution.py:24
  11.0 3.5 %collective-permute-done.2.ga.refs_2_ = bf16[2,128,768]{2,1,0:T(8,128)(2,1)S(1)} collective-permute-done((bf16[2,128,768]{2,1,0:T(8,128)(2,1)S(1)}, bf16[2,128,768]{2,1,0:T(8,128)(2,1)S(1)}, u32[]{:S(2)}, u32[]{:S(2)}) %collective-permute-start.2) | collective-permute-done | bytes 393248 | tf_op jit(solution)/shard_map/ppermute | solution.py:24
  14.5 3.4 %collective-permute-done.1 = f16[592,256]{1,0:T(8,128)(2,1)S(1)} collective-permute-done((f16[592,256]{1,0:T(8,128)(2,1)S(1)}, f16[592,256]{1,0:T(8,128)(2,1)S(1)}, u32[]{:S(2)}, u32[]{:S(2)}) %collective-permute-start.1) | collective-permute-done | bytes 303136 | tf_op jit(solution)/shard_map/ppermute | solution.py:24
  19.4 1.6 %collective-permute-start.6 = (f16[592,256]{1,0:T(8,128)(2,1)S(1)}, f16[592,256]{1,0:T(8,128)(2,1)S(1)}, u32[]{:S(2)}, u32[]{:S(2)}) collective-permute-start(f16[592,256]{1,0:T(8,128)(2,1)S(1)} %convert_element_type.156), channel_id=1, source_target_pairs={{0,4},{4,0},{8,12},{12,8},{16,20},{20,16},{24,28},{28,24},{1,5},{5... | collective-permute-start | bytes 909320 | tf_op jit(solution)/shard_map/ppermute | solution.py:24
  20.9 1.6 %collective-permute-start.7 = (f16[168,256]{1,0:T(8,128)(2,1)S(1)}, f16[168,256]{1,0:T(8,128)(2,1)S(1)}, u32[]{:S(2)}, u32[]{:S(2)}) collective-permute-start(f16[168,256]{1,0:T(8,128)(2,1)S(1)} %get-tuple-element.76), channel_id=1, source_target_pairs={{0,8},{4,12},{8,0},{12,4},{16,24},{20,28},{24,16},{28,20},{1,9},{5... | collective-permute-start | bytes 258056 | tf_op jit(solution)/shard_map/ppermute | solution.py:24
  22.5 2.6 %collective-permute-start.8 = (f16[168,256]{1,0:T(8,128)(2,1)S(1)}, f16[168,256]{1,0:T(8,128)(2,1)S(1)}, u32[]{:S(2)}, u32[]{:S(2)}) collective-permute-start(f16[168,256]{1,0:T(8,128)(2,1)S(1)} %get-tuple-element.84), channel_id=1, source_target_pairs={{0,16},{4,20},{8,24},{12,28},{16,0},{20,4},{24,8},{28,12},{1,17},{... | collective-permute-start | bytes 258056 | tf_op jit(solution)/shard_map/ppermute | solution.py:24
  25.4 2.1 %shifted_taps.3 = (bf16[2,384,768]{2,1,0:T(8,128)(2,1)S(1)}, bf16[2,256]{1,0:T(2,128)(2,1)}) custom-call(bf16[128,2,768]{2,1,0:T(2,128)(2,1)S(1)} %copy-done.1, bf16[1,256]{1,0:T(2,128)(2,1)S(1)} %broadcast_select_fusion.13.refs_0_, bf16[1,256]{1,0:T(2,128)(2,1)S(1)} %get-tuple-element.126.refs_1_), custom_call_target="tpu_custom_call" | custom-call | bytes 1574912 | tf_op jit(solution)/shard_map/shifted_taps/pallas_call | solution.py:45
  27.5 2.0 %forward_terms.1 = (f32[2,2,128,768]{3,2,1,0:T(8,128)S(1)}, f32[2,2,128,768]{3,2,1,0:T(8,128)S(1)}) custom-call(bf16[2,384,768]{2,1,0:T(8,128)(2,1)S(1)} %get-tuple-element.78.xs, bf16[3,384,512]{2,1,0:T(8,128)(2,1)S(1)} %bitcast.111), custom_call_target="tpu_custom_call" | custom-call | flops 1207959552 | bytes 5505024 | tf_op jit(solution)/shard_map/forward_terms/pallas_call | solution.py:45
  30.4 1.2 %collective-permute-done.9 = f16[168,256]{1,0:T(8,128)(2,1)S(1)} collective-permute-done((f16[168,256]{1,0:T(8,128)(2,1)S(1)}, f16[168,256]{1,0:T(8,128)(2,1)S(1)}, u32[]{:S(2)}, u32[]{:S(2)}) %collective-permute-start.9) | collective-permute-done | bytes 86048 | tf_op jit(solution)/shard_map/ppermute | solution.py:24
  32.2 1.3 %collective-permute-start.14 = (f16[152,256]{1,0:T(8,128)(2,1)S(1)}, f16[152,256]{1,0:T(8,128)(2,1)S(1)}, u32[]{:S(2)}, u32[]{:S(2)}) collective-permute-start(f16[152,256]{1,0:T(8,128)(2,1)S(1)} %convert_element_type.173), channel_id=1, source_target_pairs={{0,8},{4,12},{8,0},{12,4},{16,24},{20,28},{24,16},{28,20},{1,9},{5... | collective-permute-start | bytes 233480 | tf_op jit(solution)/shard_map/ppermute | solution.py:24
  33.5 1.6 %collective-permute-start.15 = (f16[152,256]{1,0:T(8,128)(2,1)S(1)}, f16[152,256]{1,0:T(8,128)(2,1)S(1)}, u32[]{:S(2)}, u32[]{:S(2)}) collective-permute-start(f16[152,256]{1,0:T(8,128)(2,1)S(1)} %convert_element_type.173), channel_id=1, source_target_pairs={{0,16},{4,20},{8,24},{12,28},{16,0},{20,4},{24,8},{28,12},{1,17},{... | collective-permute-start | bytes 233480 | tf_op jit(solution)/shard_map/ppermute | solution.py:24
  35.1 1.6 %collective-permute-start.16 = (f16[152,256]{1,0:T(8,128)(2,1)S(1)}, f16[152,256]{1,0:T(8,128)(2,1)S(1)}, u32[]{:S(2)}, u32[]{:S(2)}) collective-permute-start(f16[152,256]{1,0:T(8,128)(2,1)S(1)} %convert_element_type.173), channel_id=1, source_target_pairs={{0,24},{4,28},{8,16},{12,20},{16,8},{20,12},{24,0},{28,4},{1,25},{... | collective-permute-start | bytes 233480 | tf_op jit(solution)/shard_map/ppermute | solution.py:24
  37.4 2.5 %collective-permute-start.12 = (f16[168,256]{1,0:T(8,128)(2,1)S(1)}, f16[168,256]{1,0:T(8,128)(2,1)S(1)}, u32[]{:S(2)}, u32[]{:S(2)}) collective-permute-start(f16[168,256]{1,0:T(8,128)(2,1)S(1)} %get-tuple-element.95), channel_id=1, source_target_pairs={{0,16},{4,20},{8,24},{12,28},{16,0},{20,4},{24,8},{28,12},{1,17},{... | collective-permute-start | bytes 258056 | tf_op jit(solution)/shard_map/ppermute | solution.py:24
  40.2 1.6 %collective-permute-start.13 = (f16[168,256]{1,0:T(8,128)(2,1)S(1)}, f16[168,256]{1,0:T(8,128)(2,1)S(1)}, u32[]{:S(2)}, u32[]{:S(2)}) collective-permute-start(f16[168,256]{1,0:T(8,128)(2,1)S(1)} %get-tuple-element.96), channel_id=1, source_target_pairs={{0,24},{4,28},{8,16},{12,20},{16,8},{20,12},{24,0},{28,4},{1,25},{... | collective-permute-start | bytes 258056 | tf_op jit(solution)/shard_map/ppermute | solution.py:24
  42.9 5.8 %collective-permute-done.12 = f16[168,256]{1,0:T(8,128)(2,1)S(1)} collective-permute-done((f16[168,256]{1,0:T(8,128)(2,1)S(1)}, f16[168,256]{1,0:T(8,128)(2,1)S(1)}, u32[]{:S(2)}, u32[]{:S(2)}) %collective-permute-start.12) | collective-permute-done | bytes 86048 | tf_op jit(solution)/shard_map/ppermute | solution.py:24
  50.4 1.2 %collective-permute-start.20 = (f16[152,256]{1,0:T(8,128)(2,1)S(1)}, f16[152,256]{1,0:T(8,128)(2,1)S(1)}, u32[]{:S(2)}, u32[]{:S(2)}) collective-permute-start(f16[152,256]{1,0:T(8,128)(2,1)S(1)} %convert_element_type.182), channel_id=1, source_target_pairs={{0,8},{4,12},{8,0},{12,4},{16,24},{20,28},{24,16},{28,20},{1,9},{5... | collective-permute-start | bytes 233480 | tf_op jit(solution)/shard_map/ppermute | solution.py:24
  51.6 4.3 %collective-permute-start.18 = (f16[152,256]{1,0:T(8,128)(2,1)S(1)}, f16[152,256]{1,0:T(8,128)(2,1)S(1)}, u32[]{:S(2)}, u32[]{:S(2)}) collective-permute-start(f16[152,256]{1,0:T(8,128)(2,1)S(1)} %convert_element_type.182), channel_id=1, source_target_pairs={{0,16},{4,20},{8,24},{12,28},{16,0},{20,4},{24,8},{28,12},{1,17},{... | collective-permute-start | bytes 233480 | tf_op jit(solution)/shard_map/ppermute | solution.py:24
  55.9 2.6 %collective-permute-start.21 = (f16[4,152,256]{2,1,0:T(8,128)(2,1)S(1)}, f16[4,152,256]{2,1,0:T(8,128)(2,1)S(1)}, u32[]{:S(2)}, u32[]{:S(2)}) collective-permute-start(f16[4,152,256]{2,1,0:T(8,128)(2,1)S(1)} %pad_maximum_fusion), channel_id=1, source_target_pairs={{0,4},{4,0},{8,12},{12,8},{16,20},{20,16},{24,28},{28,24},{1,5},{5... | collective-permute-start | bytes 933896 | tf_op jit(solution)/shard_map/ppermute | solution.py:24
  59.1 3.0 %collective-permute-done.19 = f16[152,256]{1,0:T(8,128)(2,1)S(1)} collective-permute-done((f16[152,256]{1,0:T(8,128)(2,1)S(1)}, f16[152,256]{1,0:T(8,128)(2,1)S(1)}, u32[]{:S(2)}, u32[]{:S(2)}) %collective-permute-start.19) | collective-permute-done | bytes 77856 | tf_op jit(solution)/shard_map/ppermute | solution.py:24
  64.7 2.1 %input_terms.1 = bf16[2,128,768]{2,1,0:T(8,128)(2,1)S(1)} custom-call(bf16[1152,512]{1,0:T(8,128)(2,1)S(1)} %bitcast.112, f32[2,8,8,256]{3,2,1,0:T(8,128)S(1)} %pad_maximum_fusion.21.ends, bf16[2,128,768]{2,1,0:T(8,128)(2,1)S(1)} %bitcast.109, bf16[2,128,768]{2,1,0:T(8,128)(2,1)S(1)} %collective-permute-done.gb.refs_1_, ...), custom_call_target="tpu_custom_call" | custom-call | flops 1207959552 | bytes 3276800 | tf_op jit(solution)/shard_map/input_terms/pallas_call | solution.py:45
  68.3 1.5 %place_pieces.1 = f32[1152,512]{1,0:T(8,128)} custom-call(f32[576,256]{1,0:T(8,128)S(1)} %bitcast.98, f32[576,256]{1,0:T(8,128)S(1)} %bitcast.99, f32[288,256]{1,0:T(8,128)S(1)} %bitcast.102, f32[288,256]{1,0:T(8,128)S(1)} %bitcast.104, f32[288,256]{1,0:T(8,128)S(1)} %bitcast.101, f32[288,256]{1,0:T(8,128)S(1)} %bitcast.103), custom_call_target="tpu_custom_call" | custom-call | tf_op jit(solution)/shard_map/place_pieces/pallas_call | solution.py:509
  (103 shorter events, 14.8 us)
Async XLA Ops:
  1.7 5.6 %collective-permute-start = (bf16[2,128,768]{2,1,0:T(8,128)(2,1)S(1)}, bf16[2,128,768]{2,1,0:T(8,128)(2,1)S(1)}, u32[]{:S(2)}, u32[]{:S(2)}) collective-permute-start(bf16[2,128,768]{2,1,0:T(8,128)(2,1)S(1)} %bitcast.106), channel_id=1, source_target_pairs={{0,1},{1,0},{2,3},{3,2},{4,5},{5,4},{6,7},{7,6},{8,9},{9,8},{10,11... | collective-permute-start | bytes 1179656 | tf_op jit(solution)/shard_map/ppermute | solution.py:24
  2.2 12.3 %collective-permute-start.2 = (bf16[2,128,768]{2,1,0:T(8,128)(2,1)S(1)}, bf16[2,128,768]{2,1,0:T(8,128)(2,1)S(1)}, u32[]{:S(2)}, u32[]{:S(2)}) collective-permute-start(bf16[2,128,768]{2,1,0:T(8,128)(2,1)S(1)} %bitcast.107), channel_id=1, source_target_pairs={{0,2},{1,3},{2,0},{3,1},{4,6},{5,7},{6,4},{7,5},{8,10},{9,11},{10,... | collective-permute-start | bytes 1179656 | tf_op jit(solution)/shard_map/ppermute | solution.py:24
  8.6 9.3 %collective-permute-start.1 = (f16[592,256]{1,0:T(8,128)(2,1)S(1)}, f16[592,256]{1,0:T(8,128)(2,1)S(1)}, u32[]{:S(2)}, u32[]{:S(2)}) collective-permute-start(f16[592,256]{1,0:T(8,128)(2,1)S(1)} %convert_element_type.148), channel_id=1, source_target_pairs={{0,4},{4,0},{8,12},{12,8},{16,20},{20,16},{24,28},{28,24},{1,5},{5... | collective-permute-start | bytes 909320 | tf_op jit(solution)/shard_map/ppermute | solution.py:24
  10.1 0.8 %collective-permute-start.3 = (bf16[1,256]{1,0:T(2,128)(2,1)S(1)}, bf16[1,256]{1,0:T(2,128)(2,1)S(1)}, u32[]{:S(2)}, u32[]{:S(2)}) collective-permute-start(bf16[1,256]{1,0:T(2,128)(2,1)S(1)} %broadcast_select_fusion.15), channel_id=1, source_target_pairs={{4,8},{12,16},{20,24},{8,4},{16,12},{24,20},{5,9},{13,17},{21,25},... | collective-permute-start | bytes 1544 | tf_op jit(solution)/shard_map/ppermute | solution.py:408
  14.5 3.7 %collective-permute-start.4 = (bf16[2,128,768]{2,1,0:T(8,128)(2,1)S(1)}, bf16[2,128,768]{2,1,0:T(8,128)(2,1)S(1)}, u32[]{:S(2)}, u32[]{:S(2)}) collective-permute-start(bf16[2,128,768]{2,1,0:T(8,128)(2,1)S(1)} %collective-permute-done.2.ga.refs_2_), channel_id=1, source_target_pairs={{0,1},{1,0},{2,3},{3,2},{4,5},{5,4},{6,7},{7,6},{8,9},{9,8},{10,11... | collective-permute-start | bytes 1179656 | tf_op jit(solution)/shard_map/ppermute | solution.py:24
  19.4 10.3 %collective-permute-start.6 = (f16[592,256]{1,0:T(8,128)(2,1)S(1)}, f16[592,256]{1,0:T(8,128)(2,1)S(1)}, u32[]{:S(2)}, u32[]{:S(2)}) collective-permute-start(f16[592,256]{1,0:T(8,128)(2,1)S(1)} %convert_element_type.156), channel_id=1, source_target_pairs={{0,4},{4,0},{8,12},{12,8},{16,20},{20,16},{24,28},{28,24},{1,5},{5... | collective-permute-start | bytes 909320 | tf_op jit(solution)/shard_map/ppermute | solution.py:24
  20.9 8.7 %collective-permute-start.7 = (f16[168,256]{1,0:T(8,128)(2,1)S(1)}, f16[168,256]{1,0:T(8,128)(2,1)S(1)}, u32[]{:S(2)}, u32[]{:S(2)}) collective-permute-start(f16[168,256]{1,0:T(8,128)(2,1)S(1)} %get-tuple-element.76), channel_id=1, source_target_pairs={{0,8},{4,12},{8,0},{12,4},{16,24},{20,28},{24,16},{28,20},{1,9},{5... | collective-permute-start | bytes 258056 | tf_op jit(solution)/shard_map/ppermute | solution.py:24
  22.5 7.9 %collective-permute-start.8 = (f16[168,256]{1,0:T(8,128)(2,1)S(1)}, f16[168,256]{1,0:T(8,128)(2,1)S(1)}, u32[]{:S(2)}, u32[]{:S(2)}) collective-permute-start(f16[168,256]{1,0:T(8,128)(2,1)S(1)} %get-tuple-element.84), channel_id=1, source_target_pairs={{0,16},{4,20},{8,24},{12,28},{16,0},{20,4},{24,8},{28,12},{1,17},{... | collective-permute-start | bytes 258056 | tf_op jit(solution)/shard_map/ppermute | solution.py:24
  25.2 6.4 %collective-permute-start.9 = (f16[168,256]{1,0:T(8,128)(2,1)S(1)}, f16[168,256]{1,0:T(8,128)(2,1)S(1)}, u32[]{:S(2)}, u32[]{:S(2)}) collective-permute-start(f16[168,256]{1,0:T(8,128)(2,1)S(1)} %get-tuple-element.85), channel_id=1, source_target_pairs={{0,24},{4,28},{8,16},{12,20},{16,8},{20,12},{24,0},{28,4},{1,25},{... | collective-permute-start | bytes 258056 | tf_op jit(solution)/shard_map/ppermute | solution.py:24
  29.6 7.8 %collective-permute-start.5 = (f32[2,2,128,768]{3,2,1,0:T(8,128)S(1)}, f32[2,2,128,768]{3,2,1,0:T(8,128)S(1)}, u32[]{:S(2)}, u32[]{:S(2)}) collective-permute-start(f32[2,2,128,768]{3,2,1,0:T(8,128)S(1)} %get-tuple-element.81), channel_id=1, source_target_pairs={{0,1},{1,0},{2,3},{3,2},{4,5},{5,4},{6,7},{7,6},{8,9},{9,8},{10,11... | collective-permute-start | bytes 4718600 | tf_op jit(solution)/shard_map/ppermute | solution.py:24
  32.2 8.0 %collective-permute-start.14 = (f16[152,256]{1,0:T(8,128)(2,1)S(1)}, f16[152,256]{1,0:T(8,128)(2,1)S(1)}, u32[]{:S(2)}, u32[]{:S(2)}) collective-permute-start(f16[152,256]{1,0:T(8,128)(2,1)S(1)} %convert_element_type.173), channel_id=1, source_target_pairs={{0,8},{4,12},{8,0},{12,4},{16,24},{20,28},{24,16},{28,20},{1,9},{5... | collective-permute-start | bytes 233480 | tf_op jit(solution)/shard_map/ppermute | solution.py:24
  33.5 8.3 %collective-permute-start.15 = (f16[152,256]{1,0:T(8,128)(2,1)S(1)}, f16[152,256]{1,0:T(8,128)(2,1)S(1)}, u32[]{:S(2)}, u32[]{:S(2)}) collective-permute-start(f16[152,256]{1,0:T(8,128)(2,1)S(1)} %convert_element_type.173), channel_id=1, source_target_pairs={{0,16},{4,20},{8,24},{12,28},{16,0},{20,4},{24,8},{28,12},{1,17},{... | collective-permute-start | bytes 233480 | tf_op jit(solution)/shard_map/ppermute | solution.py:24
  35.1 7.3 %collective-permute-start.16 = (f16[152,256]{1,0:T(8,128)(2,1)S(1)}, f16[152,256]{1,0:T(8,128)(2,1)S(1)}, u32[]{:S(2)}, u32[]{:S(2)}) collective-permute-start(f16[152,256]{1,0:T(8,128)(2,1)S(1)} %convert_element_type.173), channel_id=1, source_target_pairs={{0,24},{4,28},{8,16},{12,20},{16,8},{20,12},{24,0},{28,4},{1,25},{... | collective-permute-start | bytes 233480 | tf_op jit(solution)/shard_map/ppermute | solution.py:24
  37.0 6.0 %collective-permute-start.11 = (f16[168,256]{1,0:T(8,128)(2,1)S(1)}, f16[168,256]{1,0:T(8,128)(2,1)S(1)}, u32[]{:S(2)}, u32[]{:S(2)}) collective-permute-start(f16[168,256]{1,0:T(8,128)(2,1)S(1)} %get-tuple-element.92), channel_id=1, source_target_pairs={{0,8},{4,12},{8,0},{12,4},{16,24},{20,28},{24,16},{28,20},{1,9},{5... | collective-permute-start | bytes 258056 | tf_op jit(solution)/shard_map/ppermute | solution.py:24
  37.4 11.3 %collective-permute-start.12 = (f16[168,256]{1,0:T(8,128)(2,1)S(1)}, f16[168,256]{1,0:T(8,128)(2,1)S(1)}, u32[]{:S(2)}, u32[]{:S(2)}) collective-permute-start(f16[168,256]{1,0:T(8,128)(2,1)S(1)} %get-tuple-element.95), channel_id=1, source_target_pairs={{0,16},{4,20},{8,24},{12,28},{16,0},{20,4},{24,8},{28,12},{1,17},{... | collective-permute-start | bytes 258056 | tf_op jit(solution)/shard_map/ppermute | solution.py:24
  40.2 8.5 %collective-permute-start.13 = (f16[168,256]{1,0:T(8,128)(2,1)S(1)}, f16[168,256]{1,0:T(8,128)(2,1)S(1)}, u32[]{:S(2)}, u32[]{:S(2)}) collective-permute-start(f16[168,256]{1,0:T(8,128)(2,1)S(1)} %get-tuple-element.96), channel_id=1, source_target_pairs={{0,24},{4,28},{8,16},{12,20},{16,8},{20,12},{24,0},{28,4},{1,25},{... | collective-permute-start | bytes 258056 | tf_op jit(solution)/shard_map/ppermute | solution.py:24
  41.9 8.5 %collective-permute-start.10 = (f32[128,768]{1,0:T(8,128)S(1)}, f32[128,768]{1,0:T(8,128)S(1)}, u32[]{:S(2)}, u32[]{:S(2)}) collective-permute-start(f32[128,768]{1,0:T(8,128)S(1)} %get-tuple-element.94), channel_id=1, source_target_pairs={{0,2},{1,3},{2,0},{3,1},{4,6},{5,7},{6,4},{7,5},{8,10},{9,11},{10,... | collective-permute-start | bytes 1179656 | tf_op jit(solution)/shard_map/ppermute | solution.py:24
  48.8 14.5 %collective-permute-start.17 = (f32[128,768]{1,0:T(8,128)S(1)}, f32[128,768]{1,0:T(8,128)S(1)}, u32[]{:S(2)}, u32[]{:S(2)}) collective-permute-start(f32[128,768]{1,0:T(8,128)S(1)} %get-tuple-element.97), channel_id=1, source_target_pairs={{0,2},{1,3},{2,0},{3,1},{4,6},{5,7},{6,4},{7,5},{8,10},{9,11},{10,... | collective-permute-start | bytes 1179656 | tf_op jit(solution)/shard_map/ppermute | solution.py:24
  50.4 8.2 %collective-permute-start.20 = (f16[152,256]{1,0:T(8,128)(2,1)S(1)}, f16[152,256]{1,0:T(8,128)(2,1)S(1)}, u32[]{:S(2)}, u32[]{:S(2)}) collective-permute-start(f16[152,256]{1,0:T(8,128)(2,1)S(1)} %convert_element_type.182), channel_id=1, source_target_pairs={{0,8},{4,12},{8,0},{12,4},{16,24},{20,28},{24,16},{28,20},{1,9},{5... | collective-permute-start | bytes 233480 | tf_op jit(solution)/shard_map/ppermute | solution.py:24
  51.6 7.5 %collective-permute-start.18 = (f16[152,256]{1,0:T(8,128)(2,1)S(1)}, f16[152,256]{1,0:T(8,128)(2,1)S(1)}, u32[]{:S(2)}, u32[]{:S(2)}) collective-permute-start(f16[152,256]{1,0:T(8,128)(2,1)S(1)} %convert_element_type.182), channel_id=1, source_target_pairs={{0,16},{4,20},{8,24},{12,28},{16,0},{20,4},{24,8},{28,12},{1,17},{... | collective-permute-start | bytes 233480 | tf_op jit(solution)/shard_map/ppermute | solution.py:24
  55.9 6.2 %collective-permute-start.19 = (f16[152,256]{1,0:T(8,128)(2,1)S(1)}, f16[152,256]{1,0:T(8,128)(2,1)S(1)}, u32[]{:S(2)}, u32[]{:S(2)}) collective-permute-start(f16[152,256]{1,0:T(8,128)(2,1)S(1)} %convert_element_type.182), channel_id=1, source_target_pairs={{0,24},{4,28},{8,16},{12,20},{16,8},{20,12},{24,0},{28,4},{1,25},{... | collective-permute-start | bytes 233480 | tf_op jit(solution)/shard_map/ppermute | solution.py:24
  55.9 10.8 %collective-permute-start.21 = (f16[4,152,256]{2,1,0:T(8,128)(2,1)S(1)}, f16[4,152,256]{2,1,0:T(8,128)(2,1)S(1)}, u32[]{:S(2)}, u32[]{:S(2)}) collective-permute-start(f16[4,152,256]{2,1,0:T(8,128)(2,1)S(1)} %pad_maximum_fusion), channel_id=1, source_target_pairs={{0,4},{4,0},{8,12},{12,8},{16,20},{20,16},{24,28},{28,24},{1,5},{5... | collective-permute-start | bytes 933896 | tf_op jit(solution)/shard_map/ppermute | solution.py:24
  58.7 9.3 %collective-permute-start.22 = (f16[2,152,256]{2,1,0:T(8,128)(2,1)S(1)}, f16[2,152,256]{2,1,0:T(8,128)(2,1)S(1)}, u32[]{:S(2)}, u32[]{:S(2)}) collective-permute-start(f16[2,152,256]{2,1,0:T(8,128)(2,1)S(1)} %pad_maximum_fusion.1), channel_id=1, source_target_pairs={{0,4},{4,0},{8,12},{12,8},{16,20},{20,16},{24,28},{28,24},{1,5},{5... | collective-permute-start | bytes 466952 | tf_op jit(solution)/shard_map/ppermute | solution.py:24
  62.2 5.9 %collective-permute-start.23 = (f16[2,152,256]{2,1,0:T(8,128)(2,1)S(1)}, f16[2,152,256]{2,1,0:T(8,128)(2,1)S(1)}, u32[]{:S(2)}, u32[]{:S(2)}) collective-permute-start(f16[2,152,256]{2,1,0:T(8,128)(2,1)S(1)} %pad_maximum_fusion.2), channel_id=1, source_target_pairs={{0,4},{4,0},{8,12},{12,8},{16,20},{20,16},{24,28},{28,24},{1,5},{5... | collective-permute-start | bytes 466952 | tf_op jit(solution)/shard_map/ppermute | solution.py:24
  (3 other events, 17.6 us)

commit v5 on v4

--- a/solution.py
+++ b/solution.py
@@ -339,7 +339,7 @@
 
 FIRST = (0.0, 1.9, 2.0, 3.9, 4.0, 5.9, 6.0, 7.9)
 LATER = (1.95, 3.85, 4.05, 5.95, 6.05, 6.5, 6.6, 6.7, 9.9, 10.0)
-FORWARD = (0.1, 0.2, 2.7, 4.2, 5.98, 6.75)
+FORWARD = (0.1, 0.2, 2.7, 4.03, 5.94, 6.45)
 BACKWARD = (6.72, 9.6)
 PARTNERS = 0.3
 AFTER = 2.0

time: 70.2 us -> 70 us (level)
  starting transfers between devices: 31 us -> 30 us
  waiting for transfers between devices: 18.9 us -> 19.8 us
    ppermute x23, starting transfers between devices: 30.2 us -> 29.2 us  [exchange(): return lax.ppermute(value, axis, [(i, i ^ bit) for i in range(devices)])]
    ppermute x23, waiting for transfers between devices: 18.9 us -> 19.8 us  [exchange(): return lax.ppermute(value, axis, [(i, i ^ bit) for i in range(devices)])]
  transfers between devices with their start and end apart: 24 -> 24, of which waited for: 10 -> 12; matrix products, arithmetic and copies ran while one was open for 6% -> 6% of each run, Pallas kernels for 14% -> 14%
where the time goes in v5:
time: 70 us; the launch traced here: 69.8 us
  starting transfers between devices  30 us (43%)
  waiting for transfers between devices  19.8 us (28%)
  Pallas kernels  12.5 us (18%)
  local copies, waits for them, and re-layouts  4.43 us (6%)
  other arithmetic  1.8 us (3%)
  between operations  1.27 us (2%)
    ppermute x23, starting transfers between devices, exchange(): return lax.ppermute(value, axis, [(i, i ^ bit) for i in range(devices)])  29.2 us
    ppermute x23, waiting for transfers between devices, exchange(): return lax.ppermute(value, axis, [(i, i ^ bit) for i in range(devices)])  19.8 us
    pallas_call x8, Pallas kernels, call(): pl.pallas_call(body, out_shape=outs, in_specs=[VMEM] * len(args), out_spe...  10.9 us
    unnamed x14, local copies, waits for them, and re-layouts  3.33 us
    pallas_call x1, Pallas kernels, body(): pl.pallas_call(functools.partial(place_kernel, piece, layout), out_shape=...  1.55 us
  transfers between devices with their start and end apart: 24, of which 12 were waited for; matrix products, arithmetic and copies ran while one was open for 6% of the time, Pallas kernels for 14%

profile of v5, /device:TPU:0, one launch (start us, length us, event | category | flops | bytes accessed | tf_op | source)
XLA Modules:
  0.0 69.8 jit_solution(16272658125465127131)
XLA Ops:
  2.2 2.6 %collective-permute-start.2 = (bf16[2,128,768]{2,1,0:T(8,128)(2,1)S(1)}, bf16[2,128,768]{2,1,0:T(8,128)(2,1)S(1)}, u32[]{:S(2)}, u32[]{:S(2)}) collective-permute-start(bf16[2,128,768]{2,1,0:T(8,128)(2,1)S(1)} %bitcast.107), channel_id=1, source_target_pairs={{0,2},{1,3},{2,0},{3,1},{4,6},{5,7},{6,4},{7,5},{8,10},{9,11},{10,... | collective-permute-start | bytes 1179656 | tf_op jit(solution)/shard_map/ppermute | solution.py:24
  5.8 1.5 %shifted_taps.2 = (bf16[2,384,768]{2,1,0:T(8,128)(2,1)S(1)}, bf16[2,256]{1,0:T(2,128)(2,1)S(1)}) custom-call(bf16[128,2,768]{2,1,0:T(2,128)(2,1)S(1)} %copy-done), custom_call_target="tpu_custom_call" | custom-call | bytes 1573888 | tf_op jit(solution)/shard_map/shifted_taps/pallas_call | solution.py:45
  8.6 1.6 %collective-permute-start.1 = (f16[592,256]{1,0:T(8,128)(2,1)S(1)}, f16[592,256]{1,0:T(8,128)(2,1)S(1)}, u32[]{:S(2)}, u32[]{:S(2)}) collective-permute-start(f16[592,256]{1,0:T(8,128)(2,1)S(1)} %convert_element_type.148), channel_id=1, source_target_pairs={{0,4},{4,0},{8,12},{12,8},{16,20},{20,16},{24,28},{28,24},{1,5},{5... | collective-permute-start | bytes 909320 | tf_op jit(solution)/shard_map/ppermute | solution.py:24
  11.0 3.5 %collective-permute-done.2.ga.refs_2_ = bf16[2,128,768]{2,1,0:T(8,128)(2,1)S(1)} collective-permute-done((bf16[2,128,768]{2,1,0:T(8,128)(2,1)S(1)}, bf16[2,128,768]{2,1,0:T(8,128)(2,1)S(1)}, u32[]{:S(2)}, u32[]{:S(2)}) %collective-permute-start.2) | collective-permute-done | bytes 393248 | tf_op jit(solution)/shard_map/ppermute | solution.py:24
  14.5 3.4 %collective-permute-done.1 = f16[592,256]{1,0:T(8,128)(2,1)S(1)} collective-permute-done((f16[592,256]{1,0:T(8,128)(2,1)S(1)}, f16[592,256]{1,0:T(8,128)(2,1)S(1)}, u32[]{:S(2)}, u32[]{:S(2)}) %collective-permute-start.1) | collective-permute-done | bytes 303136 | tf_op jit(solution)/shard_map/ppermute | solution.py:24
  19.4 1.6 %collective-permute-start.9 = (f16[592,256]{1,0:T(8,128)(2,1)S(1)}, f16[592,256]{1,0:T(8,128)(2,1)S(1)}, u32[]{:S(2)}, u32[]{:S(2)}) collective-permute-start(f16[592,256]{1,0:T(8,128)(2,1)S(1)} %convert_element_type.156), channel_id=1, source_target_pairs={{0,4},{4,0},{8,12},{12,8},{16,20},{20,16},{24,28},{28,24},{1,5},{5... | collective-permute-start | bytes 909320 | tf_op jit(solution)/shard_map/ppermute | solution.py:24
  20.9 1.6 %collective-permute-start.6 = (f16[168,256]{1,0:T(8,128)(2,1)S(1)}, f16[168,256]{1,0:T(8,128)(2,1)S(1)}, u32[]{:S(2)}, u32[]{:S(2)}) collective-permute-start(f16[168,256]{1,0:T(8,128)(2,1)S(1)} %get-tuple-element.76), channel_id=1, source_target_pairs={{0,8},{4,12},{8,0},{12,4},{16,24},{20,28},{24,16},{28,20},{1,9},{5... | collective-permute-start | bytes 258056 | tf_op jit(solution)/shard_map/ppermute | solution.py:24
  22.5 2.6 %collective-permute-start.7 = (f16[168,256]{1,0:T(8,128)(2,1)S(1)}, f16[168,256]{1,0:T(8,128)(2,1)S(1)}, u32[]{:S(2)}, u32[]{:S(2)}) collective-permute-start(f16[168,256]{1,0:T(8,128)(2,1)S(1)} %get-tuple-element.82), channel_id=1, source_target_pairs={{0,16},{4,20},{8,24},{12,28},{16,0},{20,4},{24,8},{28,12},{1,17},{... | collective-permute-start | bytes 258056 | tf_op jit(solution)/shard_map/ppermute | solution.py:24
  25.4 2.1 %shifted_taps.3 = (bf16[2,384,768]{2,1,0:T(8,128)(2,1)S(1)}, bf16[2,256]{1,0:T(2,128)(2,1)}) custom-call(bf16[128,2,768]{2,1,0:T(2,128)(2,1)S(1)} %copy-done.1, bf16[1,256]{1,0:T(2,128)(2,1)S(1)} %broadcast_select_fusion.13.refs_0_, bf16[1,256]{1,0:T(2,128)(2,1)S(1)} %get-tuple-element.126.refs_1_), custom_call_target="tpu_custom_call" | custom-call | bytes 1574912 | tf_op jit(solution)/shard_map/shifted_taps/pallas_call | solution.py:45
  27.5 2.0 %forward_terms.1 = (f32[2,2,128,768]{3,2,1,0:T(8,128)S(1)}, f32[2,2,128,768]{3,2,1,0:T(8,128)S(1)}) custom-call(bf16[2,384,768]{2,1,0:T(8,128)(2,1)S(1)} %get-tuple-element.78.xs, bf16[3,384,512]{2,1,0:T(8,128)(2,1)S(1)} %bitcast.111), custom_call_target="tpu_custom_call" | custom-call | flops 1207959552 | bytes 5505024 | tf_op jit(solution)/shard_map/forward_terms/pallas_call | solution.py:45
  32.2 1.3 %collective-permute-start.11 = (f16[152,256]{1,0:T(8,128)(2,1)S(1)}, f16[152,256]{1,0:T(8,128)(2,1)S(1)}, u32[]{:S(2)}, u32[]{:S(2)}) collective-permute-start(f16[152,256]{1,0:T(8,128)(2,1)S(1)} %convert_element_type.166), channel_id=1, source_target_pairs={{0,8},{4,12},{8,0},{12,4},{16,24},{20,28},{24,16},{28,20},{1,9},{5... | collective-permute-start | bytes 233480 | tf_op jit(solution)/shard_map/ppermute | solution.py:24
  33.5 1.6 %collective-permute-start.12 = (f16[152,256]{1,0:T(8,128)(2,1)S(1)}, f16[152,256]{1,0:T(8,128)(2,1)S(1)}, u32[]{:S(2)}, u32[]{:S(2)}) collective-permute-start(f16[152,256]{1,0:T(8,128)(2,1)S(1)} %convert_element_type.166), channel_id=1, source_target_pairs={{0,16},{4,20},{8,24},{12,28},{16,0},{20,4},{24,8},{28,12},{1,17},{... | collective-permute-start | bytes 233480 | tf_op jit(solution)/shard_map/ppermute | solution.py:24
  35.1 1.6 %collective-permute-start.13 = (f16[152,256]{1,0:T(8,128)(2,1)S(1)}, f16[152,256]{1,0:T(8,128)(2,1)S(1)}, u32[]{:S(2)}, u32[]{:S(2)}) collective-permute-start(f16[152,256]{1,0:T(8,128)(2,1)S(1)} %convert_element_type.166), channel_id=1, source_target_pairs={{0,24},{4,28},{8,16},{12,20},{16,8},{20,12},{24,0},{28,4},{1,25},{... | collective-permute-start | bytes 233480 | tf_op jit(solution)/shard_map/ppermute | solution.py:24
  37.9 1.6 %collective-permute-start.14 = (f32[128,768]{1,0:T(8,128)S(1)}, f32[128,768]{1,0:T(8,128)S(1)}, u32[]{:S(2)}, u32[]{:S(2)}) collective-permute-start(f32[128,768]{1,0:T(8,128)S(1)} %get-tuple-element.94), channel_id=1, source_target_pairs={{0,2},{1,3},{2,0},{3,1},{4,6},{5,7},{6,4},{7,5},{8,10},{9,11},{10,... | collective-permute-start | bytes 1179656 | tf_op jit(solution)/shard_map/ppermute | solution.py:24
  39.9 1.6 %collective-permute-done.12 = f16[152,256]{1,0:T(8,128)(2,1)S(1)} collective-permute-done((f16[152,256]{1,0:T(8,128)(2,1)S(1)}, f16[152,256]{1,0:T(8,128)(2,1)S(1)}, u32[]{:S(2)}, u32[]{:S(2)}) %collective-permute-start.12) | collective-permute-done | bytes 77856 | tf_op jit(solution)/shard_map/ppermute | solution.py:24
  41.6 2.3 %collective-permute-start.16 = (f16[168,256]{1,0:T(8,128)(2,1)S(1)}, f16[168,256]{1,0:T(8,128)(2,1)S(1)}, u32[]{:S(2)}, u32[]{:S(2)}) collective-permute-start(f16[168,256]{1,0:T(8,128)(2,1)S(1)} %get-tuple-element.98), channel_id=1, source_target_pairs={{0,16},{4,20},{8,24},{12,28},{16,0},{20,4},{24,8},{28,12},{1,17},{... | collective-permute-start | bytes 258056 | tf_op jit(solution)/shard_map/ppermute | solution.py:24
  43.8 1.4 %collective-permute-start.17 = (f16[168,256]{1,0:T(8,128)(2,1)S(1)}, f16[168,256]{1,0:T(8,128)(2,1)S(1)}, u32[]{:S(2)}, u32[]{:S(2)}) collective-permute-start(f16[168,256]{1,0:T(8,128)(2,1)S(1)} %get-tuple-element.99), channel_id=1, source_target_pairs={{0,24},{4,28},{8,16},{12,20},{16,8},{20,12},{24,0},{28,4},{1,25},{... | collective-permute-start | bytes 258056 | tf_op jit(solution)/shard_map/ppermute | solution.py:24
  45.4 3.9 %collective-permute-done.10 = f32[128,768]{1,0:T(8,128)S(1)} collective-permute-done((f32[128,768]{1,0:T(8,128)S(1)}, f32[128,768]{1,0:T(8,128)S(1)}, u32[]{:S(2)}, u32[]{:S(2)}) %collective-permute-start.10) | collective-permute-done | bytes 393248 | tf_op jit(solution)/shard_map/ppermute | solution.py:24
  53.1 2.3 %collective-permute-start.19 = (f16[152,256]{1,0:T(8,128)(2,1)S(1)}, f16[152,256]{1,0:T(8,128)(2,1)S(1)}, u32[]{:S(2)}, u32[]{:S(2)}) collective-permute-start(f16[152,256]{1,0:T(8,128)(2,1)S(1)} %convert_element_type.182), channel_id=1, source_target_pairs={{0,24},{4,28},{8,16},{12,20},{16,8},{20,12},{24,0},{28,4},{1,25},{... | collective-permute-start | bytes 233480 | tf_op jit(solution)/shard_map/ppermute | solution.py:24
  59.4 1.2 %collective-permute-start.23 = (f16[2,152,256]{2,1,0:T(8,128)(2,1)S(1)}, f16[2,152,256]{2,1,0:T(8,128)(2,1)S(1)}, u32[]{:S(2)}, u32[]{:S(2)}) collective-permute-start(f16[2,152,256]{2,1,0:T(8,128)(2,1)S(1)} %pad_maximum_fusion.2), channel_id=1, source_target_pairs={{0,4},{4,0},{8,12},{12,8},{16,20},{20,16},{24,28},{28,24},{1,5},{5... | collective-permute-start | bytes 466952 | tf_op jit(solution)/shard_map/ppermute | solution.py:24
  60.8 2.1 %input_terms.1 = bf16[2,128,768]{2,1,0:T(8,128)(2,1)S(1)} custom-call(bf16[1152,512]{1,0:T(8,128)(2,1)S(1)} %bitcast.112, f32[2,8,8,256]{3,2,1,0:T(8,128)S(1)} %pad_maximum_fusion.21.ends, bf16[2,128,768]{2,1,0:T(8,128)(2,1)S(1)} %bitcast.109, bf16[2,128,768]{2,1,0:T(8,128)(2,1)S(1)} %collective-permute-done.gb.refs_1_, ...), custom_call_target="tpu_custom_call" | custom-call | flops 1207959552 | bytes 3276800 | tf_op jit(solution)/shard_map/input_terms/pallas_call | solution.py:45
  62.8 1.7 %collective-permute-done.21 = f16[4,152,256]{2,1,0:T(8,128)(2,1)S(1)} collective-permute-done((f16[4,152,256]{2,1,0:T(8,128)(2,1)S(1)}, f16[4,152,256]{2,1,0:T(8,128)(2,1)S(1)}, u32[]{:S(2)}, u32[]{:S(2)}) %collective-permute-start.21) | collective-permute-done | bytes 311328 | tf_op jit(solution)/shard_map/ppermute | solution.py:24
  66.3 1.7 %collective-permute-done.23 = f16[2,152,256]{2,1,0:T(8,128)(2,1)S(1)} collective-permute-done((f16[2,152,256]{2,1,0:T(8,128)(2,1)S(1)}, f16[2,152,256]{2,1,0:T(8,128)(2,1)S(1)}, u32[]{:S(2)}, u32[]{:S(2)}) %collective-permute-start.23) | collective-permute-done | bytes 155680 | tf_op jit(solution)/shard_map/ppermute | solution.py:24
  68.1 1.5 %place_pieces.1 = f32[1152,512]{1,0:T(8,128)} custom-call(f32[576,256]{1,0:T(8,128)S(1)} %bitcast.98, f32[576,256]{1,0:T(8,128)S(1)} %bitcast.99, f32[288,256]{1,0:T(8,128)S(1)} %bitcast.102, f32[288,256]{1,0:T(8,128)S(1)} %bitcast.104, f32[288,256]{1,0:T(8,128)S(1)} %bitcast.101, f32[288,256]{1,0:T(8,128)S(1)} %bitcast.103), custom_call_target="tpu_custom_call" | custom-call | tf_op jit(solution)/shard_map/place_pieces/pallas_call | solution.py:509
  (103 shorter events, 20.3 us)
Async XLA Ops:
  1.7 5.6 %collective-permute-start = (bf16[2,128,768]{2,1,0:T(8,128)(2,1)S(1)}, bf16[2,128,768]{2,1,0:T(8,128)(2,1)S(1)}, u32[]{:S(2)}, u32[]{:S(2)}) collective-permute-start(bf16[2,128,768]{2,1,0:T(8,128)(2,1)S(1)} %bitcast.106), channel_id=1, source_target_pairs={{0,1},{1,0},{2,3},{3,2},{4,5},{5,4},{6,7},{7,6},{8,9},{9,8},{10,11... | collective-permute-start | bytes 1179656 | tf_op jit(solution)/shard_map/ppermute | solution.py:24
  2.2 12.3 %collective-permute-start.2 = (bf16[2,128,768]{2,1,0:T(8,128)(2,1)S(1)}, bf16[2,128,768]{2,1,0:T(8,128)(2,1)S(1)}, u32[]{:S(2)}, u32[]{:S(2)}) collective-permute-start(bf16[2,128,768]{2,1,0:T(8,128)(2,1)S(1)} %bitcast.107), channel_id=1, source_target_pairs={{0,2},{1,3},{2,0},{3,1},{4,6},{5,7},{6,4},{7,5},{8,10},{9,11},{10,... | collective-permute-start | bytes 1179656 | tf_op jit(solution)/shard_map/ppermute | solution.py:24
  8.6 9.3 %collective-permute-start.1 = (f16[592,256]{1,0:T(8,128)(2,1)S(1)}, f16[592,256]{1,0:T(8,128)(2,1)S(1)}, u32[]{:S(2)}, u32[]{:S(2)}) collective-permute-start(f16[592,256]{1,0:T(8,128)(2,1)S(1)} %convert_element_type.148), channel_id=1, source_target_pairs={{0,4},{4,0},{8,12},{12,8},{16,20},{20,16},{24,28},{28,24},{1,5},{5... | collective-permute-start | bytes 909320 | tf_op jit(solution)/shard_map/ppermute | solution.py:24
  10.1 0.8 %collective-permute-start.3 = (bf16[1,256]{1,0:T(2,128)(2,1)S(1)}, bf16[1,256]{1,0:T(2,128)(2,1)S(1)}, u32[]{:S(2)}, u32[]{:S(2)}) collective-permute-start(bf16[1,256]{1,0:T(2,128)(2,1)S(1)} %broadcast_select_fusion.15), channel_id=1, source_target_pairs={{4,8},{12,16},{20,24},{8,4},{16,12},{24,20},{5,9},{13,17},{21,25},... | collective-permute-start | bytes 1544 | tf_op jit(solution)/shard_map/ppermute | solution.py:408
  14.5 3.7 %collective-permute-start.4 = (bf16[2,128,768]{2,1,0:T(8,128)(2,1)S(1)}, bf16[2,128,768]{2,1,0:T(8,128)(2,1)S(1)}, u32[]{:S(2)}, u32[]{:S(2)}) collective-permute-start(bf16[2,128,768]{2,1,0:T(8,128)(2,1)S(1)} %collective-permute-done.2.ga.refs_2_), channel_id=1, source_target_pairs={{0,1},{1,0},{2,3},{3,2},{4,5},{5,4},{6,7},{7,6},{8,9},{9,8},{10,11... | collective-permute-start | bytes 1179656 | tf_op jit(solution)/shard_map/ppermute | solution.py:24
  19.4 10.3 %collective-permute-start.9 = (f16[592,256]{1,0:T(8,128)(2,1)S(1)}, f16[592,256]{1,0:T(8,128)(2,1)S(1)}, u32[]{:S(2)}, u32[]{:S(2)}) collective-permute-start(f16[592,256]{1,0:T(8,128)(2,1)S(1)} %convert_element_type.156), channel_id=1, source_target_pairs={{0,4},{4,0},{8,12},{12,8},{16,20},{20,16},{24,28},{28,24},{1,5},{5... | collective-permute-start | bytes 909320 | tf_op jit(solution)/shard_map/ppermute | solution.py:24
  20.9 8.7 %collective-permute-start.6 = (f16[168,256]{1,0:T(8,128)(2,1)S(1)}, f16[168,256]{1,0:T(8,128)(2,1)S(1)}, u32[]{:S(2)}, u32[]{:S(2)}) collective-permute-start(f16[168,256]{1,0:T(8,128)(2,1)S(1)} %get-tuple-element.76), channel_id=1, source_target_pairs={{0,8},{4,12},{8,0},{12,4},{16,24},{20,28},{24,16},{28,20},{1,9},{5... | collective-permute-start | bytes 258056 | tf_op jit(solution)/shard_map/ppermute | solution.py:24
  22.5 7.9 %collective-permute-start.7 = (f16[168,256]{1,0:T(8,128)(2,1)S(1)}, f16[168,256]{1,0:T(8,128)(2,1)S(1)}, u32[]{:S(2)}, u32[]{:S(2)}) collective-permute-start(f16[168,256]{1,0:T(8,128)(2,1)S(1)} %get-tuple-element.82), channel_id=1, source_target_pairs={{0,16},{4,20},{8,24},{12,28},{16,0},{20,4},{24,8},{28,12},{1,17},{... | collective-permute-start | bytes 258056 | tf_op jit(solution)/shard_map/ppermute | solution.py:24
  25.2 6.4 %collective-permute-start.8 = (f16[168,256]{1,0:T(8,128)(2,1)S(1)}, f16[168,256]{1,0:T(8,128)(2,1)S(1)}, u32[]{:S(2)}, u32[]{:S(2)}) collective-permute-start(f16[168,256]{1,0:T(8,128)(2,1)S(1)} %get-tuple-element.83), channel_id=1, source_target_pairs={{0,24},{4,28},{8,16},{12,20},{16,8},{20,12},{24,0},{28,4},{1,25},{... | collective-permute-start | bytes 258056 | tf_op jit(solution)/shard_map/ppermute | solution.py:24
  29.6 7.3 %collective-permute-start.5 = (f32[2,2,128,768]{3,2,1,0:T(8,128)S(1)}, f32[2,2,128,768]{3,2,1,0:T(8,128)S(1)}, u32[]{:S(2)}, u32[]{:S(2)}) collective-permute-start(f32[2,2,128,768]{3,2,1,0:T(8,128)S(1)} %get-tuple-element.81), channel_id=1, source_target_pairs={{0,1},{1,0},{2,3},{3,2},{4,5},{5,4},{6,7},{7,6},{8,9},{9,8},{10,11... | collective-permute-start | bytes 4718600 | tf_op jit(solution)/shard_map/ppermute | solution.py:24
  32.2 7.3 %collective-permute-start.11 = (f16[152,256]{1,0:T(8,128)(2,1)S(1)}, f16[152,256]{1,0:T(8,128)(2,1)S(1)}, u32[]{:S(2)}, u32[]{:S(2)}) collective-permute-start(f16[152,256]{1,0:T(8,128)(2,1)S(1)} %convert_element_type.166), channel_id=1, source_target_pairs={{0,8},{4,12},{8,0},{12,4},{16,24},{20,28},{24,16},{28,20},{1,9},{5... | collective-permute-start | bytes 233480 | tf_op jit(solution)/shard_map/ppermute | solution.py:24
  33.5 7.9 %collective-permute-start.12 = (f16[152,256]{1,0:T(8,128)(2,1)S(1)}, f16[152,256]{1,0:T(8,128)(2,1)S(1)}, u32[]{:S(2)}, u32[]{:S(2)}) collective-permute-start(f16[152,256]{1,0:T(8,128)(2,1)S(1)} %convert_element_type.166), channel_id=1, source_target_pairs={{0,16},{4,20},{8,24},{12,28},{16,0},{20,4},{24,8},{28,12},{1,17},{... | collective-permute-start | bytes 233480 | tf_op jit(solution)/shard_map/ppermute | solution.py:24
  35.1 6.4 %collective-permute-start.13 = (f16[152,256]{1,0:T(8,128)(2,1)S(1)}, f16[152,256]{1,0:T(8,128)(2,1)S(1)}, u32[]{:S(2)}, u32[]{:S(2)}) collective-permute-start(f16[152,256]{1,0:T(8,128)(2,1)S(1)} %convert_element_type.166), channel_id=1, source_target_pairs={{0,24},{4,28},{8,16},{12,20},{16,8},{20,12},{24,0},{28,4},{1,25},{... | collective-permute-start | bytes 233480 | tf_op jit(solution)/shard_map/ppermute | solution.py:24
  37.2 12.1 %collective-permute-start.10 = (f32[128,768]{1,0:T(8,128)S(1)}, f32[128,768]{1,0:T(8,128)S(1)}, u32[]{:S(2)}, u32[]{:S(2)}) collective-permute-start(f32[128,768]{1,0:T(8,128)S(1)} %get-tuple-element.92), channel_id=1, source_target_pairs={{0,2},{1,3},{2,0},{3,1},{4,6},{5,7},{6,4},{7,5},{8,10},{9,11},{10,... | collective-permute-start | bytes 1179656 | tf_op jit(solution)/shard_map/ppermute | solution.py:24
  37.9 18.6 %collective-permute-start.14 = (f32[128,768]{1,0:T(8,128)S(1)}, f32[128,768]{1,0:T(8,128)S(1)}, u32[]{:S(2)}, u32[]{:S(2)}) collective-permute-start(f32[128,768]{1,0:T(8,128)S(1)} %get-tuple-element.94), channel_id=1, source_target_pairs={{0,2},{1,3},{2,0},{3,1},{4,6},{5,7},{6,4},{7,5},{8,10},{9,11},{10,... | collective-permute-start | bytes 1179656 | tf_op jit(solution)/shard_map/ppermute | solution.py:24
  39.5 9.8 %collective-permute-start.15 = (f16[168,256]{1,0:T(8,128)(2,1)S(1)}, f16[168,256]{1,0:T(8,128)(2,1)S(1)}, u32[]{:S(2)}, u32[]{:S(2)}) collective-permute-start(f16[168,256]{1,0:T(8,128)(2,1)S(1)} %get-tuple-element.95), channel_id=1, source_target_pairs={{0,8},{4,12},{8,0},{12,4},{16,24},{20,28},{24,16},{28,20},{1,9},{5... | collective-permute-start | bytes 258056 | tf_op jit(solution)/shard_map/ppermute | solution.py:24
  41.6 7.8 %collective-permute-start.16 = (f16[168,256]{1,0:T(8,128)(2,1)S(1)}, f16[168,256]{1,0:T(8,128)(2,1)S(1)}, u32[]{:S(2)}, u32[]{:S(2)}) collective-permute-start(f16[168,256]{1,0:T(8,128)(2,1)S(1)} %get-tuple-element.98), channel_id=1, source_target_pairs={{0,16},{4,20},{8,24},{12,28},{16,0},{20,4},{24,8},{28,12},{1,17},{... | collective-permute-start | bytes 258056 | tf_op jit(solution)/shard_map/ppermute | solution.py:24
  43.8 6.4 %collective-permute-start.17 = (f16[168,256]{1,0:T(8,128)(2,1)S(1)}, f16[168,256]{1,0:T(8,128)(2,1)S(1)}, u32[]{:S(2)}, u32[]{:S(2)}) collective-permute-start(f16[168,256]{1,0:T(8,128)(2,1)S(1)} %get-tuple-element.99), channel_id=1, source_target_pairs={{0,24},{4,28},{8,16},{12,20},{16,8},{20,12},{24,0},{28,4},{1,25},{... | collective-permute-start | bytes 258056 | tf_op jit(solution)/shard_map/ppermute | solution.py:24
  50.9 7.0 %collective-permute-start.20 = (f16[152,256]{1,0:T(8,128)(2,1)S(1)}, f16[152,256]{1,0:T(8,128)(2,1)S(1)}, u32[]{:S(2)}, u32[]{:S(2)}) collective-permute-start(f16[152,256]{1,0:T(8,128)(2,1)S(1)} %convert_element_type.182), channel_id=1, source_target_pairs={{0,8},{4,12},{8,0},{12,4},{16,24},{20,28},{24,16},{28,20},{1,9},{5... | collective-permute-start | bytes 233480 | tf_op jit(solution)/shard_map/ppermute | solution.py:24
  51.9 7.0 %collective-permute-start.18 = (f16[152,256]{1,0:T(8,128)(2,1)S(1)}, f16[152,256]{1,0:T(8,128)(2,1)S(1)}, u32[]{:S(2)}, u32[]{:S(2)}) collective-permute-start(f16[152,256]{1,0:T(8,128)(2,1)S(1)} %convert_element_type.182), channel_id=1, source_target_pairs={{0,16},{4,20},{8,24},{12,28},{16,0},{20,4},{24,8},{28,12},{1,17},{... | collective-permute-start | bytes 233480 | tf_op jit(solution)/shard_map/ppermute | solution.py:24
  53.1 6.3 %collective-permute-start.19 = (f16[152,256]{1,0:T(8,128)(2,1)S(1)}, f16[152,256]{1,0:T(8,128)(2,1)S(1)}, u32[]{:S(2)}, u32[]{:S(2)}) collective-permute-start(f16[152,256]{1,0:T(8,128)(2,1)S(1)} %convert_element_type.182), channel_id=1, source_target_pairs={{0,24},{4,28},{8,16},{12,20},{16,8},{20,12},{24,0},{28,4},{1,25},{... | collective-permute-start | bytes 233480 | tf_op jit(solution)/shard_map/ppermute | solution.py:24
  55.3 9.2 %collective-permute-start.21 = (f16[4,152,256]{2,1,0:T(8,128)(2,1)S(1)}, f16[4,152,256]{2,1,0:T(8,128)(2,1)S(1)}, u32[]{:S(2)}, u32[]{:S(2)}) collective-permute-start(f16[4,152,256]{2,1,0:T(8,128)(2,1)S(1)} %pad_maximum_fusion), channel_id=1, source_target_pairs={{0,4},{4,0},{8,12},{12,8},{16,20},{20,16},{24,28},{28,24},{1,5},{5... | collective-permute-start | bytes 933896 | tf_op jit(solution)/shard_map/ppermute | solution.py:24
  57.9 8.3 %collective-permute-start.22 = (f16[2,152,256]{2,1,0:T(8,128)(2,1)S(1)}, f16[2,152,256]{2,1,0:T(8,128)(2,1)S(1)}, u32[]{:S(2)}, u32[]{:S(2)}) collective-permute-start(f16[2,152,256]{2,1,0:T(8,128)(2,1)S(1)} %pad_maximum_fusion.1), channel_id=1, source_target_pairs={{0,4},{4,0},{8,12},{12,8},{16,20},{20,16},{24,28},{28,24},{1,5},{5... | collective-permute-start | bytes 466952 | tf_op jit(solution)/shard_map/ppermute | solution.py:24
  59.4 8.5 %collective-permute-start.23 = (f16[2,152,256]{2,1,0:T(8,128)(2,1)S(1)}, f16[2,152,256]{2,1,0:T(8,128)(2,1)S(1)}, u32[]{:S(2)}, u32[]{:S(2)}) collective-permute-start(f16[2,152,256]{2,1,0:T(8,128)(2,1)S(1)} %pad_maximum_fusion.2), channel_id=1, source_target_pairs={{0,4},{4,0},{8,12},{12,8},{16,20},{20,16},{24,28},{28,24},{1,5},{5... | collective-permute-start | bytes 466952 | tf_op jit(solution)/shard_map/ppermute | solution.py:24
  (3 other events, 17.6 us)

commit v6 on v5

--- a/solution.py
+++ b/solution.py
@@ -170,14 +170,14 @@
 def place_kernel(piece, layout, *refs):
     *parts, out, sems = refs
     tile, me = lax.axis_index("width"), lax.axis_index("chan") >> 1
-    half = lax.axis_size("width") // 2
+    tiles = lax.axis_size("width")
     lanes = parts[0].shape[1]
     copies = []
-    for part, (chunk, other, first) in zip(parts, layout):
+    for part, (chunk, owners) in zip(parts, layout):
         col = pl.multiple_of((me ^ chunk) * lanes, LANES)
-        for n in range(part.shape[0] // piece):
-            row = ((tile & 1) ^ other) * half + ((tile >> 1) ^ (first + n))
-            place = out.at[pl.ds(pl.multiple_of(row * piece, 16), piece), pl.ds(col, lanes)]
+        for n, owner in enumerate(owners):
+            row = pl.multiple_of(piece_of(tile ^ owner, tiles) * piece, 16)
+            place = out.at[pl.ds(row, piece), pl.ds(col, lanes)]
             copies.append(pltpu.make_async_copy(part.at[pl.ds(n * piece, piece)], place, sems.at[len(copies)]))
     for copy in copies:
         copy.start()
@@ -305,30 +305,33 @@
     every = in_order([ends] + [got[piece + POWER :] for got in gots], late[1:])
     every = jnp.concatenate([v.reshape(2, EDGE, lanes) for v in every], axis=0).astype(F32)
     own = order(finish(total, every).astype(F16))
-    own = [own]
-    if direct:
-        own += [exchange(own[0], "width", 2 * n) for n in range(1, others)]
-        yield None
-    else:
-        for b in reversed(range(1, len(late))):
-            got = exchange(jnp.stack(own), "width", 1 << b)
+    if not direct:
+        own = own[None]
+        bits = [*reversed(range(2, len(late))), 0, 1]
+        tiles = [0]
+        for b in bits:
+            got = exchange(own, "width", 1 << b)
             yield None
             got = order(got)
             yield None
-            own = order([piece for piece in own] + [got[n] for n in range(len(own))])
-        own = [own[reversed_bits(n, len(late) - 1)] for n in range(others)]
-    parts = (range(others // 2), range(others // 2, others)) if direct and halves else (range(others),)
+            own = order(jnp.concatenate([own, got], axis=0))
+            tiles += [tile ^ 1 << b for tile in tiles]
+        yield [(unpacked(own), tiles)]
+        return
+    own = [own] + [exchange(own, "width", 2 * n) for n in range(1, others)]
+    yield None
     gots = []
-    for part in parts:
+    for part in (range(others // 2), range(others // 2, others)) if halves else (range(others),):
+        tiles = [2 * n for n in part]
         part = order([own[n] for n in part])
         yield None
         part = order(jnp.stack(part))
-        gots.append((part, exchange(part, "width", 1)))
-    pairs = []
-    for part, got in gots:
+        gots.append((part, exchange(part, "width", 1), tiles))
+    parts = []
+    for part, got, tiles in gots:
         yield None
-        pairs.append((unpacked(part), unpacked(order(got))))
-    yield pairs
+        parts += [(unpacked(part), tiles), (unpacked(order(got)), [tile ^ 1 for tile in tiles])]
+    yield parts
 
 
 def unpacked(every):
@@ -337,26 +340,20 @@
     return (every[:, :rows].astype(F32) * scale).reshape(-1, every.shape[2])
 
 
-FIRST = (0.0, 1.9, 2.0, 3.9, 4.0, 5.9, 6.0, 7.9)
+FIRST = (0.0, 1.9, 2.0, 3.9, 4.0, 4.6, 4.62, 5.5, 5.52, 7.9)
 LATER = (1.95, 3.85, 4.05, 5.95, 6.05, 6.5, 6.6, 6.7, 9.9, 10.0)
 FORWARD = (0.1, 0.2, 2.7, 4.03, 5.94, 6.45)
 BACKWARD = (6.72, 9.6)
 PARTNERS = 0.3
 AFTER = 2.0
-DIRECT = (True, True)
+DIRECT = (False, True)
 SPLIT = True
 HALVES = (False, True)
 
 
 def chunk_times(j, steps):
     base = FIRST if j == 0 else [now + AFTER * (j - 1) for now in LATER]
-    if DIRECT[min(j, 1)]:
-        return base
-    hops = []
-    for n in range(1, steps):
-        now = base[4] + (base[6] - base[4]) * n / (steps - 1)
-        hops += [now - 0.1 if n < steps - 1 else base[5], now]
-    return [*base[:5], *hops, *base[7:]]
+    return base
 
 
 def body(activations, filters, cotangent):
@@ -491,21 +488,18 @@
     pieces = [pieces[j] for j in range(groups // 2)]
 
     if lanes % LANES:
-        sides = [[jnp.concatenate([pair[side] for pair in pieces[j]], axis=0) for side in range(2)] for j in range(len(pieces))]
-        sides = [[jnp.split(v, width // 2, axis=0) for v in pair] for pair in sides]
-        sides = [[jnp.concatenate(in_order(v, late[1:]), axis=0) for v in pair] for pair in sides]
-        pieces = [jnp.concatenate(doubled(got, own, late[0]), axis=0) for own, got in sides]
+        for j in range(len(pieces)):
+            terms = {}
+            for part, owners in pieces[j]:
+                terms.update(zip(owners, jnp.split(part, len(owners), axis=0)))
+            terms = in_order([terms[n] for n in range(width)], late)
+            pieces[j] = jnp.concatenate([terms[p // (width // 2) + 2 * (p % (width // 2))] for p in range(width)], axis=0)
         for b in range(bits_of(groups // 2)):
             pieces = [jnp.where(swaps[b], pieces[j ^ 1 << b], pieces[j]) for j in range(len(pieces))]
         grads = jnp.concatenate(pieces, axis=1)
     else:
-        parts, layout = [], []
-        for j, pairs in enumerate(pieces):
-            first = 0
-            for own, got in pairs:
-                parts += [own, got]
-                layout += [(j, 0, first), (j, 1, first)]
-                first += own.shape[0] // piece
+        parts = [part for chunk in pieces for part, _ in chunk]
+        layout = [(j, owners) for j, chunk in enumerate(pieces) for _, owners in chunk]
         grads = pl.pallas_call(
             functools.partial(place_kernel, piece, layout),
             out_shape=jax.ShapeDtypeStruct((width * piece, outs), F32),

time: 70 us -> 68.6 us (0.980)
  starting transfers between devices: 30 us -> 27.3 us
  waiting for transfers between devices: 19.8 us -> 21 us
    ppermute x23 -> x22, starting transfers between devices: 29.2 us -> 26.4 us  [exchange(): return lax.ppermute(value, axis, [(i, i ^ bit) for i in range(devices)])]
    ppermute x23 -> x22, waiting for transfers between devices: 19.8 us -> 21 us  [exchange(): return lax.ppermute(value, axis, [(i, i ^ bit) for i in range(devices)])]
    unnamed x14 -> x13, local copies, waits for them, and re-layouts: 3.33 us -> 3.32 us
  transfers between devices with their start and end apart: 24 -> 23, of which waited for: 12 -> 10; matrix products, arithmetic and copies ran while one was open for 6% -> 6% of each run, Pallas kernels for 14% -> 14%
where the time goes in v6:
time: 68.6 us; the launch traced here: 68.4 us
  starting transfers between devices  27.3 us (40%)
  waiting for transfers between devices  21 us (31%)
  Pallas kernels  12.5 us (18%)
  local copies, waits for them, and re-layouts  4.43 us (6%)
  other arithmetic  1.97 us (3%)
  between operations  1.28 us (2%)
    ppermute x22, starting transfers between devices, exchange(): return lax.ppermute(value, axis, [(i, i ^ bit) for i in range(devices)])  26.4 us
    ppermute x22, waiting for transfers between devices, exchange(): return lax.ppermute(value, axis, [(i, i ^ bit) for i in range(devices)])  21 us
    pallas_call x8, Pallas kernels, call(): pl.pallas_call(body, out_shape=outs, in_specs=[VMEM] * len(args), out_spe...  10.9 us
    unnamed x13, local copies, waits for them, and re-layouts  3.32 us
    pallas_call x1, Pallas kernels, body(): pl.pallas_call(functools.partial(place_kernel, piece, layout), out_shape=...  1.55 us
  transfers between devices with their start and end apart: 23, of which 10 were waited for; matrix products, arithmetic and copies ran while one was open for 6% of the time, Pallas kernels for 14%

profile of v6, /device:TPU:0, one launch (start us, length us, event | category | flops | bytes accessed | tf_op | source)
XLA Modules:
  0.0 68.4 jit_solution(14656628198428589500)
XLA Ops:
  2.2 2.6 %collective-permute-start.2 = (bf16[2,128,768]{2,1,0:T(8,128)(2,1)S(1)}, bf16[2,128,768]{2,1,0:T(8,128)(2,1)S(1)}, u32[]{:S(2)}, u32[]{:S(2)}) collective-permute-start(bf16[2,128,768]{2,1,0:T(8,128)(2,1)S(1)} %bitcast.99), channel_id=1, source_target_pairs={{0,2},{1,3},{2,0},{3,1},{4,6},{5,7},{6,4},{7,5},{8,10},{9,11},{10,... | collective-permute-start | bytes 1179656 | tf_op jit(solution)/shard_map/ppermute | solution.py:24
  5.8 1.5 %shifted_taps.2 = (bf16[2,384,768]{2,1,0:T(8,128)(2,1)S(1)}, bf16[2,256]{1,0:T(2,128)(2,1)S(1)}) custom-call(bf16[128,2,768]{2,1,0:T(2,128)(2,1)S(1)} %copy-done), custom_call_target="tpu_custom_call" | custom-call | bytes 1573888 | tf_op jit(solution)/shard_map/shifted_taps/pallas_call | solution.py:45
  8.6 1.6 %collective-permute-start.1 = (f16[592,256]{1,0:T(8,128)(2,1)S(1)}, f16[592,256]{1,0:T(8,128)(2,1)S(1)}, u32[]{:S(2)}, u32[]{:S(2)}) collective-permute-start(f16[592,256]{1,0:T(8,128)(2,1)S(1)} %convert_element_type.142), channel_id=1, source_target_pairs={{0,4},{4,0},{8,12},{12,8},{16,20},{20,16},{24,28},{28,24},{1,5},{5... | collective-permute-start | bytes 909320 | tf_op jit(solution)/shard_map/ppermute | solution.py:24
  11.0 3.5 %collective-permute-done.2.ga.refs_2_ = bf16[2,128,768]{2,1,0:T(8,128)(2,1)S(1)} collective-permute-done((bf16[2,128,768]{2,1,0:T(8,128)(2,1)S(1)}, bf16[2,128,768]{2,1,0:T(8,128)(2,1)S(1)}, u32[]{:S(2)}, u32[]{:S(2)}) %collective-permute-start.2) | collective-permute-done | bytes 393248 | tf_op jit(solution)/shard_map/ppermute | solution.py:24
  14.5 3.4 %collective-permute-done.1 = f16[592,256]{1,0:T(8,128)(2,1)S(1)} collective-permute-done((f16[592,256]{1,0:T(8,128)(2,1)S(1)}, f16[592,256]{1,0:T(8,128)(2,1)S(1)}, u32[]{:S(2)}, u32[]{:S(2)}) %collective-permute-start.1) | collective-permute-done | bytes 303136 | tf_op jit(solution)/shard_map/ppermute | solution.py:24
  19.4 1.6 %collective-permute-start.9 = (f16[592,256]{1,0:T(8,128)(2,1)S(1)}, f16[592,256]{1,0:T(8,128)(2,1)S(1)}, u32[]{:S(2)}, u32[]{:S(2)}) collective-permute-start(f16[592,256]{1,0:T(8,128)(2,1)S(1)} %convert_element_type.150), channel_id=1, source_target_pairs={{0,4},{4,0},{8,12},{12,8},{16,20},{20,16},{24,28},{28,24},{1,5},{5... | collective-permute-start | bytes 909320 | tf_op jit(solution)/shard_map/ppermute | solution.py:24
  20.9 1.6 %collective-permute-start.6 = (f16[168,256]{1,0:T(8,128)(2,1)S(1)}, f16[168,256]{1,0:T(8,128)(2,1)S(1)}, u32[]{:S(2)}, u32[]{:S(2)}) collective-permute-start(f16[168,256]{1,0:T(8,128)(2,1)S(1)} %get-tuple-element.76), channel_id=1, source_target_pairs={{0,8},{4,12},{8,0},{12,4},{16,24},{20,28},{24,16},{28,20},{1,9},{5... | collective-permute-start | bytes 258056 | tf_op jit(solution)/shard_map/ppermute | solution.py:24
  22.5 2.6 %collective-permute-start.7 = (f16[168,256]{1,0:T(8,128)(2,1)S(1)}, f16[168,256]{1,0:T(8,128)(2,1)S(1)}, u32[]{:S(2)}, u32[]{:S(2)}) collective-permute-start(f16[168,256]{1,0:T(8,128)(2,1)S(1)} %get-tuple-element.82), channel_id=1, source_target_pairs={{0,16},{4,20},{8,24},{12,28},{16,0},{20,4},{24,8},{28,12},{1,17},{... | collective-permute-start | bytes 258056 | tf_op jit(solution)/shard_map/ppermute | solution.py:24
  25.4 2.1 %shifted_taps.3 = (bf16[2,384,768]{2,1,0:T(8,128)(2,1)S(1)}, bf16[2,256]{1,0:T(2,128)(2,1)}) custom-call(bf16[128,2,768]{2,1,0:T(2,128)(2,1)S(1)} %copy-done.1, bf16[1,256]{1,0:T(2,128)(2,1)S(1)} %broadcast_select_fusion.13.refs_0_, bf16[1,256]{1,0:T(2,128)(2,1)S(1)} %get-tuple-element.129.refs_1_), custom_call_target="tpu_custom_call" | custom-call | bytes 1574912 | tf_op jit(solution)/shard_map/shifted_taps/pallas_call | solution.py:45
  27.5 2.0 %forward_terms.1 = (f32[2,2,128,768]{3,2,1,0:T(8,128)S(1)}, f32[2,2,128,768]{3,2,1,0:T(8,128)S(1)}) custom-call(bf16[2,384,768]{2,1,0:T(8,128)(2,1)S(1)} %get-tuple-element.78.xs, bf16[3,384,512]{2,1,0:T(8,128)(2,1)S(1)} %bitcast.103), custom_call_target="tpu_custom_call" | custom-call | flops 1207959552 | bytes 5505024 | tf_op jit(solution)/shard_map/forward_terms/pallas_call | solution.py:45
  32.2 2.3 %collective-permute-start.11 = (f16[1,152,256]{2,1,0:T(8,128)(2,1)S(1)}, f16[1,152,256]{2,1,0:T(8,128)(2,1)S(1)}, u32[]{:S(2)}, u32[]{:S(2)}) collective-permute-start(f16[1,152,256]{2,1,0:T(8,128)(2,1)S(1)} %bitcast.106), channel_id=1, source_target_pairs={{0,16},{4,20},{8,24},{12,28},{16,0},{20,4},{24,8},{28,12},{1,17},{... | collective-permute-start | bytes 233480 | tf_op jit(solution)/shard_map/ppermute | solution.py:24
  35.8 2.6 %collective-permute-done.11 = f16[1,152,256]{2,1,0:T(8,128)(2,1)S(1)} collective-permute-done((f16[1,152,256]{2,1,0:T(8,128)(2,1)S(1)}, f16[1,152,256]{2,1,0:T(8,128)(2,1)S(1)}, u32[]{:S(2)}, u32[]{:S(2)}) %collective-permute-start.11) | collective-permute-done | bytes 77856 | tf_op jit(solution)/shard_map/ppermute | solution.py:24
  38.8 1.5 %collective-permute-start.14 = (f16[168,256]{1,0:T(8,128)(2,1)S(1)}, f16[168,256]{1,0:T(8,128)(2,1)S(1)}, u32[]{:S(2)}, u32[]{:S(2)}) collective-permute-start(f16[168,256]{1,0:T(8,128)(2,1)S(1)} %get-tuple-element.95), channel_id=1, source_target_pairs={{0,8},{4,12},{8,0},{12,4},{16,24},{20,28},{24,16},{28,20},{1,9},{5... | collective-permute-start | bytes 258056 | tf_op jit(solution)/shard_map/ppermute | solution.py:24
  40.8 1.6 %collective-permute-start.15 = (f16[168,256]{1,0:T(8,128)(2,1)S(1)}, f16[168,256]{1,0:T(8,128)(2,1)S(1)}, u32[]{:S(2)}, u32[]{:S(2)}) collective-permute-start(f16[168,256]{1,0:T(8,128)(2,1)S(1)} %get-tuple-element.101), channel_id=1, source_target_pairs={{0,16},{4,20},{8,24},{12,28},{16,0},{20,4},{24,8},{28,12},{1,17},{... | collective-permute-start | bytes 258056 | tf_op jit(solution)/shard_map/ppermute | solution.py:24
  42.3 1.4 %collective-permute-done.12 = f16[2,152,256]{2,1,0:T(8,128)(2,1)S(1)} collective-permute-done((f16[2,152,256]{2,1,0:T(8,128)(2,1)S(1)}, f16[2,152,256]{2,1,0:T(8,128)(2,1)S(1)}, u32[]{:S(2)}, u32[]{:S(2)}) %collective-permute-start.12) | collective-permute-done | bytes 155680 | tf_op jit(solution)/shard_map/ppermute | solution.py:24
  45.3 2.0 %collective-permute-done.10 = f32[128,768]{1,0:T(8,128)S(1)} collective-permute-done((f32[128,768]{1,0:T(8,128)S(1)}, f32[128,768]{1,0:T(8,128)S(1)}, u32[]{:S(2)}, u32[]{:S(2)}) %collective-permute-start.10) | collective-permute-done | bytes 393248 | tf_op jit(solution)/shard_map/ppermute | solution.py:24
  47.8 3.2 %collective-permute-done.16 = f16[168,256]{1,0:T(8,128)(2,1)S(1)} collective-permute-done((f16[168,256]{1,0:T(8,128)(2,1)S(1)}, f16[168,256]{1,0:T(8,128)(2,1)S(1)}, u32[]{:S(2)}, u32[]{:S(2)}) %collective-permute-start.16) | collective-permute-done | bytes 86048 | tf_op jit(solution)/shard_map/ppermute | solution.py:24
  51.7 2.0 %collective-permute-start.17 = (f16[152,256]{1,0:T(8,128)(2,1)S(1)}, f16[152,256]{1,0:T(8,128)(2,1)S(1)}, u32[]{:S(2)}, u32[]{:S(2)}) collective-permute-start(f16[152,256]{1,0:T(8,128)(2,1)S(1)} %convert_element_type.176), channel_id=1, source_target_pairs={{0,16},{4,20},{8,24},{12,28},{16,0},{20,4},{24,8},{28,12},{1,17},{... | collective-permute-start | bytes 233480 | tf_op jit(solution)/shard_map/ppermute | solution.py:24
  53.7 2.4 %collective-permute-start.18 = (f16[152,256]{1,0:T(8,128)(2,1)S(1)}, f16[152,256]{1,0:T(8,128)(2,1)S(1)}, u32[]{:S(2)}, u32[]{:S(2)}) collective-permute-start(f16[152,256]{1,0:T(8,128)(2,1)S(1)} %convert_element_type.176), channel_id=1, source_target_pairs={{0,24},{4,28},{8,16},{12,20},{16,8},{20,12},{24,0},{28,4},{1,25},{... | collective-permute-start | bytes 233480 | tf_op jit(solution)/shard_map/ppermute | solution.py:24
  57.4 2.2 %collective-permute-start.22 = (f16[2,152,256]{2,1,0:T(8,128)(2,1)S(1)}, f16[2,152,256]{2,1,0:T(8,128)(2,1)S(1)}, u32[]{:S(2)}, u32[]{:S(2)}) collective-permute-start(f16[2,152,256]{2,1,0:T(8,128)(2,1)S(1)} %pad_maximum_fusion.3), channel_id=1, source_target_pairs={{0,4},{4,0},{8,12},{12,8},{16,20},{20,16},{24,28},{28,24},{1,5},{5... | collective-permute-start | bytes 466952 | tf_op jit(solution)/shard_map/ppermute | solution.py:24
  59.6 1.5 %collective-permute-done.18 = f16[152,256]{1,0:T(8,128)(2,1)S(1)} collective-permute-done((f16[152,256]{1,0:T(8,128)(2,1)S(1)}, f16[152,256]{1,0:T(8,128)(2,1)S(1)}, u32[]{:S(2)}, u32[]{:S(2)}) %collective-permute-start.18) | collective-permute-done | bytes 77856 | tf_op jit(solution)/shard_map/ppermute | solution.py:24
  61.5 2.1 %input_terms.1 = bf16[2,128,768]{2,1,0:T(8,128)(2,1)S(1)} custom-call(bf16[1152,512]{1,0:T(8,128)(2,1)S(1)} %bitcast.104, f32[2,8,8,256]{3,2,1,0:T(8,128)S(1)} %pad_maximum_fusion.23.ends, bf16[2,128,768]{2,1,0:T(8,128)(2,1)S(1)} %bitcast.101, bf16[2,128,768]{2,1,0:T(8,128)(2,1)S(1)} %collective-permute-done.gb.refs_1_, ...), custom_call_target="tpu_custom_call" | custom-call | flops 1207959552 | bytes 3276800 | tf_op jit(solution)/shard_map/input_terms/pallas_call | solution.py:45
  64.9 1.5 %collective-permute-done.21 = f16[2,152,256]{2,1,0:T(8,128)(2,1)S(1)} collective-permute-done((f16[2,152,256]{2,1,0:T(8,128)(2,1)S(1)}, f16[2,152,256]{2,1,0:T(8,128)(2,1)S(1)}, u32[]{:S(2)}, u32[]{:S(2)}) %collective-permute-start.21) | collective-permute-done | bytes 155680 | tf_op jit(solution)/shard_map/ppermute | solution.py:24
  66.7 1.5 %place_pieces.1 = f32[1152,512]{1,0:T(8,128)} custom-call(f32[1152,256]{1,0:T(8,128)S(1)} %bitcast.91, f32[288,256]{1,0:T(8,128)S(1)} %bitcast.94, f32[288,256]{1,0:T(8,128)S(1)} %bitcast.96, f32[288,256]{1,0:T(8,128)S(1)} %bitcast.93, f32[288,256]{1,0:T(8,128)S(1)} %bitcast.95), custom_call_target="tpu_custom_call" | custom-call | tf_op jit(solution)/shard_map/place_pieces/pallas_call | solution.py:503
  (100 shorter events, 17.0 us)
Async XLA Ops:
  1.7 5.6 %collective-permute-start = (bf16[2,128,768]{2,1,0:T(8,128)(2,1)S(1)}, bf16[2,128,768]{2,1,0:T(8,128)(2,1)S(1)}, u32[]{:S(2)}, u32[]{:S(2)}) collective-permute-start(bf16[2,128,768]{2,1,0:T(8,128)(2,1)S(1)} %bitcast.98), channel_id=1, source_target_pairs={{0,1},{1,0},{2,3},{3,2},{4,5},{5,4},{6,7},{7,6},{8,9},{9,8},{10,11... | collective-permute-start | bytes 1179656 | tf_op jit(solution)/shard_map/ppermute | solution.py:24
  2.2 12.3 %collective-permute-start.2 = (bf16[2,128,768]{2,1,0:T(8,128)(2,1)S(1)}, bf16[2,128,768]{2,1,0:T(8,128)(2,1)S(1)}, u32[]{:S(2)}, u32[]{:S(2)}) collective-permute-start(bf16[2,128,768]{2,1,0:T(8,128)(2,1)S(1)} %bitcast.99), channel_id=1, source_target_pairs={{0,2},{1,3},{2,0},{3,1},{4,6},{5,7},{6,4},{7,5},{8,10},{9,11},{10,... | collective-permute-start | bytes 1179656 | tf_op jit(solution)/shard_map/ppermute | solution.py:24
  8.6 9.3 %collective-permute-start.1 = (f16[592,256]{1,0:T(8,128)(2,1)S(1)}, f16[592,256]{1,0:T(8,128)(2,1)S(1)}, u32[]{:S(2)}, u32[]{:S(2)}) collective-permute-start(f16[592,256]{1,0:T(8,128)(2,1)S(1)} %convert_element_type.142), channel_id=1, source_target_pairs={{0,4},{4,0},{8,12},{12,8},{16,20},{20,16},{24,28},{28,24},{1,5},{5... | collective-permute-start | bytes 909320 | tf_op jit(solution)/shard_map/ppermute | solution.py:24
  10.1 0.8 %collective-permute-start.3 = (bf16[1,256]{1,0:T(2,128)(2,1)S(1)}, bf16[1,256]{1,0:T(2,128)(2,1)S(1)}, u32[]{:S(2)}, u32[]{:S(2)}) collective-permute-start(bf16[1,256]{1,0:T(2,128)(2,1)S(1)} %broadcast_select_fusion.15), channel_id=1, source_target_pairs={{4,8},{12,16},{20,24},{8,4},{16,12},{24,20},{5,9},{13,17},{21,25},... | collective-permute-start | bytes 1544 | tf_op jit(solution)/shard_map/ppermute | solution.py:405
  14.5 3.7 %collective-permute-start.4 = (bf16[2,128,768]{2,1,0:T(8,128)(2,1)S(1)}, bf16[2,128,768]{2,1,0:T(8,128)(2,1)S(1)}, u32[]{:S(2)}, u32[]{:S(2)}) collective-permute-start(bf16[2,128,768]{2,1,0:T(8,128)(2,1)S(1)} %collective-permute-done.2.ga.refs_2_), channel_id=1, source_target_pairs={{0,1},{1,0},{2,3},{3,2},{4,5},{5,4},{6,7},{7,6},{8,9},{9,8},{10,11... | collective-permute-start | bytes 1179656 | tf_op jit(solution)/shard_map/ppermute | solution.py:24
  18.2 9.3 %copy-start.2 = (bf16[128,3,3,512]{3,0,2,1:T(8,128)(2,1)S(1)}, bf16[128,3,3,512]{3,0,2,1:T(8,128)(2,1)}, u32[]{:S(2)}) copy-start(bf16[128,3,3,512]{3,0,2,1:T(8,128)(2,1)} %param.4) | copy-start | bytes 3538948
  19.4 10.3 %collective-permute-start.9 = (f16[592,256]{1,0:T(8,128)(2,1)S(1)}, f16[592,256]{1,0:T(8,128)(2,1)S(1)}, u32[]{:S(2)}, u32[]{:S(2)}) collective-permute-start(f16[592,256]{1,0:T(8,128)(2,1)S(1)} %convert_element_type.150), channel_id=1, source_target_pairs={{0,4},{4,0},{8,12},{12,8},{16,20},{20,16},{24,28},{28,24},{1,5},{5... | collective-permute-start | bytes 909320 | tf_op jit(solution)/shard_map/ppermute | solution.py:24
  20.9 8.7 %collective-permute-start.6 = (f16[168,256]{1,0:T(8,128)(2,1)S(1)}, f16[168,256]{1,0:T(8,128)(2,1)S(1)}, u32[]{:S(2)}, u32[]{:S(2)}) collective-permute-start(f16[168,256]{1,0:T(8,128)(2,1)S(1)} %get-tuple-element.76), channel_id=1, source_target_pairs={{0,8},{4,12},{8,0},{12,4},{16,24},{20,28},{24,16},{28,20},{1,9},{5... | collective-permute-start | bytes 258056 | tf_op jit(solution)/shard_map/ppermute | solution.py:24
  22.5 7.9 %collective-permute-start.7 = (f16[168,256]{1,0:T(8,128)(2,1)S(1)}, f16[168,256]{1,0:T(8,128)(2,1)S(1)}, u32[]{:S(2)}, u32[]{:S(2)}) collective-permute-start(f16[168,256]{1,0:T(8,128)(2,1)S(1)} %get-tuple-element.82), channel_id=1, source_target_pairs={{0,16},{4,20},{8,24},{12,28},{16,0},{20,4},{24,8},{28,12},{1,17},{... | collective-permute-start | bytes 258056 | tf_op jit(solution)/shard_map/ppermute | solution.py:24
  25.2 6.4 %collective-permute-start.8 = (f16[168,256]{1,0:T(8,128)(2,1)S(1)}, f16[168,256]{1,0:T(8,128)(2,1)S(1)}, u32[]{:S(2)}, u32[]{:S(2)}) collective-permute-start(f16[168,256]{1,0:T(8,128)(2,1)S(1)} %get-tuple-element.83), channel_id=1, source_target_pairs={{0,24},{4,28},{8,16},{12,20},{16,8},{20,12},{24,0},{28,4},{1,25},{... | collective-permute-start | bytes 258056 | tf_op jit(solution)/shard_map/ppermute | solution.py:24
  29.6 5.2 %collective-permute-start.5 = (f32[2,2,128,768]{3,2,1,0:T(8,128)S(1)}, f32[2,2,128,768]{3,2,1,0:T(8,128)S(1)}, u32[]{:S(2)}, u32[]{:S(2)}) collective-permute-start(f32[2,2,128,768]{3,2,1,0:T(8,128)S(1)} %get-tuple-element.81), channel_id=1, source_target_pairs={{0,1},{1,0},{2,3},{3,2},{4,5},{5,4},{6,7},{7,6},{8,9},{9,8},{10,11... | collective-permute-start | bytes 4718600 | tf_op jit(solution)/shard_map/ppermute | solution.py:24
  32.2 6.2 %collective-permute-start.11 = (f16[1,152,256]{2,1,0:T(8,128)(2,1)S(1)}, f16[1,152,256]{2,1,0:T(8,128)(2,1)S(1)}, u32[]{:S(2)}, u32[]{:S(2)}) collective-permute-start(f16[1,152,256]{2,1,0:T(8,128)(2,1)S(1)} %bitcast.106), channel_id=1, source_target_pairs={{0,16},{4,20},{8,24},{12,28},{16,0},{20,4},{24,8},{28,12},{1,17},{... | collective-permute-start | bytes 233480 | tf_op jit(solution)/shard_map/ppermute | solution.py:24
  35.1 12.1 %collective-permute-start.10 = (f32[128,768]{1,0:T(8,128)S(1)}, f32[128,768]{1,0:T(8,128)S(1)}, u32[]{:S(2)}, u32[]{:S(2)}) collective-permute-start(f32[128,768]{1,0:T(8,128)S(1)} %get-tuple-element.92), channel_id=1, source_target_pairs={{0,2},{1,3},{2,0},{3,1},{4,6},{5,7},{6,4},{7,5},{8,10},{9,11},{10,... | collective-permute-start | bytes 1179656 | tf_op jit(solution)/shard_map/ppermute | solution.py:24
  38.5 5.3 %collective-permute-start.12 = (f16[2,152,256]{2,1,0:T(8,128)(2,1)S(1)}, f16[2,152,256]{2,1,0:T(8,128)(2,1)S(1)}, u32[]{:S(2)}, u32[]{:S(2)}) collective-permute-start(f16[2,152,256]{2,1,0:T(8,128)(2,1)S(1)} %pad_maximum_fusion.2), channel_id=1, source_target_pairs={{0,4},{4,0},{8,12},{12,8},{16,20},{20,16},{24,28},{28,24},{1,5},{5... | collective-permute-start | bytes 466952 | tf_op jit(solution)/shard_map/ppermute | solution.py:24
  38.8 9.0 %collective-permute-start.14 = (f16[168,256]{1,0:T(8,128)(2,1)S(1)}, f16[168,256]{1,0:T(8,128)(2,1)S(1)}, u32[]{:S(2)}, u32[]{:S(2)}) collective-permute-start(f16[168,256]{1,0:T(8,128)(2,1)S(1)} %get-tuple-element.95), channel_id=1, source_target_pairs={{0,8},{4,12},{8,0},{12,4},{16,24},{20,28},{24,16},{28,20},{1,9},{5... | collective-permute-start | bytes 258056 | tf_op jit(solution)/shard_map/ppermute | solution.py:24
  40.3 15.8 %collective-permute-start.13 = (f32[128,768]{1,0:T(8,128)S(1)}, f32[128,768]{1,0:T(8,128)S(1)}, u32[]{:S(2)}, u32[]{:S(2)}) collective-permute-start(f32[128,768]{1,0:T(8,128)S(1)} %get-tuple-element.94), channel_id=1, source_target_pairs={{0,2},{1,3},{2,0},{3,1},{4,6},{5,7},{6,4},{7,5},{8,10},{9,11},{10,... | collective-permute-start | bytes 1179656 | tf_op jit(solution)/shard_map/ppermute | solution.py:24
  40.8 7.0 %collective-permute-start.15 = (f16[168,256]{1,0:T(8,128)(2,1)S(1)}, f16[168,256]{1,0:T(8,128)(2,1)S(1)}, u32[]{:S(2)}, u32[]{:S(2)}) collective-permute-start(f16[168,256]{1,0:T(8,128)(2,1)S(1)} %get-tuple-element.101), channel_id=1, source_target_pairs={{0,16},{4,20},{8,24},{12,28},{16,0},{20,4},{24,8},{28,12},{1,17},{... | collective-permute-start | bytes 258056 | tf_op jit(solution)/shard_map/ppermute | solution.py:24
  43.8 7.2 %collective-permute-start.16 = (f16[168,256]{1,0:T(8,128)(2,1)S(1)}, f16[168,256]{1,0:T(8,128)(2,1)S(1)}, u32[]{:S(2)}, u32[]{:S(2)}) collective-permute-start(f16[168,256]{1,0:T(8,128)(2,1)S(1)} %get-tuple-element.102), channel_id=1, source_target_pairs={{0,24},{4,28},{8,16},{12,20},{16,8},{20,12},{24,0},{28,4},{1,25},{... | collective-permute-start | bytes 258056 | tf_op jit(solution)/shard_map/ppermute | solution.py:24
  47.3 16.3 %collective-permute-start.20 = (f16[4,152,256]{2,1,0:T(8,128)(2,1)S(1)}, f16[4,152,256]{2,1,0:T(8,128)(2,1)S(1)}, u32[]{:S(2)}, u32[]{:S(2)}) collective-permute-start(f16[4,152,256]{2,1,0:T(8,128)(2,1)S(1)} %pad_maximum_fusion.1), channel_id=1, source_target_pairs={{0,8},{4,12},{8,0},{12,4},{16,24},{20,28},{24,16},{28,20},{1,9},{5... | collective-permute-start | bytes 933896 | tf_op jit(solution)/shard_map/ppermute | solution.py:24
  51.6 5.8 %collective-permute-start.19 = (f16[152,256]{1,0:T(8,128)(2,1)S(1)}, f16[152,256]{1,0:T(8,128)(2,1)S(1)}, u32[]{:S(2)}, u32[]{:S(2)}) collective-permute-start(f16[152,256]{1,0:T(8,128)(2,1)S(1)} %convert_element_type.176), channel_id=1, source_target_pairs={{0,8},{4,12},{8,0},{12,4},{16,24},{20,28},{24,16},{28,20},{1,9},{5... | collective-permute-start | bytes 233480 | tf_op jit(solution)/shard_map/ppermute | solution.py:24
  51.7 7.9 %collective-permute-start.17 = (f16[152,256]{1,0:T(8,128)(2,1)S(1)}, f16[152,256]{1,0:T(8,128)(2,1)S(1)}, u32[]{:S(2)}, u32[]{:S(2)}) collective-permute-start(f16[152,256]{1,0:T(8,128)(2,1)S(1)} %convert_element_type.176), channel_id=1, source_target_pairs={{0,16},{4,20},{8,24},{12,28},{16,0},{20,4},{24,8},{28,12},{1,17},{... | collective-permute-start | bytes 233480 | tf_op jit(solution)/shard_map/ppermute | solution.py:24
  53.7 7.4 %collective-permute-start.18 = (f16[152,256]{1,0:T(8,128)(2,1)S(1)}, f16[152,256]{1,0:T(8,128)(2,1)S(1)}, u32[]{:S(2)}, u32[]{:S(2)}) collective-permute-start(f16[152,256]{1,0:T(8,128)(2,1)S(1)} %convert_element_type.176), channel_id=1, source_target_pairs={{0,24},{4,28},{8,16},{12,20},{16,8},{20,12},{24,0},{28,4},{1,25},{... | collective-permute-start | bytes 233480 | tf_op jit(solution)/shard_map/ppermute | solution.py:24
  57.4 7.5 %collective-permute-start.22 = (f16[2,152,256]{2,1,0:T(8,128)(2,1)S(1)}, f16[2,152,256]{2,1,0:T(8,128)(2,1)S(1)}, u32[]{:S(2)}, u32[]{:S(2)}) collective-permute-start(f16[2,152,256]{2,1,0:T(8,128)(2,1)S(1)} %pad_maximum_fusion.3), channel_id=1, source_target_pairs={{0,4},{4,0},{8,12},{12,8},{16,20},{20,16},{24,28},{28,24},{1,5},{5... | collective-permute-start | bytes 466952 | tf_op jit(solution)/shard_map/ppermute | solution.py:24
  61.1 5.3 %collective-permute-start.21 = (f16[2,152,256]{2,1,0:T(8,128)(2,1)S(1)}, f16[2,152,256]{2,1,0:T(8,128)(2,1)S(1)}, u32[]{:S(2)}, u32[]{:S(2)}) collective-permute-start(f16[2,152,256]{2,1,0:T(8,128)(2,1)S(1)} %pad_maximum_fusion.4), channel_id=1, source_target_pairs={{0,4},{4,0},{8,12},{12,8},{16,20},{20,16},{24,28},{28,24},{1,5},{5... | collective-permute-start | bytes 466952 | tf_op jit(solution)/shard_map/ppermute | solution.py:24
  (2 other events, 8.3 us)

commit v7 on v6

--- a/solution.py
+++ b/solution.py
@@ -342,7 +342,7 @@
 
 FIRST = (0.0, 1.9, 2.0, 3.9, 4.0, 4.6, 4.62, 5.5, 5.52, 7.9)
 LATER = (1.95, 3.85, 4.05, 5.95, 6.05, 6.5, 6.6, 6.7, 9.9, 10.0)
-FORWARD = (0.1, 0.2, 2.7, 4.03, 5.94, 6.45)
+FORWARD = (0.1, 0.2, 2.7, 4.06, 5.94, 6.45)
 BACKWARD = (6.72, 9.6)
 PARTNERS = 0.3
 AFTER = 2.0

time: 68.6 us -> 67.6 us (0.985)
  transfers between devices with their start and end apart: 23 -> 23, of which waited for: 10 -> 11; matrix products, arithmetic and copies ran while one was open for 6% -> 6% of each run, Pallas kernels for 14% -> 15%
where the time goes in v7:
time: 67.6 us; the launch traced here: 67.4 us
  starting transfers between devices  26.9 us (40%)
  waiting for transfers between devices  20.4 us (30%)
  Pallas kernels  12.5 us (18%)
  local copies, waits for them, and re-layouts  4.43 us (7%)
  other arithmetic  1.97 us (3%)
  between operations  1.28 us (2%)
    ppermute x22, starting transfers between devices, exchange(): return lax.ppermute(value, axis, [(i, i ^ bit) for i in range(devices)])  26 us
    ppermute x22, waiting for transfers between devices, exchange(): return lax.ppermute(value, axis, [(i, i ^ bit) for i in range(devices)])  20.4 us
    pallas_call x8, Pallas kernels, call(): pl.pallas_call(body, out_shape=outs, in_specs=[VMEM] * len(args), out_spe...  10.9 us
    unnamed x13, local copies, waits for them, and re-layouts  3.32 us
    pallas_call x1, Pallas kernels, body(): pl.pallas_call(functools.partial(place_kernel, piece, layout), out_shape=...  1.55 us
  transfers between devices with their start and end apart: 23, of which 11 were waited for; matrix products, arithmetic and copies ran while one was open for 6% of the time, Pallas kernels for 15%

profile of v7, /device:TPU:0, one launch (start us, length us, event | category | flops | bytes accessed | tf_op | source)
XLA Modules:
  0.0 67.4 jit_solution(10658853141507171362)
XLA Ops:
  2.2 2.6 %collective-permute-start.2 = (bf16[2,128,768]{2,1,0:T(8,128)(2,1)S(1)}, bf16[2,128,768]{2,1,0:T(8,128)(2,1)S(1)}, u32[]{:S(2)}, u32[]{:S(2)}) collective-permute-start(bf16[2,128,768]{2,1,0:T(8,128)(2,1)S(1)} %bitcast.99), channel_id=1, source_target_pairs={{0,2},{1,3},{2,0},{3,1},{4,6},{5,7},{6,4},{7,5},{8,10},{9,11},{10,... | collective-permute-start | bytes 1179656 | tf_op jit(solution)/shard_map/ppermute | solution.py:24
  5.8 1.5 %shifted_taps.2 = (bf16[2,384,768]{2,1,0:T(8,128)(2,1)S(1)}, bf16[2,256]{1,0:T(2,128)(2,1)S(1)}) custom-call(bf16[128,2,768]{2,1,0:T(2,128)(2,1)S(1)} %copy-done), custom_call_target="tpu_custom_call" | custom-call | bytes 1573888 | tf_op jit(solution)/shard_map/shifted_taps/pallas_call | solution.py:45
  7.3 1.2 %filter_terms.2 = (f32[592,256]{1,0:T(8,128)S(1)}, f32[584,256]{1,0:T(8,128)S(1)}) custom-call(bf16[2,384,768]{2,1,0:T(8,128)(2,1)S(1)} %get-tuple-element.63.xs, bf16[2,128,768]{2,1,0:T(8,128)(2,1)S(1)} %bitcast.100, bf16[2,128,768]{2,1,0:T(8,128)(2,1)S(1)} %collective-permute-done.gb.refs_1_), custom_call_target="tpu_custom_call" | custom-call | flops 603979776 | bytes 3170304 | tf_op jit(solution)/shard_map/filter_terms/pallas_call | solution.py:45
  8.6 1.6 %collective-permute-start.1 = (f16[592,256]{1,0:T(8,128)(2,1)S(1)}, f16[592,256]{1,0:T(8,128)(2,1)S(1)}, u32[]{:S(2)}, u32[]{:S(2)}) collective-permute-start(f16[592,256]{1,0:T(8,128)(2,1)S(1)} %convert_element_type.142), channel_id=1, source_target_pairs={{0,4},{4,0},{8,12},{12,8},{16,20},{20,16},{24,28},{28,24},{1,5},{5... | collective-permute-start | bytes 909320 | tf_op jit(solution)/shard_map/ppermute | solution.py:24
  11.0 3.5 %collective-permute-done.2.ga.refs_2_ = bf16[2,128,768]{2,1,0:T(8,128)(2,1)S(1)} collective-permute-done((bf16[2,128,768]{2,1,0:T(8,128)(2,1)S(1)}, bf16[2,128,768]{2,1,0:T(8,128)(2,1)S(1)}, u32[]{:S(2)}, u32[]{:S(2)}) %collective-permute-start.2) | collective-permute-done | bytes 393248 | tf_op jit(solution)/shard_map/ppermute | solution.py:24
  14.5 3.4 %collective-permute-done.1 = f16[592,256]{1,0:T(8,128)(2,1)S(1)} collective-permute-done((f16[592,256]{1,0:T(8,128)(2,1)S(1)}, f16[592,256]{1,0:T(8,128)(2,1)S(1)}, u32[]{:S(2)}, u32[]{:S(2)}) %collective-permute-start.1) | collective-permute-done | bytes 303136 | tf_op jit(solution)/shard_map/ppermute | solution.py:24
  19.4 1.6 %collective-permute-start.6 = (f16[592,256]{1,0:T(8,128)(2,1)S(1)}, f16[592,256]{1,0:T(8,128)(2,1)S(1)}, u32[]{:S(2)}, u32[]{:S(2)}) collective-permute-start(f16[592,256]{1,0:T(8,128)(2,1)S(1)} %convert_element_type.150), channel_id=1, source_target_pairs={{0,4},{4,0},{8,12},{12,8},{16,20},{20,16},{24,28},{28,24},{1,5},{5... | collective-permute-start | bytes 909320 | tf_op jit(solution)/shard_map/ppermute | solution.py:24
  20.9 1.6 %collective-permute-start.7 = (f16[168,256]{1,0:T(8,128)(2,1)S(1)}, f16[168,256]{1,0:T(8,128)(2,1)S(1)}, u32[]{:S(2)}, u32[]{:S(2)}) collective-permute-start(f16[168,256]{1,0:T(8,128)(2,1)S(1)} %get-tuple-element.76), channel_id=1, source_target_pairs={{0,8},{4,12},{8,0},{12,4},{16,24},{20,28},{24,16},{28,20},{1,9},{5... | collective-permute-start | bytes 258056 | tf_op jit(solution)/shard_map/ppermute | solution.py:24
  22.5 2.6 %collective-permute-start.8 = (f16[168,256]{1,0:T(8,128)(2,1)S(1)}, f16[168,256]{1,0:T(8,128)(2,1)S(1)}, u32[]{:S(2)}, u32[]{:S(2)}) collective-permute-start(f16[168,256]{1,0:T(8,128)(2,1)S(1)} %get-tuple-element.84), channel_id=1, source_target_pairs={{0,16},{4,20},{8,24},{12,28},{16,0},{20,4},{24,8},{28,12},{1,17},{... | collective-permute-start | bytes 258056 | tf_op jit(solution)/shard_map/ppermute | solution.py:24
  25.4 2.1 %shifted_taps.3 = (bf16[2,384,768]{2,1,0:T(8,128)(2,1)S(1)}, bf16[2,256]{1,0:T(2,128)(2,1)}) custom-call(bf16[128,2,768]{2,1,0:T(2,128)(2,1)S(1)} %copy-done.1, bf16[1,256]{1,0:T(2,128)(2,1)S(1)} %broadcast_select_fusion.13.refs_0_, bf16[1,256]{1,0:T(2,128)(2,1)S(1)} %get-tuple-element.129.refs_1_), custom_call_target="tpu_custom_call" | custom-call | bytes 1574912 | tf_op jit(solution)/shard_map/shifted_taps/pallas_call | solution.py:45
  27.5 2.0 %forward_terms.1 = (f32[2,2,128,768]{3,2,1,0:T(8,128)S(1)}, f32[2,2,128,768]{3,2,1,0:T(8,128)S(1)}) custom-call(bf16[2,384,768]{2,1,0:T(8,128)(2,1)S(1)} %get-tuple-element.78.xs, bf16[3,384,512]{2,1,0:T(8,128)(2,1)S(1)} %bitcast.103), custom_call_target="tpu_custom_call" | custom-call | flops 1207959552 | bytes 5505024 | tf_op jit(solution)/shard_map/forward_terms/pallas_call | solution.py:45
  30.4 1.2 %collective-permute-done.9 = f16[168,256]{1,0:T(8,128)(2,1)S(1)} collective-permute-done((f16[168,256]{1,0:T(8,128)(2,1)S(1)}, f16[168,256]{1,0:T(8,128)(2,1)S(1)}, u32[]{:S(2)}, u32[]{:S(2)}) %collective-permute-start.9) | collective-permute-done | bytes 86048 | tf_op jit(solution)/shard_map/ppermute | solution.py:24
  32.5 2.3 %collective-permute-start.11 = (f16[1,152,256]{2,1,0:T(8,128)(2,1)S(1)}, f16[1,152,256]{2,1,0:T(8,128)(2,1)S(1)}, u32[]{:S(2)}, u32[]{:S(2)}) collective-permute-start(f16[1,152,256]{2,1,0:T(8,128)(2,1)S(1)} %bitcast.106), channel_id=1, source_target_pairs={{0,16},{4,20},{8,24},{12,28},{16,0},{20,4},{24,8},{28,12},{1,17},{... | collective-permute-start | bytes 233480 | tf_op jit(solution)/shard_map/ppermute | solution.py:24
  35.8 2.9 %collective-permute-done.11 = f16[1,152,256]{2,1,0:T(8,128)(2,1)S(1)} collective-permute-done((f16[1,152,256]{2,1,0:T(8,128)(2,1)S(1)}, f16[1,152,256]{2,1,0:T(8,128)(2,1)S(1)}, u32[]{:S(2)}, u32[]{:S(2)}) %collective-permute-start.11) | collective-permute-done | bytes 77856 | tf_op jit(solution)/shard_map/ppermute | solution.py:24
  39.1 1.5 %collective-permute-start.14 = (f16[168,256]{1,0:T(8,128)(2,1)S(1)}, f16[168,256]{1,0:T(8,128)(2,1)S(1)}, u32[]{:S(2)}, u32[]{:S(2)}) collective-permute-start(f16[168,256]{1,0:T(8,128)(2,1)S(1)} %get-tuple-element.92), channel_id=1, source_target_pairs={{0,8},{4,12},{8,0},{12,4},{16,24},{20,28},{24,16},{28,20},{1,9},{5... | collective-permute-start | bytes 258056 | tf_op jit(solution)/shard_map/ppermute | solution.py:24
  40.6 1.6 %collective-permute-start.15 = (f16[168,256]{1,0:T(8,128)(2,1)S(1)}, f16[168,256]{1,0:T(8,128)(2,1)S(1)}, u32[]{:S(2)}, u32[]{:S(2)}) collective-permute-start(f16[168,256]{1,0:T(8,128)(2,1)S(1)} %get-tuple-element.101), channel_id=1, source_target_pairs={{0,16},{4,20},{8,24},{12,28},{16,0},{20,4},{24,8},{28,12},{1,17},{... | collective-permute-start | bytes 258056 | tf_op jit(solution)/shard_map/ppermute | solution.py:24
  42.1 1.4 %collective-permute-start.16 = (f16[168,256]{1,0:T(8,128)(2,1)S(1)}, f16[168,256]{1,0:T(8,128)(2,1)S(1)}, u32[]{:S(2)}, u32[]{:S(2)}) collective-permute-start(f16[168,256]{1,0:T(8,128)(2,1)S(1)} %get-tuple-element.102), channel_id=1, source_target_pairs={{0,24},{4,28},{8,16},{12,20},{16,8},{20,12},{24,0},{28,4},{1,25},{... | collective-permute-start | bytes 258056 | tf_op jit(solution)/shard_map/ppermute | solution.py:24
  44.2 2.2 %collective-permute-done.10 = f32[128,768]{1,0:T(8,128)S(1)} collective-permute-done((f32[128,768]{1,0:T(8,128)S(1)}, f32[128,768]{1,0:T(8,128)S(1)}, u32[]{:S(2)}, u32[]{:S(2)}) %collective-permute-start.10) | collective-permute-done | bytes 393248 | tf_op jit(solution)/shard_map/ppermute | solution.py:24
  46.4 1.5 %collective-permute-start.20 = (f16[4,152,256]{2,1,0:T(8,128)(2,1)S(1)}, f16[4,152,256]{2,1,0:T(8,128)(2,1)S(1)}, u32[]{:S(2)}, u32[]{:S(2)}) collective-permute-start(f16[4,152,256]{2,1,0:T(8,128)(2,1)S(1)} %pad_maximum_fusion.1), channel_id=1, source_target_pairs={{0,8},{4,12},{8,0},{12,4},{16,24},{20,28},{24,16},{28,20},{1,9},{5... | collective-permute-start | bytes 933896 | tf_op jit(solution)/shard_map/ppermute | solution.py:24
  49.2 1.5 %collective-permute-start.19 = (f16[152,256]{1,0:T(8,128)(2,1)S(1)}, f16[152,256]{1,0:T(8,128)(2,1)S(1)}, u32[]{:S(2)}, u32[]{:S(2)}) collective-permute-start(f16[152,256]{1,0:T(8,128)(2,1)S(1)} %convert_element_type.176), channel_id=1, source_target_pairs={{0,8},{4,12},{8,0},{12,4},{16,24},{20,28},{24,16},{28,20},{1,9},{5... | collective-permute-start | bytes 233480 | tf_op jit(solution)/shard_map/ppermute | solution.py:24
  51.6 2.1 %collective-permute-start.18 = (f16[152,256]{1,0:T(8,128)(2,1)S(1)}, f16[152,256]{1,0:T(8,128)(2,1)S(1)}, u32[]{:S(2)}, u32[]{:S(2)}) collective-permute-start(f16[152,256]{1,0:T(8,128)(2,1)S(1)} %convert_element_type.176), channel_id=1, source_target_pairs={{0,24},{4,28},{8,16},{12,20},{16,8},{20,12},{24,0},{28,4},{1,25},{... | collective-permute-start | bytes 233480 | tf_op jit(solution)/shard_map/ppermute | solution.py:24
  55.0 3.4 %collective-permute-done.19 = f16[152,256]{1,0:T(8,128)(2,1)S(1)} collective-permute-done((f16[152,256]{1,0:T(8,128)(2,1)S(1)}, f16[152,256]{1,0:T(8,128)(2,1)S(1)}, u32[]{:S(2)}, u32[]{:S(2)}) %collective-permute-start.19) | collective-permute-done | bytes 77856 | tf_op jit(solution)/shard_map/ppermute | solution.py:24
  61.1 2.1 %input_terms.1 = bf16[2,128,768]{2,1,0:T(8,128)(2,1)S(1)} custom-call(bf16[1152,512]{1,0:T(8,128)(2,1)S(1)} %bitcast.104, f32[2,8,8,256]{3,2,1,0:T(8,128)S(1)} %pad_maximum_fusion.23.ends, bf16[2,128,768]{2,1,0:T(8,128)(2,1)S(1)} %bitcast.101, bf16[2,128,768]{2,1,0:T(8,128)(2,1)S(1)} %collective-permute-done.gb.refs_1_, ...), custom_call_target="tpu_custom_call" | custom-call | flops 1207959552 | bytes 3276800 | tf_op jit(solution)/shard_map/input_terms/pallas_call | solution.py:45
  65.7 1.5 %place_pieces.1 = f32[1152,512]{1,0:T(8,128)} custom-call(f32[1152,256]{1,0:T(8,128)S(1)} %bitcast.91, f32[288,256]{1,0:T(8,128)S(1)} %bitcast.94, f32[288,256]{1,0:T(8,128)S(1)} %bitcast.96, f32[288,256]{1,0:T(8,128)S(1)} %bitcast.93, f32[288,256]{1,0:T(8,128)S(1)} %bitcast.95), custom_call_target="tpu_custom_call" | custom-call | tf_op jit(solution)/shard_map/place_pieces/pallas_call | solution.py:503
  (100 shorter events, 17.4 us)
Async XLA Ops:
  1.7 5.6 %collective-permute-start = (bf16[2,128,768]{2,1,0:T(8,128)(2,1)S(1)}, bf16[2,128,768]{2,1,0:T(8,128)(2,1)S(1)}, u32[]{:S(2)}, u32[]{:S(2)}) collective-permute-start(bf16[2,128,768]{2,1,0:T(8,128)(2,1)S(1)} %bitcast.98), channel_id=1, source_target_pairs={{0,1},{1,0},{2,3},{3,2},{4,5},{5,4},{6,7},{7,6},{8,9},{9,8},{10,11... | collective-permute-start | bytes 1179656 | tf_op jit(solution)/shard_map/ppermute | solution.py:24
  2.2 12.3 %collective-permute-start.2 = (bf16[2,128,768]{2,1,0:T(8,128)(2,1)S(1)}, bf16[2,128,768]{2,1,0:T(8,128)(2,1)S(1)}, u32[]{:S(2)}, u32[]{:S(2)}) collective-permute-start(bf16[2,128,768]{2,1,0:T(8,128)(2,1)S(1)} %bitcast.99), channel_id=1, source_target_pairs={{0,2},{1,3},{2,0},{3,1},{4,6},{5,7},{6,4},{7,5},{8,10},{9,11},{10,... | collective-permute-start | bytes 1179656 | tf_op jit(solution)/shard_map/ppermute | solution.py:24
  8.6 9.3 %collective-permute-start.1 = (f16[592,256]{1,0:T(8,128)(2,1)S(1)}, f16[592,256]{1,0:T(8,128)(2,1)S(1)}, u32[]{:S(2)}, u32[]{:S(2)}) collective-permute-start(f16[592,256]{1,0:T(8,128)(2,1)S(1)} %convert_element_type.142), channel_id=1, source_target_pairs={{0,4},{4,0},{8,12},{12,8},{16,20},{20,16},{24,28},{28,24},{1,5},{5... | collective-permute-start | bytes 909320 | tf_op jit(solution)/shard_map/ppermute | solution.py:24
  10.1 0.8 %collective-permute-start.3 = (bf16[1,256]{1,0:T(2,128)(2,1)S(1)}, bf16[1,256]{1,0:T(2,128)(2,1)S(1)}, u32[]{:S(2)}, u32[]{:S(2)}) collective-permute-start(bf16[1,256]{1,0:T(2,128)(2,1)S(1)} %broadcast_select_fusion.15), channel_id=1, source_target_pairs={{4,8},{12,16},{20,24},{8,4},{16,12},{24,20},{5,9},{13,17},{21,25},... | collective-permute-start | bytes 1544 | tf_op jit(solution)/shard_map/ppermute | solution.py:405
  14.5 3.7 %collective-permute-start.4 = (bf16[2,128,768]{2,1,0:T(8,128)(2,1)S(1)}, bf16[2,128,768]{2,1,0:T(8,128)(2,1)S(1)}, u32[]{:S(2)}, u32[]{:S(2)}) collective-permute-start(bf16[2,128,768]{2,1,0:T(8,128)(2,1)S(1)} %collective-permute-done.2.ga.refs_2_), channel_id=1, source_target_pairs={{0,1},{1,0},{2,3},{3,2},{4,5},{5,4},{6,7},{7,6},{8,9},{9,8},{10,11... | collective-permute-start | bytes 1179656 | tf_op jit(solution)/shard_map/ppermute | solution.py:24
  18.2 9.3 %copy-start.2 = (bf16[128,3,3,512]{3,0,2,1:T(8,128)(2,1)S(1)}, bf16[128,3,3,512]{3,0,2,1:T(8,128)(2,1)}, u32[]{:S(2)}) copy-start(bf16[128,3,3,512]{3,0,2,1:T(8,128)(2,1)} %param.4) | copy-start | bytes 3538948
  19.4 10.3 %collective-permute-start.6 = (f16[592,256]{1,0:T(8,128)(2,1)S(1)}, f16[592,256]{1,0:T(8,128)(2,1)S(1)}, u32[]{:S(2)}, u32[]{:S(2)}) collective-permute-start(f16[592,256]{1,0:T(8,128)(2,1)S(1)} %convert_element_type.150), channel_id=1, source_target_pairs={{0,4},{4,0},{8,12},{12,8},{16,20},{20,16},{24,28},{28,24},{1,5},{5... | collective-permute-start | bytes 909320 | tf_op jit(solution)/shard_map/ppermute | solution.py:24
  20.9 8.7 %collective-permute-start.7 = (f16[168,256]{1,0:T(8,128)(2,1)S(1)}, f16[168,256]{1,0:T(8,128)(2,1)S(1)}, u32[]{:S(2)}, u32[]{:S(2)}) collective-permute-start(f16[168,256]{1,0:T(8,128)(2,1)S(1)} %get-tuple-element.76), channel_id=1, source_target_pairs={{0,8},{4,12},{8,0},{12,4},{16,24},{20,28},{24,16},{28,20},{1,9},{5... | collective-permute-start | bytes 258056 | tf_op jit(solution)/shard_map/ppermute | solution.py:24
  22.5 7.9 %collective-permute-start.8 = (f16[168,256]{1,0:T(8,128)(2,1)S(1)}, f16[168,256]{1,0:T(8,128)(2,1)S(1)}, u32[]{:S(2)}, u32[]{:S(2)}) collective-permute-start(f16[168,256]{1,0:T(8,128)(2,1)S(1)} %get-tuple-element.84), channel_id=1, source_target_pairs={{0,16},{4,20},{8,24},{12,28},{16,0},{20,4},{24,8},{28,12},{1,17},{... | collective-permute-start | bytes 258056 | tf_op jit(solution)/shard_map/ppermute | solution.py:24
  25.2 6.4 %collective-permute-start.9 = (f16[168,256]{1,0:T(8,128)(2,1)S(1)}, f16[168,256]{1,0:T(8,128)(2,1)S(1)}, u32[]{:S(2)}, u32[]{:S(2)}) collective-permute-start(f16[168,256]{1,0:T(8,128)(2,1)S(1)} %get-tuple-element.85), channel_id=1, source_target_pairs={{0,24},{4,28},{8,16},{12,20},{16,8},{20,12},{24,0},{28,4},{1,25},{... | collective-permute-start | bytes 258056 | tf_op jit(solution)/shard_map/ppermute | solution.py:24
  29.6 5.3 %collective-permute-start.5 = (f32[2,2,128,768]{3,2,1,0:T(8,128)S(1)}, f32[2,2,128,768]{3,2,1,0:T(8,128)S(1)}, u32[]{:S(2)}, u32[]{:S(2)}) collective-permute-start(f32[2,2,128,768]{3,2,1,0:T(8,128)S(1)} %get-tuple-element.81), channel_id=1, source_target_pairs={{0,1},{1,0},{2,3},{3,2},{4,5},{5,4},{6,7},{7,6},{8,9},{9,8},{10,11... | collective-permute-start | bytes 4718600 | tf_op jit(solution)/shard_map/ppermute | solution.py:24
  32.5 6.2 %collective-permute-start.11 = (f16[1,152,256]{2,1,0:T(8,128)(2,1)S(1)}, f16[1,152,256]{2,1,0:T(8,128)(2,1)S(1)}, u32[]{:S(2)}, u32[]{:S(2)}) collective-permute-start(f16[1,152,256]{2,1,0:T(8,128)(2,1)S(1)} %bitcast.106), channel_id=1, source_target_pairs={{0,16},{4,20},{8,24},{12,28},{16,0},{20,4},{24,8},{28,12},{1,17},{... | collective-permute-start | bytes 233480 | tf_op jit(solution)/shard_map/ppermute | solution.py:24
  35.2 11.2 %collective-permute-start.10 = (f32[128,768]{1,0:T(8,128)S(1)}, f32[128,768]{1,0:T(8,128)S(1)}, u32[]{:S(2)}, u32[]{:S(2)}) collective-permute-start(f32[128,768]{1,0:T(8,128)S(1)} %get-tuple-element.94), channel_id=1, source_target_pairs={{0,2},{1,3},{2,0},{3,1},{4,6},{5,7},{6,4},{7,5},{8,10},{9,11},{10,... | collective-permute-start | bytes 1179656 | tf_op jit(solution)/shard_map/ppermute | solution.py:24
  38.8 5.3 %collective-permute-start.12 = (f16[2,152,256]{2,1,0:T(8,128)(2,1)S(1)}, f16[2,152,256]{2,1,0:T(8,128)(2,1)S(1)}, u32[]{:S(2)}, u32[]{:S(2)}) collective-permute-start(f16[2,152,256]{2,1,0:T(8,128)(2,1)S(1)} %pad_maximum_fusion.2), channel_id=1, source_target_pairs={{0,4},{4,0},{8,12},{12,8},{16,20},{20,16},{24,28},{28,24},{1,5},{5... | collective-permute-start | bytes 466952 | tf_op jit(solution)/shard_map/ppermute | solution.py:24
  39.1 8.8 %collective-permute-start.14 = (f16[168,256]{1,0:T(8,128)(2,1)S(1)}, f16[168,256]{1,0:T(8,128)(2,1)S(1)}, u32[]{:S(2)}, u32[]{:S(2)}) collective-permute-start(f16[168,256]{1,0:T(8,128)(2,1)S(1)} %get-tuple-element.92), channel_id=1, source_target_pairs={{0,8},{4,12},{8,0},{12,4},{16,24},{20,28},{24,16},{28,20},{1,9},{5... | collective-permute-start | bytes 258056 | tf_op jit(solution)/shard_map/ppermute | solution.py:24
  40.6 8.0 %collective-permute-start.15 = (f16[168,256]{1,0:T(8,128)(2,1)S(1)}, f16[168,256]{1,0:T(8,128)(2,1)S(1)}, u32[]{:S(2)}, u32[]{:S(2)}) collective-permute-start(f16[168,256]{1,0:T(8,128)(2,1)S(1)} %get-tuple-element.101), channel_id=1, source_target_pairs={{0,16},{4,20},{8,24},{12,28},{16,0},{20,4},{24,8},{28,12},{1,17},{... | collective-permute-start | bytes 258056 | tf_op jit(solution)/shard_map/ppermute | solution.py:24
  42.1 6.4 %collective-permute-start.16 = (f16[168,256]{1,0:T(8,128)(2,1)S(1)}, f16[168,256]{1,0:T(8,128)(2,1)S(1)}, u32[]{:S(2)}, u32[]{:S(2)}) collective-permute-start(f16[168,256]{1,0:T(8,128)(2,1)S(1)} %get-tuple-element.102), channel_id=1, source_target_pairs={{0,24},{4,28},{8,16},{12,20},{16,8},{20,12},{24,0},{28,4},{1,25},{... | collective-permute-start | bytes 258056 | tf_op jit(solution)/shard_map/ppermute | solution.py:24
  44.1 9.6 %collective-permute-start.13 = (f32[128,768]{1,0:T(8,128)S(1)}, f32[128,768]{1,0:T(8,128)S(1)}, u32[]{:S(2)}, u32[]{:S(2)}) collective-permute-start(f32[128,768]{1,0:T(8,128)S(1)} %get-tuple-element.95), channel_id=1, source_target_pairs={{0,2},{1,3},{2,0},{3,1},{4,6},{5,7},{6,4},{7,5},{8,10},{9,11},{10,... | collective-permute-start | bytes 1179656 | tf_op jit(solution)/shard_map/ppermute | solution.py:24
  46.4 16.7 %collective-permute-start.20 = (f16[4,152,256]{2,1,0:T(8,128)(2,1)S(1)}, f16[4,152,256]{2,1,0:T(8,128)(2,1)S(1)}, u32[]{:S(2)}, u32[]{:S(2)}) collective-permute-start(f16[4,152,256]{2,1,0:T(8,128)(2,1)S(1)} %pad_maximum_fusion.1), channel_id=1, source_target_pairs={{0,8},{4,12},{8,0},{12,4},{16,24},{20,28},{24,16},{28,20},{1,9},{5... | collective-permute-start | bytes 933896 | tf_op jit(solution)/shard_map/ppermute | solution.py:24
  49.2 9.1 %collective-permute-start.19 = (f16[152,256]{1,0:T(8,128)(2,1)S(1)}, f16[152,256]{1,0:T(8,128)(2,1)S(1)}, u32[]{:S(2)}, u32[]{:S(2)}) collective-permute-start(f16[152,256]{1,0:T(8,128)(2,1)S(1)} %convert_element_type.176), channel_id=1, source_target_pairs={{0,8},{4,12},{8,0},{12,4},{16,24},{20,28},{24,16},{28,20},{1,9},{5... | collective-permute-start | bytes 233480 | tf_op jit(solution)/shard_map/ppermute | solution.py:24
  50.7 8.6 %collective-permute-start.17 = (f16[152,256]{1,0:T(8,128)(2,1)S(1)}, f16[152,256]{1,0:T(8,128)(2,1)S(1)}, u32[]{:S(2)}, u32[]{:S(2)}) collective-permute-start(f16[152,256]{1,0:T(8,128)(2,1)S(1)} %convert_element_type.176), channel_id=1, source_target_pairs={{0,16},{4,20},{8,24},{12,28},{16,0},{20,4},{24,8},{28,12},{1,17},{... | collective-permute-start | bytes 233480 | tf_op jit(solution)/shard_map/ppermute | solution.py:24
  51.6 8.5 %collective-permute-start.18 = (f16[152,256]{1,0:T(8,128)(2,1)S(1)}, f16[152,256]{1,0:T(8,128)(2,1)S(1)}, u32[]{:S(2)}, u32[]{:S(2)}) collective-permute-start(f16[152,256]{1,0:T(8,128)(2,1)S(1)} %convert_element_type.176), channel_id=1, source_target_pairs={{0,24},{4,28},{8,16},{12,20},{16,8},{20,12},{24,0},{28,4},{1,25},{... | collective-permute-start | bytes 233480 | tf_op jit(solution)/shard_map/ppermute | solution.py:24
  58.4 6.0 %collective-permute-start.22 = (f16[2,152,256]{2,1,0:T(8,128)(2,1)S(1)}, f16[2,152,256]{2,1,0:T(8,128)(2,1)S(1)}, u32[]{:S(2)}, u32[]{:S(2)}) collective-permute-start(f16[2,152,256]{2,1,0:T(8,128)(2,1)S(1)} %pad_maximum_fusion.3), channel_id=1, source_target_pairs={{0,4},{4,0},{8,12},{12,8},{16,20},{20,16},{24,28},{28,24},{1,5},{5... | collective-permute-start | bytes 466952 | tf_op jit(solution)/shard_map/ppermute | solution.py:24
  60.1 5.3 %collective-permute-start.21 = (f16[2,152,256]{2,1,0:T(8,128)(2,1)S(1)}, f16[2,152,256]{2,1,0:T(8,128)(2,1)S(1)}, u32[]{:S(2)}, u32[]{:S(2)}) collective-permute-start(f16[2,152,256]{2,1,0:T(8,128)(2,1)S(1)} %pad_maximum_fusion.4), channel_id=1, source_target_pairs={{0,4},{4,0},{8,12},{12,8},{16,20},{20,16},{24,28},{28,24},{1,5},{5... | collective-permute-start | bytes 466952 | tf_op jit(solution)/shard_map/ppermute | solution.py:24
  (2 other events, 8.3 us)
